TPU v7x, 32 devices: a whole 2x2x4 slice. The times are simulated.
32 devices in a mesh: pipe: 2 (over x), dp: 4 (over y, core), tensor: 4 (over z).
Axes of the slice: x: 2, y: 2, z: 4, core: 2. Of those that a mesh axis runs over, the one named last changes fastest.
Arguments:
- tokens_in: bfloat16 [12, 1024, 1536], P('dp', 'tensor'), may hold values from -6 to 6
- cotangent: bfloat16 [12, 1024, 1536], P('dp', 'tensor'), may hold values from -6 to 6
- lengths: int32 [12], P('dp'), may hold values from 512 to 1024, as said below
- in_gate: bfloat16 [2, 1536, 3072], P('pipe', 'dp', 'tensor'), may hold values from -0.15625 to 0.15625
- in_value: bfloat16 [2, 1536, 3072], P('pipe', 'dp', 'tensor'), may hold values from -0.15625 to 0.15625
- in_state: bfloat16 [2, 1536, 256], P('pipe', 'dp'), may hold values from -0.15625 to 0.15625
- in_step: bfloat16 [2, 1536, 48], P('pipe', 'dp', 'tensor'), may hold values from -0.15625 to 0.15625
- out_proj: bfloat16 [2, 1536, 3072], P('pipe', 'dp', 'tensor'), may hold values from -0.109375 to 0.109375
- norm_gain: float32 [2, 1536], P('pipe'), may hold values from 0.5 to 1.5
- conv_value: float32 [2, 4, 3072], P('pipe', None, 'tensor'), may hold values from -3 to 3
- conv_state: float32 [2, 4, 256], P('pipe'), may hold values from -3 to 3
- bias_value: float32 [2, 3072], P('pipe', 'tensor'), may hold values from -1.5 to 1.5
- bias_state: float32 [2, 256], P('pipe'), may hold values from -1.5 to 1.5
- step_bias: float32 [2, 48], P('pipe', 'tensor'), may hold values from -7 to -2.2
- decay_log: float32 [2, 48], P('pipe', 'tensor'), may hold values from 0 to 2.77
- skip_gain: float32 [2, 48], P('pipe', 'tensor'), may hold values from 0.5 to 1.5
- gate_gain: float32 [2, 3072], P('pipe', 'tensor'), may hold values from 0.5 to 1.5
Outputs:
- outputs_both: bfloat16 [2, 12, 1024, 1536], P('pipe', 'dp', 'tensor')
- input_grads: bfloat16 [2, 12, 1024, 1536], P('pipe', 'dp', 'tensor')
- grad_in_gate: float32 [2, 1536, 3072], P('pipe', 'dp', 'tensor')
- grad_in_value: float32 [2, 1536, 3072], P('pipe', 'dp', 'tensor')
- grad_in_state: float32 [2, 1536, 256], P('pipe', None, ('dp', 'tensor'))
- grad_in_step: float32 [2, 1536, 48], P('pipe', 'dp', 'tensor')
- grad_out_proj: float32 [2, 1536, 3072], P('pipe', 'dp', 'tensor')
- grad_norm_gain: float32 [2, 1536], P('pipe', ('dp', 'tensor'))
- grad_conv_value: float32 [2, 4, 3072], P('pipe', None, 'tensor')
- grad_conv_state: float32 [2, 4, 256], P('pipe', None, ('dp', 'tensor'))
- grad_bias_value: float32 [2, 3072], P('pipe', 'tensor')
- grad_bias_state: float32 [2, 256], P('pipe', ('dp', 'tensor'))
- grad_step_bias: float32 [2, 48], P('pipe', 'tensor')
- grad_decay_log: float32 [2, 48], P('pipe', 'tensor')
- grad_skip_gain: float32 [2, 48], P('pipe', 'tensor')
- grad_gate_gain: float32 [2, 3072], P('pipe', 'tensor')
Inputs may be any that keep to these rules, and one draw needn't show every extreme that they name: `lengths`: in each group of 3 consecutive sequences one, drawn from the seed, has all 1024 positions valid.
All inputs are finite; a program needn't handle non-finite values.
Results may differ from a plain program's by a relative error of at most 0.03.
Values may be sent and summed in bfloat16 or wider, within the bound.
A program may use at most 320 MiB of HBM per device.

v0:
```python
import jax
import jax.numpy as jnp
from jax import lax
from jax.sharding import PartitionSpec as P

SPAN = 256


EPS = 1e-05
HIGHEST = lax.Precision.HIGHEST


def passed_along(value, axis, by):
    devices = lax.axis_size(axis)
    pairs = [(i, i + by) for i in range(devices) if 0 <= i + by < devices]
    return lax.ppermute(value, axis, pairs)


def causal_conv(values, taps, offsets):
    length = values.shape[0]
    tap_count = taps.shape[0]
    padded = jnp.concatenate(
        [jnp.zeros((tap_count - 1, values.shape[1]), values.dtype), values], axis=0
    )
    summed = offsets[None, :] + jnp.zeros_like(values)
    for shift_idx in range(tap_count):
        summed = summed + taps[shift_idx][None, :] * padded[shift_idx : shift_idx + length]
    return jax.nn.silu(summed)


def ssd_block(carry_state, pieces):
    head_values, step_size, log_decay, in_mat, out_mat = pieces
    cumulated = jnp.cumsum(log_decay, axis=0)
    block_len = log_decay.shape[0]
    lower_mask = (jnp.arange(block_len)[:, None] >= jnp.arange(block_len)[None, :])[:, :, None]
    spread = cumulated[:, None, :] - cumulated[None, :, :]
    decay_mat = jnp.where(lower_mask, jnp.exp(jnp.where(lower_mask, spread, 0.0)), 0.0)
    scores = jnp.dot(out_mat, in_mat.T, precision=HIGHEST)
    mixing = decay_mat * scores[:, :, None] * step_size[None, :, :]
    within = jnp.einsum("ijh,jhp->ihp", mixing, head_values, precision=HIGHEST)
    carried = (
        jnp.einsum("hpn,in->ihp", carry_state, out_mat, precision=HIGHEST)
        * jnp.exp(cumulated)[:, :, None]
    )
    remain = jnp.exp(cumulated[-1][None, :] - cumulated) * step_size
    new_state = jnp.exp(cumulated[-1])[:, None, None] * carry_state + jnp.einsum(
        "jh,jhp,jn->hpn", remain, head_values, in_mat, precision=HIGHEST
    )
    return (new_state, within + carried)


def ssd_scan(head_values, step_size, log_decay, in_mat, out_mat):
    length, head_count, head_dim = head_values.shape
    block_count = length // SPAN
    start_state = jnp.zeros((head_count, head_dim, in_mat.shape[1]), head_values.dtype)
    pieces = (
        head_values.reshape(block_count, SPAN, head_count, head_dim),
        step_size.reshape(block_count, SPAN, head_count),
        log_decay.reshape(block_count, SPAN, head_count),
        in_mat.reshape(block_count, SPAN, -1),
        out_mat.reshape(block_count, SPAN, -1),
    )
    final_state, result = lax.scan(jax.checkpoint(ssd_block), start_state, pieces)
    return result.reshape(length, head_count, head_dim)


def mixer(
    gate_pre,
    value_pre,
    state_pre,
    step_pre,
    conv_value,
    bias_value,
    conv_state,
    bias_state,
    step_bias,
    decay_log,
    skip_gain,
):
    length = gate_pre.shape[0]
    head_count = step_bias.shape[0]
    value_act = causal_conv(value_pre, conv_value, bias_value)
    state_act = causal_conv(state_pre, conv_state, bias_state)
    state_size = state_act.shape[1] // 2
    step_size = jax.nn.softplus(step_pre + step_bias[None, :])
    log_decay = -step_size * jnp.exp(decay_log)[None, :]
    head_values = value_act.reshape(length, head_count, -1)
    output = ssd_scan(
        head_values, step_size, log_decay, state_act[:, :state_size], state_act[:, state_size:]
    )
    output = output + skip_gain[None, :, None] * head_values
    return output.reshape(length, -1) * jax.nn.silu(gate_pre)


def local_mask(slot_count, seq_length):
    first_row = lax.axis_index("tensor") * slot_count
    return (first_row + jnp.arange(slot_count) < seq_length).astype(jnp.float32)


def layer_forward(tokens, seq_length, weights, smalls):
    gate_weight, value_weight, state_weight, step_weight, out_weight = weights
    (
        norm_vec,
        conv_value,
        conv_state,
        bias_value,
        bias_state,
        step_bias,
        decay_log,
        skip_gain,
        gate_vec,
    ) = smalls
    slot_count = tokens.shape[0]
    root_inv = lax.rsqrt(jnp.mean(tokens * tokens, axis=1, keepdims=True) + EPS)
    normed = (tokens * root_inv * norm_vec[None, :]).astype(jnp.bfloat16)
    full_normed = lax.all_gather(normed, "tensor", axis=0, tiled=True)
    gate_pre = jnp.dot(full_normed, gate_weight, preferred_element_type=jnp.float32)
    value_pre = jnp.dot(full_normed, value_weight, preferred_element_type=jnp.float32)
    state_pre = jnp.dot(full_normed, state_weight, preferred_element_type=jnp.float32)
    step_pre = jnp.dot(full_normed, step_weight, preferred_element_type=jnp.float32)
    gated = mixer(
        gate_pre,
        value_pre,
        state_pre,
        step_pre,
        conv_value,
        bias_value,
        conv_state,
        bias_state,
        step_bias,
        decay_log,
        skip_gain,
    )
    inner_total = gated.shape[1] * lax.axis_size("tensor")
    square_sum = lax.psum(jnp.sum(gated * gated, axis=1), "tensor")
    inverse = lax.rsqrt(square_sum / inner_total + EPS)
    scaled = (gated * inverse[:, None] * gate_vec[None, :]).astype(jnp.bfloat16)
    mixed = lax.psum_scatter(
        jnp.einsum("lc,dc->ld", scaled, out_weight, preferred_element_type=jnp.float32).astype(
            jnp.bfloat16
        ),
        "tensor",
        scatter_dimension=0,
        tiled=True,
    ).astype(jnp.float32)
    row_mask = local_mask(slot_count, seq_length)
    result = row_mask[:, None] * (tokens + mixed)
    kept = (tokens, full_normed, gate_pre, value_pre, state_pre, step_pre, gated, inverse, scaled)
    return (result, kept)


def layer_backward(incoming, seq_length, kept, weights, smalls):
    tokens, full_normed, gate_pre, value_pre, state_pre, step_pre, gated, inverse, scaled = kept
    gate_weight, value_weight, state_weight, step_weight, out_weight = weights
    (
        norm_vec,
        conv_value,
        conv_state,
        bias_value,
        bias_state,
        step_bias,
        decay_log,
        skip_gain,
        gate_vec,
    ) = smalls
    slot_count = tokens.shape[0]
    row_mask = local_mask(slot_count, seq_length)
    grad_out = incoming * row_mask[:, None]
    full_grad = lax.all_gather(grad_out.astype(jnp.bfloat16), "tensor", axis=0, tiled=True)
    grad_scaled = jnp.dot(full_grad, out_weight, preferred_element_type=jnp.float32)
    grad_out_weight = jnp.einsum("ld,lc->dc", full_grad, scaled, preferred_element_type=jnp.float32)
    grad_gate_vec = jnp.sum(grad_scaled * gated * inverse[:, None], axis=0)
    weighted = grad_scaled * gate_vec[None, :]
    inner_total = gated.shape[1] * lax.axis_size("tensor")
    inner_dot = lax.psum(jnp.sum(weighted * gated, axis=1), "tensor")
    grad_gated = (
        inverse[:, None] * weighted - gated * (inverse**3 * inner_dot / inner_total)[:, None]
    )
    unused, mixer_back = jax.vjp(
        mixer,
        gate_pre,
        value_pre,
        state_pre,
        step_pre,
        conv_value,
        bias_value,
        conv_state,
        bias_state,
        step_bias,
        decay_log,
        skip_gain,
    )
    mixer_grads = mixer_back(grad_gated)
    pre_grads = tuple((grad_piece.astype(jnp.bfloat16) for grad_piece in mixer_grads[:4]))
    in_weights = (gate_weight, value_weight, state_weight, step_weight)
    grads_proj = tuple(
        (
            jnp.einsum("ld,lc->dc", full_normed, grad_piece, preferred_element_type=jnp.float32)
            for grad_piece in pre_grads
        )
    )
    summed = jnp.zeros((lax.axis_size("tensor") * slot_count, tokens.shape[1]), jnp.float32)
    for grad_piece, weight_piece in zip(pre_grads, in_weights):
        summed = summed + jnp.einsum(
            "lc,dc->ld", grad_piece, weight_piece, preferred_element_type=jnp.float32
        )
    grad_normed = lax.psum_scatter(
        summed.astype(jnp.bfloat16), "tensor", scatter_dimension=0, tiled=True
    ).astype(jnp.float32)
    root_inv = lax.rsqrt(jnp.mean(tokens * tokens, axis=1, keepdims=True) + EPS)
    grad_norm_vec = jnp.sum(grad_normed * tokens * root_inv, axis=0)
    weighted_in = grad_normed * norm_vec[None, :]
    grad_tokens = (
        root_inv * weighted_in
        - tokens * root_inv**3 * jnp.mean(weighted_in * tokens, axis=1, keepdims=True)
        + grad_out
    )
    small_grads = (
        grad_norm_vec,
        mixer_grads[4],
        mixer_grads[6],
        mixer_grads[5],
        mixer_grads[7],
        mixer_grads[8],
        mixer_grads[9],
        mixer_grads[10],
        grad_gate_vec,
    )
    dp_grads = (grads_proj[0], grads_proj[1], grads_proj[3], grad_out_weight)
    return (grad_tokens, dp_grads, grads_proj[2], small_grads)


def add_all(totals, extra):
    if totals is None:
        return extra
    return tuple((left_part + right_part for left_part, right_part in zip(totals, extra)))


def body(
    tokens_in,
    cotangent,
    lengths,
    in_gate,
    in_value,
    in_state,
    in_step,
    out_proj,
    norm_gain,
    conv_value,
    conv_state,
    bias_value,
    bias_state,
    step_bias,
    decay_log,
    skip_gain,
    gate_gain,
):
    section_index = lax.axis_index("pipe")
    micro_count, slot_count, model_width = tokens_in.shape
    sharded = (in_gate, in_value, in_state, in_step, out_proj)
    smalls = tuple(
        (
            entry_arr[0]
            for entry_arr in (
                norm_gain,
                conv_value,
                conv_state,
                bias_value,
                bias_state,
                step_bias,
                decay_log,
                skip_gain,
                gate_gain,
            )
        )
    )
    received = jnp.zeros((slot_count, model_width), jnp.bfloat16)
    outputs_keep = jnp.zeros((micro_count, slot_count, model_width), jnp.bfloat16)
    saved = []
    for step_index in range(micro_count + 1):
        batch_index = step_index - section_index
        valid = (batch_index >= 0) & (batch_index < micro_count)
        clipped = jnp.clip(batch_index, 0, micro_count - 1)
        fresh = tokens_in[min(step_index, micro_count - 1)]
        if step_index == micro_count:
            fresh = jnp.zeros_like(fresh)
        source = jnp.where(section_index == 0, fresh, received)
        weights = tuple(
            (
                piece_arr[0]
                for piece_arr in (
                    lax.all_gather(sharded[0], "dp", axis=1, tiled=True),
                    lax.all_gather(sharded[1], "dp", axis=1, tiled=True),
                    lax.all_gather(sharded[2], "dp", axis=1, tiled=True),
                    lax.all_gather(sharded[3], "dp", axis=1, tiled=True),
                    lax.all_gather(sharded[4], "dp", axis=1, tiled=True),
                )
            )
        )
        result, kept = layer_forward(source.astype(jnp.float32), lengths[clipped], weights, smalls)
        result_low = result.astype(jnp.bfloat16)
        outputs_keep = jnp.where(
            valid,
            lax.dynamic_update_index_in_dim(outputs_keep, result_low, clipped, 0),
            outputs_keep,
        )
        saved.append(kept)
        received = passed_along(result_low, "pipe", 1)
    stacked_keep = tuple((jnp.stack(list(members)) for members in zip(*saved)))
    incoming = jnp.zeros((slot_count, model_width), jnp.bfloat16)
    grads_keep = jnp.zeros((micro_count, slot_count, model_width), jnp.bfloat16)
    dp_totals = None
    state_total = None
    small_totals = None
    for step_index in range(micro_count + 1):
        batch_index = step_index + section_index - 1
        valid = (batch_index >= 0) & (batch_index < micro_count)
        clipped = jnp.clip(batch_index, 0, micro_count - 1)
        forward_index = jnp.clip(step_index + 2 * section_index - 1, 0, micro_count)
        kept = tuple((entry_arr[forward_index] for entry_arr in stacked_keep))
        fresh = cotangent[min(step_index, micro_count - 1)]
        if step_index == micro_count:
            fresh = jnp.zeros_like(fresh)
        source = jnp.where(section_index == 1, fresh, incoming).astype(jnp.float32)
        weights = tuple(
            (
                piece_arr[0]
                for piece_arr in (
                    lax.all_gather(sharded[0], "dp", axis=1, tiled=True),
                    lax.all_gather(sharded[1], "dp", axis=1, tiled=True),
                    lax.all_gather(sharded[2], "dp", axis=1, tiled=True),
                    lax.all_gather(sharded[3], "dp", axis=1, tiled=True),
                    lax.all_gather(sharded[4], "dp", axis=1, tiled=True),
                )
            )
        )
        grad_tokens, dp_grads, state_grad, small_grads = layer_backward(
            source, lengths[clipped], kept, weights, smalls
        )
        shares = (
            lax.psum_scatter(
                dp_grads[0].astype(jnp.bfloat16), "dp", scatter_dimension=0, tiled=True
            ).astype(jnp.float32),
            lax.psum_scatter(
                dp_grads[1].astype(jnp.bfloat16), "dp", scatter_dimension=0, tiled=True
            ).astype(jnp.float32),
            lax.psum_scatter(
                dp_grads[2].astype(jnp.bfloat16), "dp", scatter_dimension=0, tiled=True
            ).astype(jnp.float32),
            lax.psum_scatter(
                dp_grads[3].astype(jnp.bfloat16), "dp", scatter_dimension=0, tiled=True
            ).astype(jnp.float32),
        )
        dp_totals = add_all(dp_totals, shares)
        state_total = add_all(state_total, (state_grad,))
        small_totals = add_all(small_totals, small_grads)
        grad_low = grad_tokens.astype(jnp.bfloat16)
        grads_keep = jnp.where(
            valid, lax.dynamic_update_index_in_dim(grads_keep, grad_low, clipped, 0), grads_keep
        )
        incoming = passed_along(grad_low, "pipe", -1)
    shared = (
        lax.psum_scatter(state_total[0], ("dp", "tensor"), scatter_dimension=1, tiled=True),
        lax.psum_scatter(small_totals[0], ("dp", "tensor"), scatter_dimension=0, tiled=True),
        lax.psum_scatter(small_totals[2], ("dp", "tensor"), scatter_dimension=1, tiled=True),
        lax.psum_scatter(small_totals[4], ("dp", "tensor"), scatter_dimension=0, tiled=True),
    )
    head_sums = lax.psum(
        (
            small_totals[1],
            small_totals[3],
            small_totals[5],
            small_totals[6],
            small_totals[7],
            small_totals[8],
        ),
        "dp",
    )
    return (
        outputs_keep[None],
        grads_keep[None],
        dp_totals[0][None],
        dp_totals[1][None],
        shared[0][None],
        dp_totals[2][None],
        dp_totals[3][None],
        shared[1][None],
        head_sums[0][None],
        shared[2][None],
        head_sums[1][None],
        shared[3][None],
        head_sums[2][None],
        head_sums[3][None],
        head_sums[4][None],
        head_sums[5][None],
    )


def solution(mesh):
    in_specs = (
        P("dp", "tensor", None),
        P("dp", "tensor", None),
        P("dp"),
        P("pipe", "dp", "tensor"),
        P("pipe", "dp", "tensor"),
        P("pipe", "dp", None),
        P("pipe", "dp", "tensor"),
        P("pipe", "dp", "tensor"),
        P("pipe", None),
        P("pipe", None, "tensor"),
        P("pipe", None, None),
        P("pipe", "tensor"),
        P("pipe", None),
        P("pipe", "tensor"),
        P("pipe", "tensor"),
        P("pipe", "tensor"),
        P("pipe", "tensor"),
    )
    out_specs = (
        P("pipe", "dp", "tensor", None),
        P("pipe", "dp", "tensor", None),
        P("pipe", "dp", "tensor"),
        P("pipe", "dp", "tensor"),
        P("pipe", None, ("dp", "tensor")),
        P("pipe", "dp", "tensor"),
        P("pipe", "dp", "tensor"),
        P("pipe", ("dp", "tensor")),
        P("pipe", None, "tensor"),
        P("pipe", None, ("dp", "tensor")),
        P("pipe", "tensor"),
        P("pipe", ("dp", "tensor")),
        P("pipe", "tensor"),
        P("pipe", "tensor"),
        P("pipe", "tensor"),
        P("pipe", "tensor"),
    )
    return jax.shard_map(body, mesh=mesh, in_specs=in_specs, out_specs=out_specs, check_vma=False)
```

profile of v0, /device:TPU:0, one launch (start us, length us, event | category | flops | bytes accessed | tf_op | source)
XLA Modules:
  0.0 4026.5 jit_solution(14698923426541793834)
XLA Ops:
  38.2 66.5 %all-gather.12.cloned.1.call-done = bf16[1024,1536]{1,0:T(8,128)(2,1)} async-done(((bf16[256,1536]{1,0:T(8,128)(2,1)}), bf16[1024,1536]{1,0:T(8,128)(2,1)}) %all-gather.12.cloned.1.call-update) | async-done | bytes 3145744 | tf_op jit(solution)/shard_map/all_gather | solution.py:116
  133.4 114.8 %while.224 = (s32[]{:T(128)}, f32[12,64,128]{2,1,0:T(8,128)S(1)}, f32[4,256,12,64]{1,0,3,2:T(4,128)}, f32[4,256,12]{1,0,2:T(4,128)S(1)}, f32[4,256,12]{1,0,2:T(4...) while((s32[]{:T(128)}, f32[12,64,128]{2,1,0:T(8,128)S(1)}, ...), condition=%wide.region_4.5_spmd.clone, body=%wide.region_1.4_spmd.clone.sunk | while | flops 1314002944 | bytes 11401816 | solution.py:63
  282.0 57.3 %reduce-scatter.37.cloned.1.call-done = bf16[256,1536]{1,0:T(8,128)(2,1)} async-done(((bf16[1024,1536]{1,0:T(8,128)(2,1)}), bf16[256,1536]{1,0:T(8,128)(2,1)}) %reduce-scatter.37.cloned.1.call-update) | async-done | bytes 786448 | tf_op jit(solution)/shard_map/reduce_scatter | solution.py:138
  367.3 64.9 %all-gather.20.cloned.1.call-done = bf16[1024,1536]{1,0:T(8,128)(2,1)} async-done(((bf16[256,1536]{1,0:T(8,128)(2,1)}), bf16[1024,1536]{1,0:T(8,128)(2,1)}) %all-gather.20.cloned.1.call-update) | async-done | bytes 3145744 | tf_op jit(solution)/shard_map/all_gather | solution.py:116
  461.2 114.7 %while.225 = (s32[]{:T(128)}, f32[12,64,128]{2,1,0:T(8,128)S(1)}, f32[4,256,12,64]{1,0,3,2:T(4,128)}, f32[4,256,12]{1,0,2:T(4,128)S(1)}, f32[4,256,12]{1,0,2:T(4...) while((s32[]{:T(128)}, f32[12,64,128]{2,1,0:T(8,128)S(1)}, ...), condition=%wide.region_12.13_spmd.clone, body=%wide.region_9.12_spmd.clone.sunk | while | flops 1314002944 | bytes 11401816 | solution.py:63
  608.2 58.6 %reduce-scatter.39.cloned.1.call-done = bf16[256,1536]{1,0:T(8,128)(2,1)} async-done(((bf16[1024,1536]{1,0:T(8,128)(2,1)}), bf16[256,1536]{1,0:T(8,128)(2,1)}) %reduce-scatter.39.cloned.1.call-update) | async-done | bytes 786448 | tf_op jit(solution)/shard_map/reduce_scatter | solution.py:138
  694.0 64.9 %all-gather.22.cloned.1.call-done = bf16[1024,1536]{1,0:T(8,128)(2,1)} async-done(((bf16[256,1536]{1,0:T(8,128)(2,1)}), bf16[1024,1536]{1,0:T(8,128)(2,1)}) %all-gather.22.cloned.1.call-update) | async-done | bytes 3145744 | tf_op jit(solution)/shard_map/all_gather | solution.py:116
  787.7 115.1 %while.226 = (s32[]{:T(128)}, f32[12,64,128]{2,1,0:T(8,128)S(1)}, f32[4,256,12,64]{1,0,3,2:T(4,128)}, f32[4,256,12]{1,0,2:T(4,128)S(1)}, f32[4,256,12]{1,0,2:T(4...) while((s32[]{:T(128)}, f32[12,64,128]{2,1,0:T(8,128)S(1)}, ...), condition=%wide.region_20.21_spmd.clone, body=%wide.region_17.20_spmd.clone.sunk | while | flops 1314002944 | bytes 11401816 | solution.py:63
  935.5 58.5 %reduce-scatter.41.cloned.1.call-done = bf16[256,1536]{1,0:T(8,128)(2,1)} async-done(((bf16[1024,1536]{1,0:T(8,128)(2,1)}), bf16[256,1536]{1,0:T(8,128)(2,1)}) %reduce-scatter.41.cloned.1.call-update) | async-done | bytes 786448 | tf_op jit(solution)/shard_map/reduce_scatter | solution.py:138
  1022.6 61.2 %all-gather.24.cloned.1.call-done = bf16[1024,1536]{1,0:T(8,128)(2,1)} async-done(((bf16[256,1536]{1,0:T(8,128)(2,1)}), bf16[1024,1536]{1,0:T(8,128)(2,1)}) %all-gather.24.cloned.1.call-update) | async-done | bytes 3145744 | tf_op jit(solution)/shard_map/all_gather | solution.py:116
  1117.9 121.9 %while.227 = (s32[]{:T(128)}, f32[12,64,128]{2,1,0:T(8,128)S(1)}, f32[4,256,12,64]{1,0,3,2:T(4,128)}, f32[4,256,12]{1,0,2:T(4,128)S(1)}, f32[4,256,12]{1,0,2:T(4...) while((s32[]{:T(128)}, f32[12,64,128]{2,1,0:T(8,128)S(1)}, ...), condition=%wide.region_28.29_spmd.clone, body=%wide.region_25.28_spmd.clone.sunk | while | flops 1314002944 | bytes 11398228 | solution.py:63
  1349.8 115.4 %while.232 = (s32[]{:T(128)}, f32[12,64,128]{2,1,0:T(8,128)S(1)}, f32[4,256,12,64]{1,0,3,2:T(4,128)}, f32[4,12,64,128]{3,2,1,0:T(8,128)}, f32[4,256,12]{1,2,0:T(...) while((s32[]{:T(128)}, f32[12,64,128]{2,1,0:T(8,128)S(1)}, ...), condition=%wide.region_36.38_spmd.clone.clone, body=%wide.region_33.37_spmd.clone.clone.sunk | while | flops 1314035712 | bytes 11301477 | solution.py:63
  1477.4 193.1 %while.228 = (s32[]{:T(128)}, f32[12,64,128]{2,1,0:T(8,128)S(1)}, f32[4,256,12,64]{1,0,3,2:T(4,128)}, f32[4,256,12]{1,0,2:T(4,128)S(1)}, f32[4,256,12]{1,0,2:T(4...) while((s32[]{:T(128)}, f32[12,64,128]{2,1,0:T(8,128)S(1)}, ...), condition=%wide.region_51.53_spmd.clone, body=%wide.region_39.52_spmd.clone.sunk | while | flops 3038771200 | bytes 26081692 | solution.py:63
  1722.3 51.8 %reduce-scatter.45.cloned.1.call-done = bf16[256,1536]{1,0:T(8,128)(2,1)} async-done(((bf16[1024,1536]{1,0:T(8,128)(2,1)}), bf16[256,1536]{1,0:T(8,128)(2,1)}) %reduce-scatter.45.cloned.1.call-update) | async-done | bytes 786448 | tf_op jit(solution)/shard_map/reduce_scatter | solution.py:207
  1806.8 61.6 %all-gather.28.cloned.1.call-done = bf16[1024,1536]{1,0:T(8,128)(2,1)} async-done(((bf16[256,1536]{1,0:T(8,128)(2,1)}), bf16[1024,1536]{1,0:T(8,128)(2,1)}) %all-gather.28.cloned.1.call-update) | async-done | bytes 3145744 | tf_op jit(solution)/shard_map/all_gather | solution.py:169
  1913.3 121.1 %while.233 = (s32[]{:T(128)}, f32[12,64,128]{2,1,0:T(8,128)S(1)}, f32[4,256,12,64]{1,0,3,2:T(4,128)}, f32[4,12,64,128]{3,2,1,0:T(8,128)}, f32[4,256,12]{1,2,0:T(...) while((s32[]{:T(128)}, f32[12,64,128]{2,1,0:T(8,128)S(1)}, ...), condition=%wide.region_58.60_spmd.clone.clone, body=%wide.region_55.59_spmd.clone.clone.sunk | while | flops 1314035712 | bytes 11301477 | solution.py:63
  2044.4 193.3 %while.229 = (s32[]{:T(128)}, f32[12,64,128]{2,1,0:T(8,128)S(1)}, f32[4,256,12,64]{1,0,3,2:T(4,128)}, f32[4,256,12]{1,0,2:T(4,128)S(1)}, f32[4,256,12]{1,0,2:T(4...) while((s32[]{:T(128)}, f32[12,64,128]{2,1,0:T(8,128)S(1)}, ...), condition=%wide.region_73.75_spmd.clone, body=%wide.region_61.74_spmd.clone.sunk | while | flops 3038771200 | bytes 26081692 | solution.py:63
  2283.0 58.6 %reduce-scatter.47.cloned.1.call-done = bf16[256,1536]{1,0:T(8,128)(2,1)} async-done(((bf16[1024,1536]{1,0:T(8,128)(2,1)}), bf16[256,1536]{1,0:T(8,128)(2,1)}) %reduce-scatter.47.cloned.1.call-update) | async-done | bytes 786448 | tf_op jit(solution)/shard_map/reduce_scatter | solution.py:207
  2376.7 58.7 %all-gather.30.cloned.1.call-done = bf16[1024,1536]{1,0:T(8,128)(2,1)} async-done(((bf16[256,1536]{1,0:T(8,128)(2,1)}), bf16[1024,1536]{1,0:T(8,128)(2,1)}) %all-gather.30.cloned.1.call-update) | async-done | bytes 3145744 | tf_op jit(solution)/shard_map/all_gather | solution.py:169
  2480.4 121.2 %while.234 = (s32[]{:T(128)}, f32[12,64,128]{2,1,0:T(8,128)S(1)}, f32[4,256,12,64]{1,0,3,2:T(4,128)}, f32[4,12,64,128]{3,2,1,0:T(8,128)}, f32[4,256,12]{1,2,0:T(...) while((s32[]{:T(128)}, f32[12,64,128]{2,1,0:T(8,128)S(1)}, ...), condition=%wide.region_80.82_spmd.clone.clone, body=%wide.region_77.81_spmd.clone.clone.sunk | while | flops 1314035712 | bytes 11301477 | solution.py:63
  2610.9 193.0 %while.230 = (s32[]{:T(128)}, f32[12,64,128]{2,1,0:T(8,128)S(1)}, f32[4,256,12,64]{1,0,3,2:T(4,128)}, f32[4,256,12]{1,0,2:T(4,128)S(1)}, f32[4,256,12]{1,0,2:T(4...) while((s32[]{:T(128)}, f32[12,64,128]{2,1,0:T(8,128)S(1)}, ...), condition=%wide.region_95.97_spmd.clone, body=%wide.region_83.96_spmd.clone.sunk | while | flops 3038771200 | bytes 26081692 | solution.py:63
  2849.2 58.7 %reduce-scatter.49.cloned.1.call-done = bf16[256,1536]{1,0:T(8,128)(2,1)} async-done(((bf16[1024,1536]{1,0:T(8,128)(2,1)}), bf16[256,1536]{1,0:T(8,128)(2,1)}) %reduce-scatter.49.cloned.1.call-update) | async-done | bytes 786448 | tf_op jit(solution)/shard_map/reduce_scatter | solution.py:207
  3045.7 121.3 %while.235 = (s32[]{:T(128)}, f32[12,64,128]{2,1,0:T(8,128)S(1)}, f32[4,256,12,64]{1,0,3,2:T(4,128)}, f32[4,12,64,128]{3,2,1,0:T(8,128)}, f32[4,256,12]{1,2,0:T(...) while((s32[]{:T(128)}, f32[12,64,128]{2,1,0:T(8,128)S(1)}, ...), condition=%wide.region_102.104_spmd.clone.clone, body=%wide.region_99.103_spmd.clone.clone.sunk | while | flops 1314035712 | bytes 11301477 | solution.py:63
  3176.2 193.0 %while.231 = (s32[]{:T(128)}, f32[12,64,128]{2,1,0:T(8,128)S(1)}, f32[4,256,12,64]{1,0,3,2:T(4,128)}, f32[4,256,12]{1,0,2:T(4,128)S(1)}, f32[4,256,12]{1,0,2:T(4...) while((s32[]{:T(128)}, f32[12,64,128]{2,1,0:T(8,128)S(1)}, ...), condition=%wide.region_117.119_spmd.clone, body=%wide.region_105.118_spmd.clone.sunk | while | flops 3038771200 | bytes 26081692 | solution.py:63
  3572.1 35.7 reduce-scatter.77.cloned.1.call-done
  3643.4 35.8 reduce-scatter.63.cloned.1.call-done
  3679.2 35.4 reduce-scatter.65.cloned.1.call-done
  3714.7 35.8 reduce-scatter.67.cloned.1.call-done
  3786.1 35.7 reduce-scatter.55.cloned.1.call-done
  3821.8 35.7 reduce-scatter.57.cloned.1.call-done
  3857.5 35.8 reduce-scatter.59.cloned.1.call-done
  3896.1 59.6 %reduce-scatter.51.cloned.1.call-done = bf16[256,1536]{1,0:T(8,128)(2,1)} async-done(((bf16[1024,1536]{1,0:T(8,128)(2,1)}), bf16[256,1536]{1,0:T(8,128)(2,1)}) %reduce-scatter.51.cloned.1.call-update) | async-done | bytes 786448 | tf_op jit(solution)/shard_map/reduce_scatter | solution.py:207
  (2659 shorter events, 2965.7 us)
Async XLA Ops:
  12.5 243.7 %all-gather.16.cloned.1.call-start = ((), (), s32[]{:S(2)}) async-start(), calls=%async_computation.28 | async-start | bytes 2949120 | tf_op jit(solution)/shard_map/all_gather | solution.py:292
  13.2 259.8 %all-gather.18.cloned.1.call-start = ((), (), s32[]{:S(2)}) async-start(), calls=%async_computation.29 | async-start | bytes 2949120 | tf_op jit(solution)/shard_map/all_gather | solution.py:296
  13.8 325.5 %reduce-scatter.37.cloned.1.call-start = ((), (), s32[]{:S(2)}) async-start(), calls=%async_computation.30 | async-start | bytes 3932160 | tf_op jit(solution)/shard_map/reduce_scatter | solution.py:138
  280.1 152.0 %all-gather.20.cloned.1.call-start = ((), (), s32[]{:S(2)}) async-start(), calls=%async_computation.31 | async-start | bytes 3932160 | tf_op jit(solution)/shard_map/all_gather | solution.py:116
  367.2 299.6 %reduce-scatter.39.cloned.1.call-start = ((), (), s32[]{:S(2)}) async-start(), calls=%async_computation.32 | async-start | bytes 3932160 | tf_op jit(solution)/shard_map/reduce_scatter | solution.py:138
  607.5 151.4 %all-gather.22.cloned.1.call-start = ((), (), s32[]{:S(2)}) async-start(), calls=%async_computation.33 | async-start | bytes 3932160 | tf_op jit(solution)/shard_map/all_gather | solution.py:116
  694.0 300.1 %reduce-scatter.41.cloned.1.call-start = ((), (), s32[]{:S(2)}) async-start(), calls=%async_computation.34 | async-start | bytes 3932160 | tf_op jit(solution)/shard_map/reduce_scatter | solution.py:138
  1018.9 276.5 %all-gather.26.cloned.1.call-start = ((), (), s32[]{:S(2)}) async-start(), calls=%async_computation.37 | async-start | bytes 3932160 | tf_op jit(solution)/shard_map/all_gather | solution.py:169
  1021.9 752.1 %reduce-scatter.45.cloned.1.call-start = ((), (), s32[]{:S(2)}) async-start(), calls=%async_computation.38 | async-start | bytes 3932160 | tf_op jit(solution)/shard_map/reduce_scatter | solution.py:207
  1715.1 153.4 %all-gather.28.cloned.1.call-start = ((), (), s32[]{:S(2)}) async-start(), calls=%async_computation.39 | async-start | bytes 3932160 | tf_op jit(solution)/shard_map/all_gather | solution.py:169
  1805.4 536.2 %reduce-scatter.47.cloned.1.call-start = ((), (), s32[]{:S(2)}) async-start(), calls=%async_computation.40 | async-start | bytes 3932160 | tf_op jit(solution)/shard_map/reduce_scatter | solution.py:207
  2282.4 153.0 %all-gather.30.cloned.1.call-start = ((), (), s32[]{:S(2)}) async-start(), calls=%async_computation.41 | async-start | bytes 3932160 | tf_op jit(solution)/shard_map/all_gather | solution.py:169
  2372.4 535.6 %reduce-scatter.49.cloned.1.call-start = ((), (), s32[]{:S(2)}) async-start(), calls=%async_computation.42 | async-start | bytes 3932160 | tf_op jit(solution)/shard_map/reduce_scatter | solution.py:207
  2848.6 152.3 %all-gather.32.cloned.1.call-start = ((), (), s32[]{:S(2)}) async-start(), calls=%async_computation.43 | async-start | bytes 3932160 | tf_op jit(solution)/shard_map/all_gather | solution.py:169
  2938.0 571.0 %reduce-scatter.79.cloned.1.call-start = ((), (), s32[]{:S(2)}) async-start(), calls=%async_computation.58 | async-start | bytes 491520
  2950.1 559.9 %reduce-scatter.43.cloned.1.call-start = ((), (), s32[]{:S(2)}) async-start(), calls=%async_computation.36 | async-start | bytes 3932160 | tf_op jit(solution)/shard_map/reduce_scatter | solution.py:138
  2956.6 563.7 %reduce-scatter.81.cloned.1.call-start = ((), (), s32[]{:S(2)}) async-start(), calls=%async_computation.59 | async-start | bytes 491520
  2962.1 562.9 %reduce-scatter.83.cloned.1.call-start = ((), (), s32[]{:S(2)}) async-start(), calls=%async_computation.60 | async-start | bytes 491520
  2965.6 579.7 %reduce-scatter.87.cloned.1.call-start = ((), (), s32[]{:S(2)}) async-start(), calls=%async_computation.62 | async-start | bytes 139264
  3387.9 158.8 %reduce-scatter.85.cloned.1.call-start = ((), (), s32[]{:S(2)}) async-start(), calls=%async_computation.61 | async-start | bytes 491520
  3422.8 149.3 %reduce-scatter.71.cloned.1.call-start = ((), (), s32[]{:S(2)}) async-start(), calls=%async_computation.54 | async-start | bytes 2949120 | tf_op jit(solution)/shard_map/reduce_scatter | solution.py:350
  3428.5 179.3 %reduce-scatter.77.cloned.1.call-start = ((), (), s32[]{:S(2)}) async-start(), calls=%async_computation.57 | async-start | bytes 2949120 | tf_op jit(solution)/shard_map/reduce_scatter | solution.py:350
  3435.2 208.2 %reduce-scatter.61.cloned.1.call-start = ((), (), s32[]{:S(2)}) async-start(), calls=%async_computation.49 | async-start | bytes 2949120 | tf_op jit(solution)/shard_map/reduce_scatter | solution.py:344
  3441.4 237.9 %reduce-scatter.63.cloned.1.call-start = ((), (), s32[]{:S(2)}) async-start(), calls=%async_computation.50 | async-start | bytes 2949120 | tf_op jit(solution)/shard_map/reduce_scatter | solution.py:344
  3447.5 267.2 %reduce-scatter.65.cloned.1.call-start = ((), (), s32[]{:S(2)}) async-start(), calls=%async_computation.51 | async-start | bytes 2949120 | tf_op jit(solution)/shard_map/reduce_scatter | solution.py:344
  3454.6 295.9 %reduce-scatter.67.cloned.1.call-start = ((), (), s32[]{:S(2)}) async-start(), calls=%async_computation.52 | async-start | bytes 2949120 | tf_op jit(solution)/shard_map/reduce_scatter | solution.py:344
  3464.7 321.4 %reduce-scatter.53.cloned.1.call-start = ((), (), s32[]{:S(2)}) async-start(), calls=%async_computation.45 | async-start | bytes 2949120 | tf_op jit(solution)/shard_map/reduce_scatter | solution.py:341
  3470.9 350.9 %reduce-scatter.55.cloned.1.call-start = ((), (), s32[]{:S(2)}) async-start(), calls=%async_computation.46 | async-start | bytes 2949120 | tf_op jit(solution)/shard_map/reduce_scatter | solution.py:341
  3477.3 380.1 %reduce-scatter.57.cloned.1.call-start = ((), (), s32[]{:S(2)}) async-start(), calls=%async_computation.47 | async-start | bytes 2949120 | tf_op jit(solution)/shard_map/reduce_scatter | solution.py:341
  3483.5 409.7 %reduce-scatter.59.cloned.1.call-start = ((), (), s32[]{:S(2)}) async-start(), calls=%async_computation.48 | async-start | bytes 2949120 | tf_op jit(solution)/shard_map/reduce_scatter | solution.py:341
  3490.1 465.6 %reduce-scatter.51.cloned.1.call-start = ((), (), s32[]{:S(2)}) async-start(), calls=%async_computation.44 | async-start | bytes 3932160 | tf_op jit(solution)/shard_map/reduce_scatter | solution.py:207
  3502.2 517.1 %reduce-scatter.69.cloned.1.call-start = ((), (), s32[]{:S(2)}) async-start(), calls=%async_computation.53 | async-start | bytes 1671168 | tf_op jit(solution)/shard_map/reduce_scatter | solution.py:363
  (324 other events, 16206.7 us)
Sparse Core Ops, SparseCore 0:
  9.7 28.4 all-gather.13
  40.3 64.3 all-gather.11
  130.4 24.1 all-gather.17
  280.2 59.0 reduce-scatter.36
  367.3 64.7 all-gather.19
  607.6 59.1 reduce-scatter.38
  694.1 64.7 all-gather.21
  934.9 59.1 reduce-scatter.40
  1019.0 64.7 all-gather.23
  1085.4 62.1 all-gather.25
  1715.2 58.7 reduce-scatter.44
  1805.5 62.8 all-gather.27
  2282.5 59.0 reduce-scatter.46
  2372.5 62.8 all-gather.29
  2848.8 59.1 reduce-scatter.48
  2938.1 62.8 all-gather.31
  3025.1 60.2 reduce-scatter.42
  3388.0 54.3 reduce-scatter.86
  3467.8 33.0 reduce-scatter.72
  3503.5 33.0 reduce-scatter.74
  3539.0 33.0 reduce-scatter.70
  3574.6 33.0 reduce-scatter.76
  3610.3 33.0 reduce-scatter.60
  3646.1 33.0 reduce-scatter.62
  3681.6 33.0 reduce-scatter.64
  3717.4 33.0 reduce-scatter.66
  3753.0 33.0 reduce-scatter.52
  3788.7 33.0 reduce-scatter.54
  3824.3 33.0 reduce-scatter.56
  3860.2 33.0 reduce-scatter.58
  3895.4 60.2 reduce-scatter.50
  3959.8 59.5 reduce-scatter.68
  (5 shorter events, 103.4 us)
where the time goes:
time: 4060 us; the launch traced here: 4030 us
  local copies, waits for them, and re-layouts  1400 us (34%)
  waiting for transfers between devices  1290 us (32%)
  matrix products  776 us (19%)
  other arithmetic  373 us (9%)
  blocking collectives  140 us (3%)
    dynamic_update_slice x160, local copies, waits for them, and re-layouts, ssd_scan(): lax.scan(jax.checkpoint(ssd_block), start_state, pieces)  900 us
    dot_general x64, matrix products, ssd_block(): within = jnp.einsum('ijh,jhp->ihp', mixing, head_values, precision=HIGHEST)  284 us
    all_gather x4, waiting for transfers between devices, layer_forward(): full_normed = lax.all_gather(normed, 'tensor', axis=0, tiled=True)  257 us
    reduce_scatter x4, waiting for transfers between devices, layer_backward(): lax.psum_scatter(summed.astype(jnp.bfloat16), 'tensor', scatter_dimension...  229 us
    reduce_scatter x4, waiting for transfers between devices, layer_forward(): lax.psum_scatter(jnp.einsum('lc,dc->ld', scaled, out_weight, preferred_el...  174 us
    all_gather x4, waiting for transfers between devices, layer_backward(): lax.all_gather(grad_out.astype(jnp.bfloat16), 'tensor', axis=0, tiled=True)  156 us
    reduce_scatter x4, waiting for transfers between devices, body(): lax.psum_scatter(dp_grads[0].astype(jnp.bfloat16), 'dp', scatter_dimensio...  140 us
    reduce_scatter x4, waiting for transfers between devices, body(): lax.psum_scatter(dp_grads[1].astype(jnp.bfloat16), 'dp', scatter_dimensio...  140 us
  transfers between devices with their start and end apart: 43, of which 32 were waited for; matrix products, arithmetic and copies ran while one was open for 23% of the time, Pallas kernels for 0%

commit v1 on v0

v1 whole, which is shorter than its diff:
```python
import functools
import types

import jax
import jax.numpy as jnp
from jax import lax
from jax.experimental import pallas as pl
from jax.experimental.pallas import tpu as pltpu
from jax.sharding import PartitionSpec as P

EPS = 1e-05
PIPE, DP, TENSOR = "pipe", "dp", "tensor"
SEQUENTIAL = "arbitrary"
Bundle = types.SimpleNamespace
HIGHEST = lax.Precision.HIGHEST
BF = jnp.bfloat16
F32 = jnp.float32
HALO = 16
GC = 256
LANES = 128


def nn(a, b):
    return jnp.dot(a, b, preferred_element_type=F32)


def nt(a, b):
    return lax.dot_general(a, b, (((1,), (1,)), ((), ())), preferred_element_type=F32)


def tn(a, b):
    return lax.dot_general(a, b, (((0,), (0,)), ((), ())), preferred_element_type=F32)


def exact(a, b):
    return jnp.dot(a, b, precision=HIGHEST, preferred_element_type=F32)


def sigmoid(v):
    return 1.0 / (1.0 + jnp.exp(-v))


def iota(shape, dim):
    return lax.broadcasted_iota(jnp.int32, shape, dim)


def spread(per_head, width, head_dim):
    lane = iota(per_head.shape, 1)
    parts = []
    for pair in range(width // LANES):
        parts.append(
            jnp.where(lane < head_dim, per_head[:, 2 * pair : 2 * pair + 1], per_head[:, 2 * pair + 1 : 2 * pair + 2])
        )
    return jnp.concatenate(parts, axis=1)


def conv_rows(pre, taps, rows):
    total = taps[4:5, :] + taps[3:4, :] * pre[HALO : HALO + rows, :]
    for k in range(3):
        total = total + taps[k : k + 1, :] * pre[HALO - 3 + k : HALO - 3 + k + rows, :]
    return total


def conv_sums(grad, pre, rows):
    sums = [jnp.sum(grad * pre[HALO - 3 + k : HALO - 3 + k + rows, :], axis=0, keepdims=True) for k in range(4)]
    sums.append(jnp.sum(grad, axis=0, keepdims=True))
    return sums


def conv_transposed(grad, halo, taps, rows):
    ext = jnp.concatenate([grad, halo], axis=0)
    total = taps[3:4, :] * grad
    for k in range(3):
        total = total + taps[k : k + 1, :] * ext[3 - k : 3 - k + rows, :]
    return total


def silu_slope(v):
    s = sigmoid(v)
    return s * (1.0 + v * (1.0 - s))


def group_lanes(values, dst, groups, per_group):
    for g in range(groups):
        dst[g] = values if g == 0 else pltpu.roll(values, LANES - per_group * g, 1)


def group_rows(values, dst, groups, per_group):
    turned = values.T
    for g in range(groups):
        dst[g, 0:per_group, :] = turned[per_group * g : per_group * (g + 1), :]


def scan_front(
    head_dim, nx, wv, ws, wt, pv, ps, ph, vpre_o, spre_o, x_o, bc_o, dtc_o, yw_o, loc_o, sc_s, dt_s, cum_s, cumt_s
):
    g = pl.program_id(0)
    groups = pl.num_programs(0)
    rows = x_o.shape[0]
    state = bc_o.shape[1] // 2
    per_group = GC // head_dim

    @pl.when(g == 0)
    def _():
        spre = nn(nx[...], ws[...])
        spre_o[...] = spre
        conv = conv_rows(spre, ps, rows)
        bc = (conv * sigmoid(conv)).astype(BF)
        bc_o[...] = bc
        scores = nt(bc[:, state:], bc[:, :state])
        lower = iota((rows, rows), 0) >= iota((rows, rows), 1)
        sc_s[...] = jnp.where(lower, scores, 0.0)
        raw = nn(nx[HALO:, :], wt[...]) + ph[0:1, :]
        step = jnp.maximum(raw, 0.0) + jnp.log(1.0 + jnp.exp(-jnp.abs(raw)))
        decay = -step * jnp.exp(ph[1:2, :])
        cum = exact(lower.astype(F32), decay)
        dtc_o[0] = step
        dtc_o[1] = cum
        dtc_o[2] = sigmoid(raw)
        group_lanes(step, dt_s, dt_s.shape[0], per_group)
        group_lanes(cum, cum_s, cum_s.shape[0], per_group)
        group_rows(cum, cumt_s, cumt_s.shape[0], per_group)

    pre = nn(nx[...], wv[...])
    vpre_o[...] = pre
    conv = conv_rows(pre, pv, rows)
    x = conv * sigmoid(conv)
    x_o[...] = x.astype(BF)
    step, cum, cumt = dt_s[g], cum_s[g], cumt_s[g]
    to_end = jnp.exp(cum[rows - 1 : rows, :] - cum)
    xp = (x * spread(step, GC, head_dim)).astype(BF)
    xr = (x * spread(step * to_end, GC, head_dim)).astype(BF)
    loc_o[...] = tn(xr, bc_o[:, :state])
    scores = sc_s[...]
    lane = iota((rows, LANES), 1)
    for pair in range(GC // LANES):
        cols = slice(LANES * pair, LANES * (pair + 1))
        outs = []
        for i in (2 * pair, 2 * pair + 1):
            diff = cum[:, i : i + 1] - cumt[i : i + 1, :]
            mix = (jnp.exp(jnp.minimum(diff, 0.0)) * scores).astype(BF)
            outs.append(nn(mix, xp[:, cols]))
        yw_o[:, cols] = jnp.where(lane < head_dim, outs[0], outs[1]) + pv[6:7, cols] * x[:, cols]


def scan_finish(
    head_dim, nx, wg, wo, yw, s_in, bc, dtc, pv, gate_o, y_o, gg_o, p_o, sq_o, acc_s, sq_s, cum_s
):
    g = pl.program_id(0)
    rows = yw.shape[0]
    state = bc.shape[1] // 2

    @pl.when(g == 0)
    def _():
        group_lanes(dtc[1], cum_s, cum_s.shape[0], GC // head_dim)
        acc_s[...] = jnp.zeros_like(acc_s)
        sq_s[...] = jnp.zeros_like(sq_s)

    gate = nn(nx[HALO:, :], wg[...])
    gate_o[...] = gate
    carried = nt(bc[:, state:], s_in[...])
    y = yw[...] + spread(jnp.exp(cum_s[g]), GC, head_dim) * carried
    y_o[...] = y
    gated = y * (gate * sigmoid(gate))
    gg = (gated * pv[5:6, :]).astype(BF)
    gg_o[...] = gg
    squares = gated * gated
    for part in range(GC // LANES):
        sq_s[...] += squares[:, LANES * part : LANES * (part + 1)]
    acc_s[...] += nt(gg, wo[...])

    @pl.when(g == pl.num_programs(0) - 1)
    def _():
        p_o[...] = acc_s[...].astype(BF)
        sq_o[...] = jnp.broadcast_to(jnp.sum(sq_s[...], axis=1, keepdims=True), sq_o.shape)


def gate_backward(head_dim, gm, wo, y, gate, rowsc, pv, bc, dtc, dy_o, dgate_o, dsl_o, dgain_o, cum_s):
    g = pl.program_id(0)
    state = bc.shape[1] // 2

    @pl.when(g == 0)
    def _():
        group_lanes(dtc[1], cum_s, cum_s.shape[0], GC // head_dim)

    gs = nn(gm[...], wo[...])
    inverse, shrink = rowsc[:, 0:1], rowsc[:, 1:2]
    gv, yv = gate[...], y[...]
    s = sigmoid(gv)
    silu = gv * s
    gated = yv * silu
    dgain = jnp.sum(gs * gated * inverse, axis=0, keepdims=True)
    dgain_o[...] = jnp.broadcast_to(dgain, dgain_o.shape)
    dgated = inverse * (gs * pv[5:6, :]) - gated * shrink
    dgate_o[...] = (dgated * yv * (s * (1.0 + gv * (1.0 - s)))).astype(BF)
    dy = dgated * silu
    dy_o[...] = dy.astype(BF)
    dye = (dy * spread(jnp.exp(cum_s[g]), GC, head_dim)).astype(BF)
    dsl_o[...] = tn(dye, bc[:, state:])


def scan_backward(
    head_dim,
    dy,
    x,
    vpre,
    spre,
    bc,
    dtc,
    s_in,
    g_in,
    pv,
    ps,
    ph,
    dconv_o,
    dsc_o,
    dstep_o,
    vs_o,
    ss_o,
    hs_o,
    sct_s,
    scts_s,
    wsum_s,
    dbc_s,
    dt_s,
    cum_s,
    cumt_s,
    net_s,
    rv_s,
    ddir_s,
    k_s,
    rt_s,
    rall_s,
):
    g = pl.program_id(0)
    rows = x.shape[0]
    state = bc.shape[1] // 2
    per_group = GC // head_dim
    groups = dt_s.shape[0]

    @pl.when(g == 0)
    def _():
        scores = nt(bc[:, :state], bc[:, state:])
        first, second = iota((rows, rows), 0), iota((rows, rows), 1)
        sct_s[...] = jnp.where(second >= first, scores, 0.0)
        scts_s[...] = jnp.where(second > first, scores, 0.0)
        wsum_s[...] = jnp.zeros_like(wsum_s)
        dbc_s[...] = jnp.zeros_like(dbc_s)
        rall_s[...] = jnp.zeros_like(rall_s)
        group_lanes(dtc[0], dt_s, groups, per_group)
        group_lanes(dtc[1], cum_s, groups, per_group)
        group_rows(dtc[1], cumt_s, groups, per_group)

    step, cum, cumt = dt_s[g], cum_s[g], cumt_s[g]
    last = cum[rows - 1 : rows, :]
    to_end = jnp.exp(last - cum)
    stepx = spread(step, GC, head_dim)
    endx = spread(to_end, GC, head_dim)
    fromx = spread(jnp.exp(cum), GC, head_dim)
    xf = x[...].astype(F32)
    dyb = dy[...]
    dyf = dyb.astype(F32)
    xp = (xf * stepx).astype(BF)
    xr = (xf * stepx * endx).astype(BF)
    dyef = dyf * fromx
    dye = dyef.astype(BF)
    gb = nt(bc[:, :state], g_in[...])
    cs = nt(bc[:, state:], s_in[...])
    dbc_s[:, :state] += nn(xr, g_in[...])
    dbc_s[:, state:] += nn(dye, s_in[...])

    lane = iota((rows, LANES), 1)
    wsum = wsum_s[...]
    colsum = jnp.zeros((rows, LANES), F32)
    within = []
    for pair in range(GC // LANES):
        cols = slice(LANES * pair, LANES * (pair + 1))
        xpp, dyp = xp[:, cols], dyb[:, cols]
        outs = []
        for side in range(2):
            i = 2 * pair + side
            mine = (lane < head_dim) if side == 0 else (lane >= head_dim)
            decay = jnp.exp(jnp.minimum(cumt[i : i + 1, :] - cum[:, i : i + 1], 0.0))
            outs.append(nn((decay * sct_s[...]).astype(BF), dyp))
            weight = decay * nt(jnp.where(mine, xpp, jnp.zeros_like(xpp)), dyp)
            wsum = wsum + weight
            pairs = (weight * scts_s[...]).astype(BF)
            colsum = colsum + nn(pairs, (lane == i).astype(BF))
            rt_s[g, i : i + 1, :] = jnp.sum(pairs.astype(F32), axis=0, keepdims=True)
        within.append(jnp.where(lane < head_dim, outs[0], outs[1]))
    wsum_s[...] = wsum
    u = jnp.concatenate(within, axis=1) + endx * gb

    heads = (iota((GC, LANES), 0) // head_dim == iota((GC, LANES), 1)).astype(BF)
    ddir_s[g] = nn((xf * u).astype(BF), heads)
    net_s[g] = nn((dyef * cs).astype(BF), heads) - colsum
    rv_s[g] = step * to_end * nn((xf * gb).astype(BF), heads)
    inner = g_in[...].astype(F32) * s_in[...].astype(F32)
    per_channel = lax.dot_general(
        jnp.ones((8, inner.shape[1]), F32), inner, (((1,), (1,)), ((), ())), precision=HIGHEST, preferred_element_type=F32
    )
    k_s[g] = jnp.exp(last) * exact(per_channel, heads.astype(F32))

    dx = stepx * u + pv[6:7, :] * dyf
    dconv = dx * silu_slope(conv_rows(vpre, pv, rows))
    dconv_o[...] = dconv
    sums = conv_sums(dconv, vpre, rows)
    sums.append(jnp.sum(dyf * xf, axis=0, keepdims=True))
    sums.append(jnp.zeros((2, GC), F32))
    vs_o[...] = jnp.concatenate(sums, axis=0)

    @pl.when(g == pl.num_programs(0) - 1)
    def _():
        first, second = iota((rows, rows), 0), iota((rows, rows), 1)
        net, rv, ddir, const = net_s[0], rv_s[0], ddir_s[0], k_s[0]
        rall_s[0:per_group, :] = rt_s[0, 0:per_group, :]
        for other in range(1, groups):
            shift = per_group * other
            net = net + pltpu.roll(net_s[other], shift, 1)
            rv = rv + pltpu.roll(rv_s[other], shift, 1)
            ddir = ddir + pltpu.roll(ddir_s[other], shift, 1)
            const = const + pltpu.roll(k_s[other], shift, 1)
            rall_s[shift : shift + per_group, :] = rt_s[other, 0:per_group, :]
        net = net + rall_s[...].T
        da = exact((second >= first).astype(F32), net) + exact((second < first).astype(F32), rv) + const[0:1, :]
        rate = jnp.exp(ph[1:2, :])
        dstep = (ddir - da * rate) * dtc[2]
        dstep_o[...] = dstep.astype(BF)
        hs_o[...] = jnp.concatenate(
            [
                jnp.sum(dstep, axis=0, keepdims=True),
                jnp.sum(-da * dtc[0] * rate, axis=0, keepdims=True),
                jnp.zeros((6, LANES), F32),
            ],
            axis=0,
        )
        weights = jnp.where(second >= first, wsum_s[...], 0.0).astype(BF)
        db = dbc_s[:, :state] + nn(weights, bc[:, state:])
        dc = dbc_s[:, state:] + tn(weights, bc[:, :state])
        dsc = jnp.concatenate([db, dc], axis=1) * silu_slope(conv_rows(spre, ps, rows))
        dsc_o[...] = dsc
        ssums = conv_sums(dsc, spre, rows)
        ssums.append(jnp.zeros((3, 2 * state), F32))
        ss_o[...] = jnp.concatenate(ssums, axis=0)


def conv_backward(dconv, halo_v, dsc, halo_s, dgate, dstep, pv, ps, wv, wg, ws, wt, dval_o, dst_o, p_o, acc_s):
    g = pl.program_id(0)
    rows = dconv.shape[0]

    @pl.when(g == 0)
    def _():
        dst = conv_transposed(dsc[...], halo_s[...], ps, rows).astype(BF)
        dst_o[...] = dst
        acc_s[...] = nt(dst, ws[...]) + nt(dstep[...], wt[...])

    dval = conv_transposed(dconv[...], halo_v[...], pv, rows).astype(BF)
    dval_o[...] = dval
    acc_s[...] += nt(dval, wv[...]) + nt(dgate[...], wg[...])

    @pl.when(g == pl.num_programs(0) - 1)
    def _():
        p_o[...] = acc_s[...].astype(BF)


def whole(shape):
    return pl.BlockSpec(shape, lambda g: (0,) * len(shape))


def by_cols(rows):
    return pl.BlockSpec((rows, GC), lambda g: (0, g))


def by_rows(cols):
    return pl.BlockSpec((GC, cols), lambda g: (g, 0))


def call(kernel, groups, ins, outs, scratch, flops, traffic, exps=0):
    arrays, in_specs = zip(*ins)
    shapes, out_specs = zip(*outs)
    return pl.pallas_call(
        kernel,
        grid=(groups,),
        in_specs=list(in_specs),
        out_specs=list(out_specs),
        out_shape=[jax.ShapeDtypeStruct(s, d) for s, d in shapes],
        scratch_shapes=scratch,
        cost_estimate=pl.CostEstimate(flops=flops, bytes_accessed=traffic, transcendentals=exps),
        compiler_params=pltpu.CompilerParams(vmem_limit_bytes=40 * 2**20, dimension_semantics=(SEQUENTIAL,)),
    )(*arrays)


def front_call(nx, w, par, head_dim, state):
    rows, width = nx.shape[0] - HALO, w.value.shape[1]
    model = nx.shape[1]
    groups = width // GC
    return call(
        functools.partial(scan_front, head_dim),
        groups,
        [
            (nx, whole(nx.shape)),
            (w.value, by_cols(model)),
            (w.state, whole(w.state.shape)),
            (w.step, whole(w.step.shape)),
            (par.value, by_cols(8)),
            (par.state, whole(par.state.shape)),
            (par.head, whole(par.head.shape)),
        ],
        [
            (((rows + HALO, width), F32), by_cols(rows + HALO)),
            (((rows + HALO, 2 * state), F32), whole((rows + HALO, 2 * state))),
            (((rows, width), BF), by_cols(rows)),
            (((rows, 2 * state), BF), whole((rows, 2 * state))),
            (((3, rows, LANES), F32), whole((3, rows, LANES))),
            (((rows, width), F32), by_cols(rows)),
            (((width, state), F32), by_rows(state)),
        ],
        [
            pltpu.VMEM((rows, rows), F32),
            pltpu.VMEM((groups, rows, LANES), F32),
            pltpu.VMEM((groups, rows, LANES), F32),
            pltpu.VMEM((groups, 8, rows), F32),
        ],
        2 * rows * model * (width + 3 * LANES) + 4 * rows * rows * width,
        2 * model * width + 12 * rows * width,
        rows * rows * width // head_dim,
    )


def finish_call(nx, w, par, yw, s_in, bc, dtc, head_dim):
    rows, width = yw.shape
    model = nx.shape[1]
    groups = width // GC
    state = s_in.shape[1]
    return call(
        functools.partial(scan_finish, head_dim),
        groups,
        [
            (nx, whole(nx.shape)),
            (w.gate, by_cols(model)),
            (w.out, by_cols(model)),
            (yw, by_cols(rows)),
            (s_in, by_rows(state)),
            (bc, whole(bc.shape)),
            (dtc, whole(dtc.shape)),
            (par.value, by_cols(8)),
        ],
        [
            (((rows, width), F32), by_cols(rows)),
            (((rows, width), F32), by_cols(rows)),
            (((rows, width), BF), by_cols(rows)),
            (((rows, model), BF), whole((rows, model))),
            (((rows, LANES), F32), whole((rows, LANES))),
        ],
        [
            pltpu.VMEM((rows, model), F32),
            pltpu.VMEM((rows, LANES), F32),
            pltpu.VMEM((groups, rows, LANES), F32),
        ],
        4 * rows * model * width,
        4 * model * width + 14 * rows * width,
    )


def gate_call(gm, w, par, y, gate, rowsc, bc, dtc, head_dim):
    rows, width = y.shape
    model = gm.shape[1]
    groups = width // GC
    state = bc.shape[1] // 2
    return call(
        functools.partial(gate_backward, head_dim),
        groups,
        [
            (gm, whole(gm.shape)),
            (w.out, by_cols(model)),
            (y, by_cols(rows)),
            (gate, by_cols(rows)),
            (rowsc, whole(rowsc.shape)),
            (par.value, by_cols(8)),
            (bc, whole(bc.shape)),
            (dtc, whole(dtc.shape)),
        ],
        [
            (((rows, width), BF), by_cols(rows)),
            (((rows, width), BF), by_cols(rows)),
            (((width, state), F32), by_rows(state)),
            (((8, width), F32), by_cols(8)),
        ],
        [pltpu.VMEM((groups, rows, LANES), F32)],
        2 * rows * model * width,
        2 * model * width + 14 * rows * width,
    )


def backward_call(dy, x, vpre, spre, bc, dtc, s_in, g_in, par, head_dim):
    rows, width = x.shape
    groups = width // GC
    state = bc.shape[1] // 2
    lanes = pltpu.VMEM((groups, rows, LANES), F32)
    square = pltpu.VMEM((rows, rows), F32)
    return call(
        functools.partial(scan_backward, head_dim),
        groups,
        [
            (dy, by_cols(rows)),
            (x, by_cols(rows)),
            (vpre, by_cols(rows + HALO)),
            (spre, whole(spre.shape)),
            (bc, whole(bc.shape)),
            (dtc, whole(dtc.shape)),
            (s_in, by_rows(state)),
            (g_in, by_rows(state)),
            (par.value, by_cols(8)),
            (par.state, whole(par.state.shape)),
            (par.head, whole(par.head.shape)),
        ],
        [
            (((rows, width), F32), by_cols(rows)),
            (((rows, 2 * state), F32), whole((rows, 2 * state))),
            (((rows, LANES), BF), whole((rows, LANES))),
            (((8, width), F32), by_cols(8)),
            (((8, 2 * state), F32), whole((8, 2 * state))),
            (((8, LANES), F32), whole((8, LANES))),
        ],
        [
            square,
            square,
            square,
            pltpu.VMEM((rows, 2 * state), F32),
            lanes,
            lanes,
            pltpu.VMEM((groups, 8, rows), F32),
            lanes,
            lanes,
            lanes,
            pltpu.VMEM((groups, 8, LANES), F32),
            pltpu.VMEM((groups, 8, rows), F32),
            pltpu.VMEM((LANES, rows), F32),
        ],
        12 * rows * rows * width,
        14 * rows * width,
        3 * rows * rows * width // head_dim,
    )


def conv_call(dconv, halo, dsc, dgate, dstep, w, par):
    rows, width = dconv.shape
    model = w.value.shape[0]
    groups = width // GC
    states = dsc.shape[1]
    halo_v, halo_s = halo[:, :width], halo[:, width:]
    return call(
        conv_backward,
        groups,
        [
            (dconv, by_cols(rows)),
            (halo_v, by_cols(8)),
            (dsc, whole(dsc.shape)),
            (halo_s, whole(halo_s.shape)),
            (dgate, by_cols(rows)),
            (dstep, whole(dstep.shape)),
            (par.value, by_cols(8)),
            (par.state, whole(par.state.shape)),
            (w.value, by_cols(model)),
            (w.gate, by_cols(model)),
            (w.state, whole(w.state.shape)),
            (w.step, whole(w.step.shape)),
        ],
        [
            (((rows, width), BF), by_cols(rows)),
            (((rows, states), BF), whole((rows, states))),
            (((rows, model), BF), whole((rows, model))),
        ],
        [pltpu.VMEM((rows, model), F32)],
        4 * rows * model * width,
        4 * model * width + 10 * rows * width,
    )


def swap_pipe(value):
    return lax.ppermute(value, PIPE, [(0, 1), (1, 0)])


def shift_tensor(value, by):
    count = lax.axis_size(TENSOR)
    return lax.ppermute(value, TENSOR, [(i, i + by) for i in range(count) if 0 <= i + by < count])


def flip_dp(value, bit):
    return lax.ppermute(value, DP, [(i, i ^ bit) for i in range(lax.axis_size(DP))])


def dp_bits():
    bits, bit = [], 1
    while bit < lax.axis_size(DP):
        bits.append(bit)
        bit *= 2
    return bits


def gather_tensor(piece):
    count, me = lax.axis_size(TENSOR), lax.axis_index(TENSOR)
    rows, cols = piece.shape
    right, left = [piece], [piece]
    for _ in range(count - 1):
        right.append(shift_tensor(right[-1], 1))
        left.append(shift_tensor(left[-1], -1))
    full = jnp.zeros((rows, count * cols), piece.dtype)
    for k in range(count):
        part = piece if k == 0 else jnp.where(me >= k, right[k], left[count - k])
        full = lax.dynamic_update_slice(full, part, (0, lax.rem(me - k + count, count) * cols))
    return full


def gather_dp(piece):
    count, me = lax.axis_size(DP), lax.axis_index(DP)
    rows, cols = piece.shape
    held = {0: piece}
    for bit in reversed(dp_bits()):
        for offset in list(held):
            held[offset ^ bit] = flip_dp(held[offset], bit)
    full = jnp.zeros((count * rows, cols), piece.dtype)
    for offset, part in held.items():
        full = lax.dynamic_update_slice(full, part, ((me ^ offset) * rows, 0))
    return full


def add_low(a, b):
    return (a.astype(F32) + b.astype(F32)).astype(a.dtype)


def reduce_dp(value):
    me = lax.axis_index(DP)
    count = lax.axis_size(DP)
    rows, cols = value.shape[0] // count, value.shape[1]
    for bit in dp_bits():
        count //= 2
        split = value.reshape(count, 2, rows, cols)
        mine = (me // bit) % 2
        keep = lax.dynamic_index_in_dim(split, mine, 1, keepdims=False)
        send = lax.dynamic_index_in_dim(split, 1 - mine, 1, keepdims=False)
        value = add_low(keep, flip_dp(send, bit)).reshape(count * rows, cols)
    return value


def reduce_tensor(take):
    count, me = lax.axis_size(TENSOR), lax.axis_index(TENSOR)
    moving_right = moving_left = None
    for k in range(count - 1, 0, -1):
        right, left = take(jnp.minimum(me + k, count - 1)), take(jnp.maximum(me - k, 0))
        if moving_right is not None:
            right, left = add_low(right, moving_right), add_low(left, moving_left)
        moving_right, moving_left = shift_tensor(right, 1), shift_tensor(left, -1)
    own = take(me)
    if moving_right is None:
        return own.astype(F32)
    return own.astype(F32) + moving_right.astype(F32) + moving_left.astype(F32)


def take_cols(value):
    width = value.shape[1] // lax.axis_size(TENSOR)
    return lambda j: lax.dynamic_slice_in_dim(value, j * width, width, 1)


def take_first(value):
    return lambda j: lax.dynamic_index_in_dim(value, j, 0, keepdims=False)


def sum_all_dp(value):
    for bit in dp_bits():
        value = value + flip_dp(value, bit)
    return value


def sum_all_tensor(value):
    count, bit = lax.axis_size(TENSOR), 1
    while bit < count:
        value = value + lax.ppermute(value, TENSOR, [(i, i ^ bit) for i in range(count)])
        bit *= 2
    return value


MESH = pl.DeviceIdType.MESH
VMEM_LIMIT = 60 * 2**20


def remote(src, dst, send, recv, axis, index):
    return pltpu.make_async_remote_copy(
        src_ref=src, dst_ref=dst, send_sem=send, recv_sem=recv, device_id={axis: index}, device_id_type=MESH
    )


def greet(partners):
    barrier = pltpu.get_barrier_semaphore()
    for axis, index in partners:
        pl.semaphore_signal(barrier, inc=1, device_id={axis: index}, device_id_type=MESH)
    pl.semaphore_wait(barrier, len(partners))


def ring_neighbours(count):
    t = lax.axis_index(TENSOR)
    return [(TENSOR, lax.rem(t + 1, count)), (TENSOR, lax.rem(t + count - 1, count))]


def aligned(index, size):
    return pl.ds(pl.multiple_of(index * size, size), size)


def gather_weights(count, *refs):
    (value, gate, out, step, state, chan, shared, wv, wg, wo, wt, ws, ch, sh) = refs[:14]
    (own_sem, xs_sem, xr_sem, right_sem, left_sem, zr_sem, ys_sem, yr_sem, cs_sem, cr_sem) = refs[14:24]
    (st_own, st_xs, st_xr, st_ys, st_yr, st_cs, st_cr, ch_s, ch_r) = refs[24:]
    p, d, t = lax.axis_index(PIPE), lax.axis_index(DP), lax.axis_index(TENSOR)
    y, c = d // 2, lax.rem(d, 2)
    y_mate, core_mate, far_mate = 2 * (1 - y) + c, 2 * y + 1 - c, 2 * (1 - y) + 1 - c
    sources, targets = (value, gate, out, step), (wv, wg, wo, wt)
    kinds = len(sources)
    rows = value.shape[0]

    def half(kind):
        return sources[kind].shape[1] // 2

    def region(item, row, col):
        kind = item % kinds
        return targets[kind].at[item // kinds, aligned(row, rows), aligned(col, half(kind))]

    def strip(item, row):
        return targets[item % kinds].at[item // kinds, aligned(row, rows), :]

    def own_copy(w):
        src = sources[w].at[:, aligned(p, half(w))]
        return pltpu.make_async_copy(src, targets[w].at[p, aligned(d, rows), aligned(t, half(w))], own_sem.at[w])

    def swap_copy(w):
        src = sources[w].at[:, aligned(1 - p, half(w))]
        dst = targets[w].at[p, aligned(d, rows), aligned(t, half(w))]
        return remote(src, dst, xs_sem.at[w], xr_sem.at[w], PIPE, 1 - p)

    def z_copy(item, src, by, sem):
        ref = region(item, d, src)
        return remote(ref, ref, sem.at[item, src], zr_sem.at[item, src], TENSOR, t + by)

    def y_copy(item, src):
        ref = region(item, d, src)
        return remote(ref, ref, ys_sem.at[item, src], yr_sem.at[item, src], DP, y_mate)

    def core_copy(item, which):
        ref = strip(item, d if which == 0 else y_mate)
        return remote(ref, ref, cs_sem.at[item, which], cr_sem.at[item, which], DP, core_mate)

    def y_arrival(item, src):
        ref = region(item, y_mate, src)
        return remote(ref, ref, ys_sem.at[item, src], yr_sem.at[item, src], DP, y_mate)

    def core_arrival(item, which):
        ref = strip(item, core_mate if which == 0 else far_mate)
        return remote(ref, ref, cs_sem.at[item, which], cr_sem.at[item, which], DP, core_mate)

    def swap_arrival(w):
        ref = targets[w].at[1 - p, aligned(d, rows), aligned(t, half(w))]
        return remote(sources[w].at[:, aligned(1 - p, half(w))], ref, xs_sem.at[w], xr_sem.at[w], PIPE, 1 - p)

    def state_rows(layer, row):
        return ws.at[layer, aligned(row, rows), :]

    small = ((state, state_rows(p, d), state_rows(1 - p, d)), (chan, ch.at[p, t], ch.at[1 - p, t]), (shared, sh.at[p], sh.at[1 - p]))

    def small_own(k):
        return pltpu.make_async_copy(small[k][0], small[k][1], st_own.at[k])

    def small_swap(k):
        return remote(small[k][0], small[k][1], st_xs.at[k], st_xr.at[k], PIPE, 1 - p)

    def small_arrival(k):
        return remote(small[k][0], small[k][2], st_xs.at[k], st_xr.at[k], PIPE, 1 - p)

    def state_y(layer):
        ref = state_rows(layer, d)
        return remote(ref, ref, st_ys.at[layer], st_yr.at[layer], DP, y_mate)

    def state_y_arrival(layer):
        ref = state_rows(layer, y_mate)
        return remote(ref, ref, st_ys.at[layer], st_yr.at[layer], DP, y_mate)

    def state_core(layer, which):
        ref = state_rows(layer, d if which == 0 else y_mate)
        return remote(ref, ref, st_cs.at[layer, which], st_cr.at[layer, which], DP, core_mate)

    def state_core_arrival(layer, which):
        ref = state_rows(layer, core_mate if which == 0 else far_mate)
        return remote(ref, ref, st_cs.at[layer, which], st_cr.at[layer, which], DP, core_mate)

    def chan_copy(k):
        ref = ch.at[:, t]
        return remote(ref, ref, ch_s.at[k], ch_r.at[k], TENSOR, lax.rem(t + k, count))

    def chan_arrival(k):
        ref = ch.at[:, lax.rem(t - k + count, count)]
        return remote(ref, ref, ch_s.at[k], ch_r.at[k], TENSOR, lax.rem(t + k, count))

    def begin(item):
        if item < kinds:
            own_copy(item).wait()
            swap_arrival(item).wait_recv()

        @pl.when(t < count - 1)
        def _():
            z_copy(item, t, 1, right_sem).start()

        @pl.when(t > 0)
        def _():
            z_copy(item, t, -1, left_sem).start()

        y_copy(item, t).start()

    def relay(item):
        for hop in range(1, count):
            lower, upper = t - hop, t + hop

            @pl.when(lower >= 0)
            def _():
                z_copy(item, lower, 1, right_sem).wait_recv()

                @pl.when(t < count - 1)
                def _():
                    z_copy(item, lower, 1, right_sem).start()

                y_copy(item, lower).start()

            @pl.when(upper < count)
            def _():
                z_copy(item, upper, -1, left_sem).wait_recv()

                @pl.when(t > 0)
                def _():
                    z_copy(item, upper, -1, left_sem).start()

                y_copy(item, upper).start()

        core_copy(item, 0).start()

    def share(item):
        for src in range(count):
            y_arrival(item, src).wait_recv()
        core_copy(item, 1).start()

    others = [(TENSOR, lax.rem(t + k, count)) for k in range(1, count)]
    greet(others + [(PIPE, 1 - p), (DP, y_mate), (DP, core_mate)])
    for k in range(3):
        small_swap(k).start()
        small_own(k).start()
    order = [kinds - 1] + list(range(kinds - 1))
    for w in order:
        swap_copy(w).start()
        own_copy(w).start()
    for k in range(3):
        small_own(k).wait()
        small_arrival(k).wait_recv()
    for layer in range(2):
        state_y(layer).start()
        state_core(layer, 0).start()
    for k in range(1, count):
        chan_copy(k).start()
    order = order + [kinds + w for w in order]
    begin(order[0])
    for n, item in enumerate(order):
        if n + 1 < len(order):
            begin(order[n + 1])
        relay(item)
        if n == 0:
            for layer in range(2):
                state_y_arrival(layer).wait_recv()
                state_core(layer, 1).start()
        else:
            share(order[n - 1])
    share(order[-1])
    for k in range(3):
        small_swap(k).wait_send()
    for k in range(1, count):
        chan_copy(k).wait_send()
        chan_arrival(k).wait_recv()
    for layer in range(2):
        state_y(layer).wait_send()
        for which in range(2):
            state_core_arrival(layer, which).wait_recv()
            state_core(layer, which).wait_send()
    for w in range(kinds):
        swap_copy(w).wait_send()
    for item in order:
        for which in range(2):
            core_arrival(item, which).wait_recv()
            core_copy(item, which).wait_send()
        for src in range(count):
            y_copy(item, src).wait_send()

            @pl.when((src <= t) & (t < count - 1))
            def _():
                z_copy(item, src, 1, right_sem).wait_send()

            @pl.when((src >= t) & (t > 0))
            def _():
                z_copy(item, src, -1, left_sem).wait_send()


def gather_call(value, gate, out, step, state, chan, shared, count, groups):
    rows = value.shape[0]
    model = groups * rows
    dma = pltpu.SemaphoreType.DMA
    big = [jax.ShapeDtypeStruct((2, model, count * v.shape[1] // 2), BF) for v in (value, gate, out, step)]
    shapes = big + [
        jax.ShapeDtypeStruct((2, model, state.shape[1]), BF),
        jax.ShapeDtypeStruct((2, count) + chan.shape, F32),
        jax.ShapeDtypeStruct((2,) + shared.shape, F32),
    ]
    return pl.pallas_call(
        functools.partial(gather_weights, count),
        in_specs=[pl.BlockSpec(memory_space=pl.ANY)] * 7,
        out_specs=[pl.BlockSpec(memory_space=pl.ANY)] * 7,
        out_shape=shapes,
        scratch_shapes=[dma((4,))] * 3
        + [dma((8, count))] * 5
        + [dma((8, 2))] * 2
        + [dma((3,))] * 3
        + [dma((2,))] * 2
        + [dma((2, 2))] * 2
        + [dma((count,))] * 2,
        compiler_params=pltpu.CompilerParams(collective_id=0, has_side_effects=True),
    )(value, gate, out, step, state, chan, shared)


def add_into(dst, src, chunk=64):
    def step(i, carry):
        at = aligned(i, chunk)
        dst[at, :] = (dst[at, :].astype(F32) + src[at, :].astype(F32)).astype(BF)
        return carry

    lax.fori_loop(0, dst.shape[0] // chunk, step, 0)


def reduce_grads(count, *refs):
    grads, pack, results, (chan_o, step_o, rest_o) = refs[:6], refs[6], refs[7:10], refs[10:13]
    (own, crecv, yrecv, rrecv, lrecv, xsend, xrecv) = refs[13:20]
    (own_sem, cs_sem, cr_sem, ys_sem, yr_sem, rs_sem, rr_sem, ls_sem, lr_sem, xs_sem, xr_sem) = refs[20:31]
    (total_s, part_s, far_s, sum_ss, sum_rs) = refs[31:]
    p, d, t = lax.axis_index(PIPE), lax.axis_index(DP), lax.axis_index(TENSOR)
    y, c = d // 2, lax.rem(d, 2)
    y_mate, core_mate = 2 * (1 - y) + c, 2 * y + 1 - c
    items, kinds = 6, 3
    rows, half = xsend.shape[1], xsend.shape[2]

    def core_copy(item, row):
        src = grads[item].at[aligned(2 * row + 1 - c, rows), :]
        return remote(src, crecv.at[item, row], cs_sem.at[item, row], cr_sem.at[item, row], DP, core_mate)

    def own_copy(item, row):
        src = grads[item].at[aligned(2 * row + c, rows), :]
        return pltpu.make_async_copy(src, own.at[item % 2, row], own_sem.at[item % 2, row])

    def y_copy(item):
        return remote(crecv.at[item, 1 - y], yrecv.at[item], ys_sem.at[item], yr_sem.at[item], DP, y_mate)

    def right_copy(item, j):
        ref = rrecv.at[item, j]
        return remote(ref, ref, rs_sem.at[item, j], rr_sem.at[item, j], TENSOR, t + 1)

    def left_copy(item, j):
        ref = lrecv.at[item, j]
        return remote(ref, ref, ls_sem.at[item, j], lr_sem.at[item, j], TENSOR, t - 1)

    def x_copy(item):
        return remote(xsend.at[item], xrecv.at[item % kinds], xs_sem.at[item], xr_sem.at[item % kinds], PIPE, 1 - p)

    def near(item):
        for row in range(2):
            own_copy(item, row).wait()
            core_copy(item, row).wait_recv()
            add_into(crecv.at[item, row], own.at[item % 2, row])
        y_copy(item).start()
        if item + 2 < items:
            for row in range(2):
                own_copy(item + 2, row).start()

    def far(item):
        y_copy(item).wait_recv()
        add_into(yrecv.at[item], crecv.at[item, y])

        def column(j):
            return yrecv.at[item, :, aligned(j, half)]

        for j in range(count - 1, 0, -1):

            @pl.when(t < j)
            def _():
                @pl.when(t == 0)
                def _():
                    rrecv[item, j] = column(j)[...]

                @pl.when(t > 0)
                def _():
                    right_copy(item, j).wait_recv()
                    add_into(rrecv.at[item, j], column(j))

                right_copy(item, j).start()

        for j in range(count - 1):

            @pl.when(t > j)
            def _():
                @pl.when(t == count - 1)
                def _():
                    lrecv[item, j] = column(j)[...]

                @pl.when(t < count - 1)
                def _():
                    left_copy(item, j).wait_recv()
                    add_into(lrecv.at[item, j], column(j))

                left_copy(item, j).start()

    def close(item):
        w = item % kinds
        total = xsend.at[item]
        total[...] = yrecv[item, :, aligned(t, half)]

        @pl.when(t > 0)
        def _():
            right_copy(item, t).wait_recv()
            add_into(total, rrecv.at[item, t])

        @pl.when(t < count - 1)
        def _():
            left_copy(item, t).wait_recv()
            add_into(total, lrecv.at[item, t])

        @pl.when(p != item // kinds)
        def _():
            x_copy(item).start()

        @pl.when(p == item // kinds)
        def _():
            results[w][:, aligned(p, half)] = total[...].astype(F32)

    steps, bit = [(DP, core_mate), (DP, y_mate)], 1
    while bit < count:
        steps.append((TENSOR, t + bit * (1 - 2 * lax.rem(t // bit, 2))))
        bit *= 2

    def sum_copy(k):
        axis, index = steps[k]
        return remote(total_s.at[k], part_s.at[k], sum_ss.at[k], sum_rs.at[k], axis, index)

    def pipe_copy():
        k = len(steps)
        return remote(total_s.at[k, 1 - p], far_s, sum_ss.at[k], sum_rs.at[k], PIPE, 1 - p)

    def sum_step(k):
        sum_copy(k).wait_recv()
        total_s[k + 1] = total_s[k] + part_s[k]
        if k + 1 < len(steps):
            sum_copy(k + 1).start()
        else:
            pipe_copy().start()

    def sum_close():
        k = len(steps)
        pipe_copy().wait_recv()
        mine = total_s.at[k, p]
        for ref, where in ((mine, p), (far_s, 1 - p)):
            chan_o[:, aligned(where, half)] = ref[0:8, aligned(t, half)]
            step_o[aligned(where, 8), :] = ref[pl.ds(pl.multiple_of(8 + 8 * t, 8), 8), aligned(d, rows)]
        last = total_s.shape[2] - 8
        row = iota((8, total_s.shape[3]), 0)
        rest_o[...] = mine[last:, :] + jnp.where(row == 0, 0.0, far_s[last:, :])

    others = [axis_index for axis_index in steps if axis_index[0] == TENSOR]
    greet(ring_neighbours(count) + [(PIPE, 1 - p), (DP, y_mate), (DP, core_mate)] + others)
    total_s[0] = pack[...]
    sum_copy(0).start()
    for item in range(items):
        for row in range(2):
            core_copy(item, row).start()
            if item < 2:
                own_copy(item, row).start()
    for k in range(items + 2):
        if k < items:
            near(k)
        if 1 <= k <= items:
            far(k - 1)
        if k >= 2:
            close(k - 2)
        if 1 <= k <= len(steps):
            sum_step(k - 1)
    sum_close()
    for k in range(len(steps)):
        sum_copy(k).wait_send()
    pipe_copy().wait_send()
    for w in range(kinds):
        x_copy(w).wait_recv()
        results[w][:, aligned(1 - p, half)] = xrecv[w].astype(F32)
    for item in range(items):
        for row in range(2):
            core_copy(item, row).wait_send()
        y_copy(item).wait_send()

        @pl.when(p != item // kinds)
        def _():
            x_copy(item).wait_send()

        for j in range(count):

            @pl.when(t < j)
            def _():
                right_copy(item, j).wait_send()

            @pl.when(t > j)
            def _():
                left_copy(item, j).wait_send()


def reduce_call(grads, pack, count, groups):
    model, width = grads[0].shape
    rows, half = model // groups, width // count
    dma = pltpu.SemaphoreType.DMA
    vmem = pltpu.VMEM
    steps = 2 + (count - 1).bit_length()
    inside = pl.BlockSpec(memory_space=pltpu.VMEM)
    return pl.pallas_call(
        functools.partial(reduce_grads, count),
        in_specs=[pl.BlockSpec(memory_space=pl.ANY)] * 6 + [inside],
        out_specs=[inside] * 6,
        out_shape=[jax.ShapeDtypeStruct((rows, 2 * half), F32)] * 3
        + [
            jax.ShapeDtypeStruct((8, 2 * half), F32),
            jax.ShapeDtypeStruct((16, rows), F32),
            jax.ShapeDtypeStruct((8, width), F32),
        ],
        scratch_shapes=[
            vmem((2, 2, rows, width), BF),
            vmem((6, 2, rows, width), BF),
            vmem((6, rows, width), BF),
            vmem((6, count, rows, half), BF),
            vmem((6, count, rows, half), BF),
            vmem((6, rows, half), BF),
            vmem((3, rows, half), BF),
            dma((2, 2)),
            dma((6, 2)),
            dma((6, 2)),
            dma((6,)),
            dma((6,)),
            dma((6, count)),
            dma((6, count)),
            dma((6, count)),
            dma((6, count)),
            dma((6,)),
            dma((3,)),
            vmem((steps + 1,) + pack.shape, F32),
            vmem((steps,) + pack.shape, F32),
            vmem(pack.shape[1:], F32),
            dma((steps + 1,)),
            dma((steps + 1,)),
        ],
        compiler_params=pltpu.CompilerParams(collective_id=1, has_side_effects=True, vmem_limit_bytes=VMEM_LIMIT),
    )(*grads, pack)


def fused_forward(count, head_dim, micro, *refs):
    (tokens, mask, wv, wg, wo, ws, wt, pv, ps, ph, pn) = refs[:11]
    (out_h, low_h, mix_h, inv_o, nx_o, vpre_o, spre_o, x_o, bc_o, dtc_o, gate_o, y_o, gg_o, sin_o) = refs[11:25]
    (nx_s, sc_s, dt_s, cum_s, cumt_s, acc_s, sq_s, psend, precv, sqsend, sqrecv, csend, crecv, hrecv, trecv) = refs[25:40]
    (ps_sem, pr_sem, ss_sem, sr_sem, cs_sem, cr_sem, hs_sem, hr_sem, ts_sem, tr_sem, low_sem, out_sem, mix_sem) = refs[40:]
    q, s, g = pl.program_id(0), pl.program_id(1), pl.program_id(2)
    groups = dt_s.shape[0]
    p, t = lax.axis_index(PIPE), lax.axis_index(TENSOR)
    idx = q * micro + s
    slot = idx * groups + g
    total_idx = 2 * micro
    rows, model = tokens.shape[1], tokens.shape[2]
    state = bc_o.shape[1] // 2
    per_group = GC // head_dim
    inner_total = 2 * groups * GC

    def part_copy(i):
        return remote(psend.at[i], precv.at[i], ps_sem.at[i], pr_sem.at[i], PIPE, 1 - p)

    def square_copy(i):
        return remote(sqsend.at[i], sqrecv.at[i], ss_sem.at[i], sr_sem.at[i], PIPE, 1 - p)

    def chain_copy(i):
        return remote(csend.at[i], crecv.at[i], cs_sem.at[i], cr_sem.at[i], TENSOR, t + 1)

    def halo_copy(i):
        return remote(psend.at[i, rows - HALO :, :], hrecv.at[i], hs_sem.at[i], hr_sem.at[i], TENSOR, t + 1)

    def tokens_copy():
        return remote(tokens.at[:, rows - HALO :, :], trecv, ts_sem.at[0], tr_sem.at[0], TENSOR, t + 1)

    def low_copy(i):
        return pltpu.make_async_copy(psend.at[i], low_h.at[i], low_sem.at[i])

    def out_copy(i):
        return pltpu.make_async_copy(psend.at[i], out_h.at[lax.rem(i, micro)], out_sem.at[i])

    def mix_copy(i):
        return pltpu.make_async_copy(precv.at[i], mix_h.at[i], mix_sem.at[i])

    @pl.when((idx == 0) & (g == 0))
    def _():
        greet(ring_neighbours(count) + [(PIPE, 1 - p)])

        @pl.when(t < count - 1)
        def _():
            tokens_copy().start()

    def normed(u):
        uf = u.astype(F32)
        return (uf * lax.rsqrt(jnp.mean(uf * uf, axis=1, keepdims=True) + EPS) * pn[0:1, :]).astype(BF)

    @pl.when((g == 0) & (q == 0))
    def _():
        nx_s[HALO:, :] = normed(tokens[s])

        @pl.when(t == 0)
        def _():
            nx_s[:HALO, :] = jnp.zeros((HALO, model), BF)

        @pl.when(t > 0)
        def _():
            @pl.when(s == 0)
            def _():
                tokens_copy().wait_recv()

            nx_s[:HALO, :] = normed(trecv[s])

    @pl.when((g == 0) & (q == 1))
    def _():
        nx_s[HALO:, :] = normed(psend[s])

        @pl.when(t == 0)
        def _():
            nx_s[:HALO, :] = jnp.zeros((HALO, model), BF)

        @pl.when(t > 0)
        def _():
            halo_copy(s).wait_recv()
            nx_s[:HALO, :] = normed(hrecv[s])

    @pl.when(g == 0)
    def _():
        nx_o[...] = nx_s[HALO:, :]
        spre = nn(nx_s[...], ws[...])
        spre_o[...] = spre
        conv = conv_rows(spre, ps, rows)
        bc = (conv * sigmoid(conv)).astype(BF)
        bc_o[...] = bc
        scores = nt(bc[:, state:], bc[:, :state])
        lower = iota((rows, rows), 0) >= iota((rows, rows), 1)
        sc_s[...] = jnp.where(lower, scores, 0.0)
        raw = nn(nx_s[HALO:, :], wt[...]) + ph[0:1, :]
        step = jnp.maximum(raw, 0.0) + jnp.log(1.0 + jnp.exp(-jnp.abs(raw)))
        cum = exact(lower.astype(F32), -step * jnp.exp(ph[1:2, :]))
        dtc_o[0] = step
        dtc_o[1] = cum
        dtc_o[2] = sigmoid(raw)
        group_lanes(step, dt_s, groups, per_group)
        group_lanes(cum, cum_s, groups, per_group)
        group_rows(cum, cumt_s, groups, per_group)
        acc_s[...] = jnp.zeros_like(acc_s)
        sq_s[...] = jnp.zeros_like(sq_s)

    pre = nn(nx_s[...], wv[...])
    vpre_o[...] = pre
    conv = conv_rows(pre, pv, rows)
    x = conv * sigmoid(conv)
    x_o[...] = x.astype(BF)
    step, cum, cumt = dt_s[g], cum_s[g], cumt_s[g]
    to_end = jnp.exp(cum[rows - 1 : rows, :] - cum)
    xp = (x * spread(step, GC, head_dim)).astype(BF)
    xr = (x * spread(step * to_end, GC, head_dim)).astype(BF)
    local = tn(xr, bc_o[:, :state])

    @pl.when(t == 0)
    def _():
        sin_o[...] = jnp.zeros_like(sin_o)

    @pl.when(t > 0)
    def _():
        chain_copy(slot).wait_recv()
        sin_o[...] = crecv[slot]

    @pl.when(t < count - 1)
    def _():
        csend[slot] = (through_rows(cumt, rows, head_dim, state) * sin_o[...].astype(F32) + local).astype(BF)
        chain_copy(slot).start()

    scores = sc_s[...]
    lane = iota((rows, LANES), 1)
    within = []
    for pair in range(GC // LANES):
        cols = slice(LANES * pair, LANES * (pair + 1))
        outs = []
        for i in (2 * pair, 2 * pair + 1):
            diff = cum[:, i : i + 1] - cumt[i : i + 1, :]
            mix = (jnp.exp(jnp.minimum(diff, 0.0)) * scores).astype(BF)
            outs.append(nn(mix, xp[:, cols]))
        within.append(jnp.where(lane < head_dim, outs[0], outs[1]))
    gate = nn(nx_s[HALO:, :], wg[...])
    gate_o[...] = gate
    carried = nt(bc_o[:, state:], sin_o[...])
    y = jnp.concatenate(within, axis=1) + pv[6:7, :] * x + spread(jnp.exp(cum), GC, head_dim) * carried
    y_o[...] = y
    gated = y * (gate * sigmoid(gate))
    gg = (gated * pv[5:6, :]).astype(BF)
    gg_o[...] = gg
    squares = gated * gated
    for part in range(GC // LANES):
        sq_s[...] += squares[:, LANES * part : LANES * (part + 1)]
    acc_s[...] += nt(gg, wo[...])

    @pl.when(g == groups - 1)
    def _():
        psend[idx] = acc_s[...].astype(BF)
        sqsend[idx] = jnp.broadcast_to(jnp.sum(sq_s[...], axis=1, keepdims=True), (rows, LANES))
        part_copy(idx).start()
        square_copy(idx).start()

    def finish(i):
        j = lax.rem(i, micro)
        part_copy(i).wait()
        square_copy(i).wait()
        inverse = lax.rsqrt((sqsend[i] + sqrecv[i]) / inner_total + EPS)
        inv_o[i] = inverse
        mixed = inverse[:, 0:1] * (psend[i].astype(F32) + precv[i].astype(F32))
        precv[i] = mixed.astype(BF)
        row_mask = mask[j][:, 0:1]

        @pl.when(i < micro)
        def _():
            psend[i] = (row_mask * (tokens[j].astype(F32) + mixed)).astype(BF)

            @pl.when(t < count - 1)
            def _():
                halo_copy(j).start()

            low_copy(j).start()

        @pl.when(i >= micro)
        def _():
            psend[i] = (row_mask * (psend[j].astype(F32) + mixed)).astype(BF)

        @pl.when(i // micro == p)
        def _():
            out_copy(i).start()

        mix_copy(i).start()

    @pl.when((g == 1) & (idx > 1))
    def _():
        finish(idx - 2)

    @pl.when((g == groups - 1) & (idx == total_idx - 1))
    def _():
        finish(idx - 1)
        finish(idx)
        for i in range(total_idx):
            mix_copy(i).wait()

            @pl.when(i // micro == p)
            def _():
                out_copy(i).wait()

        for i in range(micro):
            low_copy(i).wait()

        @pl.when(t < count - 1)
        def _():
            tokens_copy().wait_send()
            for i in range(micro):
                halo_copy(i).wait_send()

            def drain(i, carry):
                chain_copy(i).wait_send()
                return carry

            lax.fori_loop(0, total_idx * groups, drain, 0)


def through_rows(cumt, rows, head_dim, state):
    end = jnp.exp(cumt[:, rows - 1 : rows])
    parts = [jnp.broadcast_to(end[i : i + 1, :], (head_dim, state)) for i in range(GC // head_dim)]
    return jnp.concatenate(parts, axis=0)


def fused_backward(count, head_dim, micro, *refs):
    (cot, tokens, out0, mask, inv, mix, vpre, spre, x, bc, dtc, gate, y, s_in) = refs[:14]
    (wv, wg, wo, ws, wt, pv, ps, ph, pn) = refs[14:23]
    (grad_h, dval_o, dgate_o, dst_o, dstep_o, sgm_o, vs_o, ss_o, hs_o, norm_o) = refs[23:33]
    (gm_s, rowsc_s, gin_s, halo_s, halo2_s, acc_s, nacc_s) = refs[33:40]
    (sct_s, scts_s, wsum_s, dbc_s, dt_s, cum_s, cumt_s, net_s, rv_s, ddir_s, k_s, rt_s, rall_s) = refs[40:53]
    (psend, precv, csend, crecv, hsend, hrecv, tsend, trecv) = refs[53:61]
    (ps_sem, pr_sem, cs_sem, cr_sem, hs_sem, hr_sem, ts_sem, tr_sem, out_sem) = refs[61:]
    turn, s, g = pl.program_id(0), pl.program_id(1), pl.program_id(2)
    groups = dt_s.shape[0]
    p, t = lax.axis_index(PIPE), lax.axis_index(TENSOR)
    idx = turn * micro + s
    slot = idx * groups + g
    total_idx = 2 * micro
    rows, model = cot.shape[1], cot.shape[2]
    state = bc.shape[1] // 2
    per_group = GC // head_dim
    inner_total = 2 * groups * GC

    def part_copy(i):
        return remote(psend.at[i], precv.at[i], ps_sem.at[i], pr_sem.at[i], PIPE, 1 - p)

    def chain_copy(i):
        return remote(csend.at[i], crecv.at[i], cs_sem.at[i], cr_sem.at[i], TENSOR, t - 1)

    def halo_copy(i):
        return remote(hsend.at[i], hrecv.at[i], hs_sem.at[i], hr_sem.at[i], TENSOR, t - 1)

    def tail_copy(i):
        return remote(tsend.at[i], trecv.at[i], ts_sem.at[i], tr_sem.at[i], TENSOR, t - 1)

    def out_copy(i):
        return pltpu.make_async_copy(psend.at[i], grad_h.at[lax.rem(i, micro)], out_sem.at[i])

    @pl.when((idx == 0) & (g == 0))
    def _():
        greet(ring_neighbours(count) + [(PIPE, 1 - p)])
        nacc_s[...] = jnp.zeros_like(nacc_s)

    @pl.when((g == 0) & (turn == 0))
    def _():
        gm_s[...] = (mask[s][:, 0:1] * cot[s].astype(F32)).astype(BF)

    @pl.when((g == 0) & (turn == 1))
    def _():
        gm_s[...] = (mask[s][:, 0:1] * psend[s].astype(F32)).astype(BF)

    @pl.when(g == 0)
    def _():
        gmf = gm_s[...].astype(F32)
        inverse = inv[...]
        dot = jnp.sum(gmf * mix[...].astype(F32), axis=1, keepdims=True)
        rowsc_s[...] = inverse * inverse * dot / inner_total
        sgm_o[...] = (gmf * inverse[:, 0:1]).astype(BF)
        scores = nt(bc[:, :state], bc[:, state:])
        first, second = iota((rows, rows), 0), iota((rows, rows), 1)
        sct_s[...] = jnp.where(second >= first, scores, 0.0)
        scts_s[...] = jnp.where(second > first, scores, 0.0)
        wsum_s[...] = jnp.zeros_like(wsum_s)
        dbc_s[...] = jnp.zeros_like(dbc_s)
        rall_s[...] = jnp.zeros_like(rall_s)
        acc_s[...] = jnp.zeros_like(acc_s)
        group_lanes(dtc[0], dt_s, groups, per_group)
        group_lanes(dtc[1], cum_s, groups, per_group)
        group_rows(dtc[1], cumt_s, groups, per_group)

    step, cum, cumt = dt_s[g], cum_s[g], cumt_s[g]
    last = cum[rows - 1 : rows, :]
    fromx = spread(jnp.exp(cum), GC, head_dim)

    gs = nn(gm_s[...], wo[...])
    inverse, shrink = inv[:, 0:1], rowsc_s[:, 0:1]
    gv, yv = gate[...], y[...]
    sig = sigmoid(gv)
    silu = gv * sig
    gated = yv * silu
    dgain = jnp.sum(gs * gated * inverse, axis=0, keepdims=True)
    dgated = inverse * (gs * pv[5:6, :]) - gated * shrink
    dgate = (dgated * yv * (sig * (1.0 + gv * (1.0 - sig)))).astype(BF)
    dgate_o[...] = dgate
    dyb = (dgated * silu).astype(BF)
    dyf = dyb.astype(F32)
    dyef = dyf * fromx
    dye = dyef.astype(BF)
    dsl = tn(dye, bc[:, state:])

    @pl.when(t == count - 1)
    def _():
        gin_s[...] = jnp.zeros_like(gin_s)

    @pl.when(t < count - 1)
    def _():
        chain_copy(slot).wait_recv()
        gin_s[...] = crecv[slot]

    @pl.when(t > 0)
    def _():
        csend[slot] = (through_rows(cumt, rows, head_dim, state) * gin_s[...].astype(F32) + dsl).astype(BF)
        chain_copy(slot).start()

    to_end = jnp.exp(last - cum)
    stepx = spread(step, GC, head_dim)
    endx = spread(to_end, GC, head_dim)
    xf = x[...].astype(F32)
    xp = (xf * stepx).astype(BF)
    xr = (xf * stepx * endx).astype(BF)
    gb = nt(bc[:, :state], gin_s[...])
    cs = nt(bc[:, state:], s_in[...])
    dbc_s[:, :state] += nn(xr, gin_s[...])
    dbc_s[:, state:] += nn(dye, s_in[...])

    lane = iota((rows, LANES), 1)
    wsum = wsum_s[...]
    colsum = jnp.zeros((rows, LANES), F32)
    within = []
    for pair in range(GC // LANES):
        cols = slice(LANES * pair, LANES * (pair + 1))
        xpp, dyp = xp[:, cols], dyb[:, cols]
        outs = []
        for side in range(2):
            i = 2 * pair + side
            mine = (lane < head_dim) if side == 0 else (lane >= head_dim)
            decay = jnp.exp(jnp.minimum(cumt[i : i + 1, :] - cum[:, i : i + 1], 0.0))
            outs.append(nn((decay * sct_s[...]).astype(BF), dyp))
            weight = decay * nt(jnp.where(mine, xpp, jnp.zeros_like(xpp)), dyp)
            wsum = wsum + weight
            pairs = (weight * scts_s[...]).astype(BF)
            colsum = colsum + nn(pairs, (lane == i).astype(BF))
            rt_s[g, i : i + 1, :] = jnp.sum(pairs.astype(F32), axis=0, keepdims=True)
        within.append(jnp.where(lane < head_dim, outs[0], outs[1]))
    wsum_s[...] = wsum
    u = jnp.concatenate(within, axis=1) + endx * gb

    heads = (iota((GC, LANES), 0) // head_dim == iota((GC, LANES), 1)).astype(BF)
    ddir_s[g] = nn((xf * u).astype(BF), heads)
    net_s[g] = nn((dyef * cs).astype(BF), heads) - colsum
    rv_s[g] = step * to_end * nn((xf * gb).astype(BF), heads)
    inner = gin_s[...].astype(F32) * s_in[...].astype(F32)
    per_channel = lax.dot_general(
        jnp.ones((8, inner.shape[1]), F32), inner, (((1,), (1,)), ((), ())), precision=HIGHEST, preferred_element_type=F32
    )
    k_s[g] = jnp.exp(last) * exact(per_channel, heads.astype(F32))

    dx = stepx * u + pv[6:7, :] * dyf
    dconv = dx * silu_slope(conv_rows(vpre, pv, rows))

    @pl.when(t > 0)
    def _():
        hsend[slot] = dconv[:8, :]
        halo_copy(slot).start()

    sums = conv_sums(dconv, vpre, rows)
    sums.append(dgain)
    sums.append(jnp.sum(dyf * xf, axis=0, keepdims=True))
    sums.append(jnp.zeros((1, GC), F32))
    vs_o[...] = jnp.concatenate(sums, axis=0)
    acc_s[...] += nt(dgate, wg[...])

    @pl.when(t == count - 1)
    def _():
        halo_s[...] = jnp.zeros_like(halo_s)

    @pl.when(t < count - 1)
    def _():
        halo_copy(slot).wait_recv()
        halo_s[...] = hrecv[slot]

    dval = conv_transposed(dconv, halo_s[...], pv, rows).astype(BF)
    dval_o[...] = dval
    acc_s[...] += nt(dval, wv[...])

    @pl.when(g == groups - 1)
    def _():
        first, second = iota((rows, rows), 0), iota((rows, rows), 1)
        weights = jnp.where(second >= first, wsum_s[...], 0.0).astype(BF)
        db = dbc_s[:, :state] + nn(weights, bc[:, state:])
        dc = dbc_s[:, state:] + tn(weights, bc[:, :state])
        dsc = jnp.concatenate([db, dc], axis=1) * silu_slope(conv_rows(spre, ps, rows))

        @pl.when(t > 0)
        def _():
            tsend[idx] = dsc[:8, :]
            tail_copy(idx).start()

        ssums = conv_sums(dsc, spre, rows)
        ssums.append(jnp.zeros((3, 2 * state), F32))
        ss_o[...] = jnp.concatenate(ssums, axis=0)
        net, rv, ddir, const = net_s[0], rv_s[0], ddir_s[0], k_s[0]
        rall_s[0:per_group, :] = rt_s[0, 0:per_group, :]
        for other in range(1, groups):
            shift = per_group * other
            net = net + pltpu.roll(net_s[other], shift, 1)
            rv = rv + pltpu.roll(rv_s[other], shift, 1)
            ddir = ddir + pltpu.roll(ddir_s[other], shift, 1)
            const = const + pltpu.roll(k_s[other], shift, 1)
            rall_s[shift : shift + per_group, :] = rt_s[other, 0:per_group, :]
        net = net + rall_s[...].T
        da = exact((second >= first).astype(F32), net) + exact((second < first).astype(F32), rv) + const[0:1, :]
        rate = jnp.exp(ph[1:2, :])
        dstep = (ddir - da * rate) * dtc[2]
        dstep_o[...] = dstep.astype(BF)
        hs_o[...] = jnp.concatenate(
            [
                jnp.sum(dstep, axis=0, keepdims=True),
                jnp.sum(-da * dtc[0] * rate, axis=0, keepdims=True),
                jnp.zeros((6, LANES), F32),
            ],
            axis=0,
        )

        @pl.when(t == count - 1)
        def _():
            halo2_s[...] = jnp.zeros_like(halo2_s)

        @pl.when(t < count - 1)
        def _():
            tail_copy(idx).wait_recv()
            halo2_s[...] = trecv[idx]

        dst = conv_transposed(dsc, halo2_s[...], ps, rows).astype(BF)
        dst_o[...] = dst
        psend[idx] = (acc_s[...] + nt(dst, ws[...]) + nt(dstep_o[...], wt[...])).astype(BF)
        part_copy(idx).start()

    def finish(i):
        j = lax.rem(i, micro)
        part_copy(i).wait()
        which = 1 - i // micro
        row_mask = mask[j][:, 0:1]

        def close(u, incoming):
            uf = u.astype(F32)
            grad_normed = psend[i].astype(F32) + precv[i].astype(F32)
            root_inv = lax.rsqrt(jnp.mean(uf * uf, axis=1, keepdims=True) + EPS)
            nacc_s[which] += jnp.broadcast_to(jnp.sum(grad_normed * uf * root_inv, axis=0, keepdims=True), (8, model))
            weighted = grad_normed * pn[which][0:1, :]
            shared = jnp.mean(weighted * uf, axis=1, keepdims=True) * root_inv * root_inv * root_inv
            kept = (row_mask * incoming.astype(F32)).astype(BF).astype(F32)
            psend[i] = (root_inv * weighted - uf * shared + kept).astype(BF)

        @pl.when(i < micro)
        def _():
            close(out0[j], cot[j])

        @pl.when(i >= micro)
        def _():
            close(tokens[j], psend[j])

        @pl.when(which == p)
        def _():
            out_copy(i).start()

    @pl.when((g == 1) & (idx > 1))
    def _():
        finish(idx - 2)

    @pl.when((g == groups - 1) & (idx == total_idx - 1))
    def _():
        finish(idx - 1)
        finish(idx)
        norm_o[...] = nacc_s[...]
        for i in range(total_idx):

            @pl.when(1 - i // micro == p)
            def _():
                out_copy(i).wait()

        @pl.when(t > 0)
        def _():
            for i in range(total_idx):
                tail_copy(i).wait_send()

            def drain(i, carry):
                chain_copy(i).wait_send()
                halo_copy(i).wait_send()
                return carry

            lax.fori_loop(0, total_idx * groups, drain, 0)


def all_of(shape, buffers=2):
    spec = functools.partial(pl.BlockSpec, shape, lambda q, s, g: (0,) * len(shape))
    return spec(pipeline_mode=pl.Buffered(buffers)) if buffers != 2 else spec()


def fused_specs(turned):
    def layer(q):
        return 1 - q if turned else q

    def item(*shape):
        zeros = (0,) * len(shape)
        return pl.BlockSpec((None, None) + shape, lambda q, s, g: (layer(q), s) + zeros)

    def item_cols(rows):
        return pl.BlockSpec((None, None, rows, GC), lambda q, s, g: (layer(q), s, 0, g))

    def item_rows(cols):
        return pl.BlockSpec((None, None, GC, cols), lambda q, s, g: (layer(q), s, g, 0))

    def layer_cols(rows):
        return pl.BlockSpec((None, rows, GC), lambda q, s, g: (layer(q), 0, g))

    def layer_all(*shape):
        zeros = (0,) * len(shape)
        return pl.BlockSpec((None,) + shape, lambda q, s, g: (layer(q),) + zeros)

    return item, item_cols, item_rows, layer_cols, layer_all


def forward_call(tokens, mask, w, par, count, head_dim):
    micro, rows, model = tokens.shape
    width, states = w.value.shape[2], w.state.shape[2]
    state = states // 2
    groups = width // GC
    item, item_cols, item_rows, layer_cols, layer_all = fused_specs(False)
    slots = 2 * micro
    dma = pltpu.SemaphoreType.DMA
    vmem = pltpu.VMEM
    ins = [
        (tokens, all_of(tokens.shape, 1)),
        (mask, all_of(mask.shape, 1)),
        (w.value, layer_cols(model)),
        (w.gate, layer_cols(model)),
        (w.out, layer_cols(model)),
        (w.state, layer_all(model, states)),
        (w.step, layer_all(model, LANES)),
        (par.value, layer_cols(8)),
        (par.state, layer_all(8, states)),
        (par.head, layer_all(8, LANES)),
        (par.norm, layer_all(8, model)),
    ]
    anywhere = pl.BlockSpec(memory_space=pl.ANY)
    pair = (2, micro)
    outs = [
        (((micro, rows, model), BF), anywhere),
        (((micro, rows, model), BF), anywhere),
        (((slots, rows, model), BF), anywhere),
        (((slots, rows, LANES), F32), all_of((slots, rows, LANES))),
        ((pair + (rows, model), BF), item(rows, model)),
        ((pair + (rows + HALO, width), F32), item_cols(rows + HALO)),
        ((pair + (rows + HALO, states), F32), item(rows + HALO, states)),
        ((pair + (rows, width), BF), item_cols(rows)),
        ((pair + (rows, states), BF), item(rows, states)),
        ((pair + (3, rows, LANES), F32), item(3, rows, LANES)),
        ((pair + (rows, width), F32), item_cols(rows)),
        ((pair + (rows, width), F32), item_cols(rows)),
        ((pair + (rows, width), BF), item_cols(rows)),
        ((pair + (width, state), BF), item_rows(state)),
    ]
    lanes = vmem((groups, rows, LANES), F32)
    scratch = [
        vmem((rows + HALO, model), BF),
        vmem((rows, rows), F32),
        lanes,
        lanes,
        vmem((groups, 8, rows), F32),
        vmem((rows, model), F32),
        vmem((rows, LANES), F32),
        vmem((slots, rows, model), BF),
        vmem((slots, rows, model), BF),
        vmem((slots, rows, LANES), F32),
        vmem((slots, rows, LANES), F32),
        vmem((slots * groups, GC, state), BF),
        vmem((slots * groups, GC, state), BF),
        vmem((micro, HALO, model), BF),
        vmem((micro, HALO, model), BF),
        dma((slots,)),
        dma((slots,)),
        dma((slots,)),
        dma((slots,)),
        dma((slots * groups,)),
        dma((slots * groups,)),
        dma((micro,)),
        dma((micro,)),
        dma((1,)),
        dma((1,)),
        dma((micro,)),
        dma((slots,)),
        dma((slots,)),
    ]
    kernel = functools.partial(fused_forward, count, head_dim, micro)
    flops = slots * (6 * rows * model * width + 6 * rows * rows * width)
    options = fused_options(pair + (groups,), ins, outs, scratch, 2, flops, 60 * slots * rows * width)
    return pl.pallas_call(kernel, **options)(*[array for array, _ in ins])


def fused_options(grid, ins, outs, scratch, collective, flops, traffic):
    return dict(
        grid=grid,
        in_specs=[spec for _, spec in ins],
        out_specs=[spec for _, spec in outs],
        out_shape=[jax.ShapeDtypeStruct(*kind) for kind, _ in outs],
        scratch_shapes=scratch,
        cost_estimate=pl.CostEstimate(flops=flops, bytes_accessed=traffic, transcendentals=0),
        compiler_params=pltpu.CompilerParams(
            collective_id=collective,
            has_side_effects=True,
            vmem_limit_bytes=VMEM_LIMIT,
            dimension_semantics=(SEQUENTIAL,) * len(grid),
        ),
    )


def backward_fused_call(cot, tokens, out0, mask, kept, w, par, count, head_dim):
    micro, rows, model = tokens.shape
    width, states = w.value.shape[2], w.state.shape[2]
    state = states // 2
    groups = width // GC
    item, item_cols, item_rows, layer_cols, layer_all = fused_specs(True)
    slots = 2 * micro
    dma = pltpu.SemaphoreType.DMA
    vmem = pltpu.VMEM
    ins = [
        (cot, all_of(cot.shape, 1)),
        (tokens, all_of(tokens.shape, 1)),
        (out0, all_of(out0.shape, 1)),
        (mask, all_of(mask.shape, 1)),
        (kept.inv, item(rows, LANES)),
        (kept.mix, item(rows, model)),
        (kept.vpre, item_cols(rows + HALO)),
        (kept.spre, item(rows + HALO, states)),
        (kept.x, item_cols(rows)),
        (kept.bc, item(rows, states)),
        (kept.dtc, item(3, rows, LANES)),
        (kept.gate, item_cols(rows)),
        (kept.y, item_cols(rows)),
        (kept.s_in, item_rows(state)),
        (w.value, layer_cols(model)),
        (w.gate, layer_cols(model)),
        (w.out, layer_cols(model)),
        (w.state, layer_all(model, states)),
        (w.step, layer_all(model, LANES)),
        (par.value, layer_cols(8)),
        (par.state, layer_all(8, states)),
        (par.head, layer_all(8, LANES)),
        (par.norm, all_of(par.norm.shape, 1)),
    ]
    pair = (2, micro)
    outs = [
        (((micro, rows, model), BF), pl.BlockSpec(memory_space=pl.ANY)),
        ((pair + (rows, width), BF), item_cols(rows)),
        ((pair + (rows, width), BF), item_cols(rows)),
        ((pair + (rows, states), BF), item(rows, states)),
        ((pair + (rows, LANES), BF), item(rows, LANES)),
        ((pair + (rows, model), BF), item(rows, model)),
        ((pair + (8, width), F32), item_cols(8)),
        ((pair + (8, states), F32), item(8, states)),
        ((pair + (8, LANES), F32), item(8, LANES)),
        (((2, 8, model), F32), all_of((2, 8, model))),
    ]
    lanes = vmem((groups, rows, LANES), F32)
    square = vmem((rows, rows), F32)
    scratch = [
        vmem((rows, model), BF),
        vmem((rows, LANES), F32),
        vmem((GC, state), BF),
        vmem((8, GC), F32),
        vmem((8, states), F32),
        vmem((rows, model), F32),
        vmem((2, 8, model), F32),
        square,
        square,
        square,
        vmem((rows, states), F32),
        lanes,
        lanes,
        vmem((groups, 8, rows), F32),
        lanes,
        lanes,
        lanes,
        vmem((groups, 8, LANES), F32),
        vmem((groups, 8, rows), F32),
        vmem((LANES, rows), F32),
        vmem((slots, rows, model), BF),
        vmem((slots, rows, model), BF),
        vmem((slots * groups, GC, state), BF),
        vmem((slots * groups, GC, state), BF),
        vmem((slots * groups, 8, GC), F32),
        vmem((slots * groups, 8, GC), F32),
        vmem((slots, 8, states), F32),
        vmem((slots, 8, states), F32),
        dma((slots,)),
        dma((slots,)),
        dma((slots * groups,)),
        dma((slots * groups,)),
        dma((slots * groups,)),
        dma((slots * groups,)),
        dma((slots,)),
        dma((slots,)),
        dma((slots,)),
    ]
    kernel = functools.partial(fused_backward, count, head_dim, micro)
    flops = slots * (8 * rows * model * width + 16 * rows * rows * width)
    options = fused_options(pair + (groups,), ins, outs, scratch, 3, flops, 60 * slots * rows * width)
    return pl.pallas_call(kernel, **options)(*[array for array, _ in ins])


def fused_body(
    tokens_in,
    cotangent,
    lengths,
    in_gate,
    in_value,
    in_state,
    in_step,
    out_proj,
    norm_gain,
    conv_value,
    conv_state,
    bias_value,
    bias_state,
    step_bias,
    decay_log,
    skip_gain,
    gate_gain,
):
    layer, group, block = lax.axis_index(PIPE), lax.axis_index(DP), lax.axis_index(TENSOR)
    blocks, groups = lax.axis_size(TENSOR), lax.axis_size(DP)
    first_half = layer == 0
    micro, rows, model = tokens_in.shape
    shard_rows = in_value.shape[1]
    half = in_value.shape[2] // 2
    heads = step_bias.shape[1] // 2
    head_dim = half // heads
    width = half * blocks
    all_heads = heads * blocks
    states = in_state.shape[2]

    place = jnp.arange(2 * LANES)[None, :]
    head = jnp.arange(2 * heads)[:, None]
    step_lanes = (place == head // heads * LANES + lax.rem(head, heads)).astype(BF)
    per_head = jnp.pad(jnp.concatenate([step_bias, decay_log], axis=1), ((0, 0), (0, 2 * half - 4 * heads)))
    skip = jnp.repeat(skip_gain, head_dim, axis=1)
    channel = jnp.concatenate([conv_value[0], bias_value, gate_gain, skip, per_head], axis=0)
    shared = jnp.concatenate([norm_gain[0], conv_state[0].reshape(-1), bias_state[0]], axis=0)
    shared = jnp.pad(shared, (0, -shared.shape[0] % (8 * LANES))).reshape(-1, LANES)
    wv, wg, wo, wt, ws, channel, shared = gather_call(
        in_value[0],
        in_gate[0],
        out_proj[0],
        nn(in_step[0], step_lanes).astype(BF),
        in_state[0],
        channel,
        shared,
        blocks,
        groups,
    )
    place = jnp.arange(blocks * LANES)[:, None]
    packed = lax.rem(place, LANES) + heads * (place // LANES) == jnp.arange(LANES)[None, :]
    packed = (packed & (lax.rem(place, LANES) < heads)).astype(BF)
    step_w = nn(wt.reshape(2 * model, blocks * LANES), packed).astype(BF).reshape(2, model, LANES)
    per_head = channel[:, :, 7, : 4 * heads].reshape(2, blocks, 2, 2, heads)
    per_head = lax.dynamic_index_in_dim(per_head, layer, 3, keepdims=False)
    head_par = per_head.transpose(0, 2, 1, 3).reshape(2, 2, all_heads)
    head_par = jnp.pad(head_par, ((0, 0), (0, 6), (0, LANES - all_heads)))
    channel = lax.dynamic_slice_in_dim(channel, layer * half, half, 3)
    value_par = channel.transpose(0, 2, 1, 3).reshape(2, 8, width)
    shared = shared.reshape(2, -1)
    state_par = jnp.pad(shared[:, model : model + 5 * states].reshape(2, 5, states), ((0, 0), (0, 3), (0, 0)))
    norm_par = jnp.broadcast_to(shared[:, None, :model], (2, 8, model))
    par = Bundle(value=value_par, head=head_par, state=state_par, norm=norm_par)
    w = Bundle(value=wv, gate=wg, out=wo, state=ws, step=step_w)

    valid = block * rows + jnp.arange(rows)[None, :] < lengths[:, None]
    mask = jnp.broadcast_to(valid.astype(F32)[:, :, None], (micro, rows, LANES))

    out, low_out, mix, inv, nx, vpre, spre, x, bc, dtc, gate, y, gg, s_in = forward_call(
        tokens_in, mask, w, par, blocks, head_dim
    )
    kept = Bundle(
        inv=inv.reshape(2, micro, rows, LANES),
        mix=mix.reshape(2, micro, rows, model),
        vpre=vpre,
        spre=spre,
        x=x,
        bc=bc,
        dtc=dtc,
        gate=gate,
        y=y,
        s_in=s_in,
    )
    grads, dval, dgate, dst, dstep, sgm, vsums, ssums, hsums, nsums = backward_fused_call(
        cotangent, tokens_in, low_out, mask, kept, w, par, blocks, head_dim
    )

    def long(value, q):
        return value[q].reshape(micro * rows, value.shape[3])

    lane = jnp.arange(LANES)[:, None]
    by_block = (8 * (lane // heads) + lax.rem(lane, heads) == jnp.arange(LANES)[None, :]) & (lane < all_heads)
    big, pack, turned = [], [], []
    for q in range(2):
        normed = long(nx, q)
        big += [
            tn(normed, long(dval, q)).astype(BF),
            tn(normed, long(dgate, q)).astype(BF),
            tn(long(sgm, q), long(gg, q)).astype(BF),
        ]
        turned.append(tn(long(dst, q), normed))
        step_lanes = nn(long(dstep, q), by_block.astype(BF)).astype(BF)
        step_grad = tn(step_lanes[:, : 8 * blocks], normed)
        ssum, hsum = jnp.sum(ssums[q], axis=0), jnp.sum(hsums[q], axis=0)
        rest = [
            nsums[q, 0][None],
            jnp.pad(ssum[:5].reshape(1, -1), ((0, 0), (0, width - 5 * states))),
            jnp.zeros((6, width), F32),
        ]
        hsum = hsum[:2, :all_heads].reshape(2, blocks, heads).transpose(1, 0, 2).reshape(blocks, 2 * heads)
        hsum = jnp.pad(hsum, ((0, 0), (0, half - 2 * heads))).reshape(1, width)
        pack.append(jnp.concatenate([jnp.sum(vsums[q], axis=0)[:7], hsum, step_grad] + rest, axis=0))
    turned = lax.psum_scatter(
        jnp.concatenate(turned, axis=0), (PIPE, DP, TENSOR), scatter_dimension=0, tiled=True
    )
    grad_value, grad_gate, grad_out, chan, step_grad, rest = reduce_call(big, jnp.stack(pack), blocks, groups)

    step_grad = step_grad.reshape(2, 8, shard_rows)[:, :heads].reshape(2 * heads, shard_rows).T
    grad_state = turned.T
    position = group * blocks + block
    ranks = groups * blocks

    def share(value):
        size = value.shape[-1] // ranks
        return lax.dynamic_slice_in_dim(value, position * size, size, value.ndim - 1)

    head_sums = chan[7].reshape(2, half)[:, : 2 * heads].reshape(2, 2, heads).transpose(1, 0, 2).reshape(2, -1)
    norm_sum = share(rest[0])
    conv_sum = share(rest[1, : 5 * states].reshape(5, states))
    return (
        out[None],
        grads[None],
        grad_gate[None],
        grad_value[None],
        grad_state[None],
        step_grad[None],
        grad_out[None],
        norm_sum[None],
        chan[None, :4],
        conv_sum[None, :4],
        chan[None, 4],
        conv_sum[None, 4],
        head_sums[None, 0],
        head_sums[None, 1],
        jnp.sum(chan[6].reshape(2 * heads, head_dim), axis=1)[None],
        chan[None, 5],
    )


def body(
    tokens_in,
    cotangent,
    lengths,
    in_gate,
    in_value,
    in_state,
    in_step,
    out_proj,
    norm_gain,
    conv_value,
    conv_state,
    bias_value,
    bias_state,
    step_bias,
    decay_log,
    skip_gain,
    gate_gain,
):
    layer = lax.axis_index(PIPE)
    block = lax.axis_index(TENSOR)
    blocks = lax.axis_size(TENSOR)
    group = lax.axis_index(DP)
    groups = lax.axis_size(DP)
    first_half = layer == 0
    micro, rows, model = tokens_in.shape
    shard_rows = in_value.shape[1]
    half = in_value.shape[2] // 2
    heads = step_bias.shape[1] // 2
    head_dim = half // heads
    width = half * blocks
    all_heads = heads * blocks
    states = in_state.shape[2]
    state = states // 2
    inner_total = 2 * width

    def halves(value):
        keep = lax.dynamic_slice_in_dim(value, layer * half_of(value), half_of(value), value.ndim - 1)
        send = lax.dynamic_slice_in_dim(value, (1 - layer) * half_of(value), half_of(value), value.ndim - 1)
        return by_layer(keep, swap_pipe(send))

    def half_of(value):
        return value.shape[-1] // 2

    def by_layer(own, other):
        return jnp.where(first_half, own, other), jnp.where(first_half, other, own)

    channel = jnp.concatenate([conv_value[0], bias_value, gate_gain], axis=0)
    channel_both = halves(channel)
    head_both = halves(jnp.concatenate([step_bias, decay_log, skip_gain], axis=0))
    flat_heads = [jnp.pad(v.reshape(1, 3 * heads), ((0, 0), (0, half - 3 * heads))) for v in head_both]
    packed = gather_tensor(jnp.concatenate(list(channel_both) + flat_heads + [jnp.zeros((2, half), F32)], axis=0))
    shared = jnp.concatenate([norm_gain[0], conv_state[0].reshape(-1), bias_state[0]], axis=0)
    shared_both = by_layer(shared, swap_pipe(shared))
    params = []
    for q in range(2):
        per_head = packed[12 + q].reshape(blocks, half)[:, : 3 * heads].reshape(blocks, 3, heads)
        per_head = per_head.transpose(1, 0, 2).reshape(3, all_heads)
        skip = jnp.repeat(per_head[2:3], head_dim, axis=1)
        value_par = jnp.concatenate([packed[6 * q : 6 * q + 6], skip, jnp.zeros((1, width), F32)], axis=0)
        head_par = jnp.pad(per_head, ((0, 5), (0, LANES - all_heads)))
        state_par = jnp.concatenate(
            [
                shared_both[q][model : model + 4 * states].reshape(4, states),
                shared_both[q][model + 4 * states :].reshape(1, states),
                jnp.zeros((3, states), F32),
            ],
            axis=0,
        )
        params.append(Bundle(value=value_par, head=head_par, state=state_par, norm=shared_both[q][:model]))

    step_both = halves(in_step[0])
    step_all = gather_tensor(jnp.concatenate(step_both, axis=1)).reshape(shard_rows, blocks, 2, heads)
    state_both = by_layer(in_state[0], swap_pipe(in_state[0]))
    value_both, gate_both, out_both = halves(in_value[0]), halves(in_gate[0]), halves(out_proj[0])
    weights = []
    for q in range(2):
        step_q = jnp.pad(step_all[:, :, q].reshape(shard_rows, all_heads), ((0, 0), (0, LANES - all_heads)))
        small = gather_dp(jnp.concatenate([state_both[q], step_q], axis=1))
        weights.append(
            Bundle(
                state=small[:, :states],
                step=small[:, states:],
                value=gather_dp(gather_tensor(value_both[q])),
                gate=gather_dp(gather_tensor(gate_both[q])),
                out=gather_dp(gather_tensor(out_both[q])),
            )
        )

    masks = [
        (block * rows + jnp.arange(rows) < lengths[s]).astype(F32)[:, None] for s in range(micro)
    ]

    def forward(u, s, q):
        w, par = weights[q], params[q]
        ext = jnp.concatenate([shift_tensor(u[-HALO:], 1), u], axis=0).astype(F32)
        root_inv = lax.rsqrt(jnp.mean(ext * ext, axis=1, keepdims=True) + EPS)
        nx = (ext * root_inv * par.norm[None, :]).astype(BF)
        vpre, spre, x, bc, dtc, yw, loc = front_call(nx, w, par, head_dim, state)
        through = jnp.repeat(jnp.exp(dtc[1, rows - 1, :all_heads]), head_dim)[:, None]
        s_in = jnp.zeros((width, state), BF)
        for k in range(1, blocks):
            sent = (through * s_in.astype(F32) + loc).astype(BF)
            got = lax.ppermute(sent, TENSOR, [(k - 1, k)])
            s_in = got if k == 1 else jnp.where(block == k, got, s_in)
        gate, y, gg, part, squares = finish_call(nx, w, par, yw, s_in, bc, dtc, head_dim)
        total = squares[:, 0]
        total = total + swap_pipe(total)
        inverse = lax.rsqrt(total / inner_total + EPS)[:, None]
        mixed = inverse * (part.astype(F32) + swap_pipe(part).astype(F32))
        result = (masks[s] * (u.astype(F32) + mixed)).astype(BF)
        kept = Bundle(
            u=u, nx=nx, root_inv=root_inv[HALO:], vpre=vpre, spre=spre, x=x, bc=bc, dtc=dtc, s_in=s_in, through=through,
            gate=gate, y=y, gg=gg, inverse=inverse, mixed=mixed,
        )
        return result, kept

    def backward(incoming, s, q, kept):
        w, par = weights[q], params[q]
        gm = (masks[s] * incoming.astype(F32)).astype(BF)
        gmf = gm.astype(F32)
        inverse = kept.inverse
        dot = jnp.sum(gmf * kept.mixed, axis=1, keepdims=True)
        shrink = inverse * inverse * dot / inner_total
        rowsc = jnp.concatenate([inverse, shrink, jnp.zeros((rows, LANES - 2), F32)], axis=1)
        dy, dgate, dsl, dgain = gate_call(gm, w, par, kept.y, kept.gate, rowsc, kept.bc, kept.dtc, head_dim)
        g_in = jnp.zeros((width, state), BF)
        for k in range(blocks - 2, -1, -1):
            sent = (kept.through * g_in.astype(F32) + dsl).astype(BF)
            got = lax.ppermute(sent, TENSOR, [(k + 1, k)])
            g_in = got if k == blocks - 2 else jnp.where(block == k, got, g_in)
        dconv, dsc, dstep, vsums, ssums, hsums = backward_call(
            dy, kept.x, kept.vpre, kept.spre, kept.bc, kept.dtc, kept.s_in, g_in, par, head_dim
        )
        halo = shift_tensor(jnp.concatenate([dconv[:8], dsc[:8]], axis=1), -1)
        dval, dst, part = conv_call(dconv, halo, dsc, dgate, dstep, w, par)
        grad_normed = part.astype(F32) + swap_pipe(part).astype(F32)
        uf, root_inv = kept.u.astype(F32), kept.root_inv
        grad_norm = jnp.sum(grad_normed * uf * root_inv, axis=0)
        weighted = grad_normed * par.norm[None, :]
        grad_u = root_inv * weighted - uf * root_inv**3 * jnp.mean(weighted * uf, axis=1, keepdims=True) + gmf
        scaled_gm = (gmf * inverse).astype(BF)
        channel_sums = jnp.concatenate([vsums[:5], dgain[:1], vsums[5:6]], axis=0)
        sums = (channel_sums, ssums[:5], hsums[:2, :all_heads], grad_norm)
        return grad_u.astype(BF), (dval, dgate, dst, dstep, scaled_gm), sums

    outs, kept = [], []
    current = [tokens_in[s] for s in range(micro)]
    for q in range(2):
        pairs = [forward(current[s], s, q) for s in range(micro)]
        current = [pair[0] for pair in pairs]
        outs.append(jnp.stack(current))
        kept.append([pair[1] for pair in pairs])

    grads = [None, None]
    reduced = [None, None]
    incoming = [cotangent[s] for s in range(micro)]
    for q in (1, 0):
        results = [backward(incoming[s], s, q, kept[q][s]) for s in range(micro)]
        incoming = [r[0] for r in results]
        grads[q] = jnp.stack(incoming)
        stacked = [jnp.concatenate([r[1][k] for r in results], axis=0) for k in range(5)]
        dval, dgate, dst, dstep, scaled_gm = stacked
        normed = jnp.concatenate([kept[q][s].nx[HALO:] for s in range(micro)], axis=0)
        gg = jnp.concatenate([kept[q][s].gg for s in range(micro)], axis=0)
        sums = [functools.reduce(jnp.add, [r[2][k] for r in results]) for k in range(4)]

        big = [tn(scaled_gm, gg).astype(BF), tn(normed, dgate).astype(BF), tn(normed, dval).astype(BF)]
        big = [reduce_tensor(take_cols(reduce_dp(v))) for v in big]
        turned = reduce_dp(tn(dst, normed).astype(BF))
        turned = reduce_tensor(take_first(turned.reshape(blocks, -1, model)))
        step_grad = tn(dstep, normed)[:all_heads]
        by_block = jnp.concatenate(
            [
                sums[0].reshape(7, blocks, half).transpose(1, 0, 2).reshape(blocks, -1),
                step_grad.reshape(blocks, -1),
                sums[2].reshape(2, blocks, heads).transpose(1, 0, 2).reshape(blocks, -1),
            ],
            axis=1,
        )
        per_block = reduce_tensor(take_first(sum_all_dp(by_block)))
        common = sum_all_tensor(sum_all_dp(jnp.concatenate([sums[1].reshape(-1), sums[3]], axis=0)))
        reduced[q] = (big, turned, per_block, common)

    def own_and_other(kind):
        return jnp.where(first_half, kind(0), kind(1)), jnp.where(first_half, kind(1), kind(0))

    def join(kind):
        own, other = own_and_other(kind)
        got = swap_pipe(other)
        return jnp.where(first_half, own, got), jnp.where(first_half, got, own)

    def columns(k):
        low, high = join(lambda q: reduced[q][0][k].astype(BF))
        return jnp.concatenate([low, high], axis=1).astype(F32)

    grad_out, grad_gate, grad_value = columns(0), columns(1), columns(2)
    own, other = own_and_other(lambda q: reduced[q][1])
    grad_state = (own + swap_pipe(other.astype(BF)).astype(F32)).T
    low, high = join(lambda q: reduced[q][2])
    cut1, cut2 = 7 * half, 7 * half + heads * model
    chan = jnp.concatenate([low[:cut1].reshape(7, half), high[:cut1].reshape(7, half)], axis=1)
    step_grad = jnp.concatenate([low[cut1:cut2].reshape(heads, model), high[cut1:cut2].reshape(heads, model)], axis=0)
    step_grad = lax.dynamic_slice_in_dim(step_grad, group * shard_rows, shard_rows, 1).T
    head_sums = jnp.concatenate([low[cut2:].reshape(2, heads), high[cut2:].reshape(2, heads)], axis=1)
    own, other = own_and_other(lambda q: reduced[q][3])
    conv_sum = own[: 5 * states] + swap_pipe(other[: 5 * states])
    norm_sum = own[5 * states :]
    position = group * blocks + block
    ranks = groups * blocks

    def share(value):
        size = value.shape[-1] // ranks
        return lax.dynamic_slice_in_dim(value, position * size, size, value.ndim - 1)

    conv_sum = share(conv_sum.reshape(5, states))
    return (
        jnp.where(first_half, outs[0], outs[1])[None],
        jnp.where(first_half, grads[0], grads[1])[None],
        grad_gate[None],
        grad_value[None],
        grad_state[None],
        step_grad[None],
        grad_out[None],
        share(norm_sum)[None],
        chan[None, :4],
        conv_sum[None, :4],
        chan[None, 4],
        conv_sum[None, 4],
        head_sums[None, 0],
        head_sums[None, 1],
        jnp.sum(chan[6].reshape(2 * heads, head_dim), axis=1)[None],
        chan[None, 5],
    )


def solution(mesh):
    in_specs = (
        P(DP, TENSOR, None),
        P(DP, TENSOR, None),
        P(DP),
        P(PIPE, DP, TENSOR),
        P(PIPE, DP, TENSOR),
        P(PIPE, DP, None),
        P(PIPE, DP, TENSOR),
        P(PIPE, DP, TENSOR),
        P(PIPE, None),
        P(PIPE, None, TENSOR),
        P(PIPE, None, None),
        P(PIPE, TENSOR),
        P(PIPE, None),
        P(PIPE, TENSOR),
        P(PIPE, TENSOR),
        P(PIPE, TENSOR),
        P(PIPE, TENSOR),
    )
    out_specs = (
        P(PIPE, DP, TENSOR, None),
        P(PIPE, DP, TENSOR, None),
        P(PIPE, DP, TENSOR),
        P(PIPE, DP, TENSOR),
        P(PIPE, None, (DP, TENSOR)),
        P(PIPE, DP, TENSOR),
        P(PIPE, DP, TENSOR),
        P(PIPE, (DP, TENSOR)),
        P(PIPE, None, TENSOR),
        P(PIPE, None, (DP, TENSOR)),
        P(PIPE, TENSOR),
        P(PIPE, (DP, TENSOR)),
        P(PIPE, TENSOR),
        P(PIPE, TENSOR),
        P(PIPE, TENSOR),
        P(PIPE, TENSOR),
    )

    def program(*args):
        columns = args[4].shape[2] // mesh.shape[TENSOR]
        fused = mesh.shape[DP] == 4 and mesh.shape[TENSOR] > 2 and columns // 2 % LANES == 0
        return mapped(fused_body if fused else body)(*args)

    def mapped(function):
        return jax.shard_map(function, mesh=mesh, in_specs=in_specs, out_specs=out_specs, check_vma=False)

    return program
```

time: 4060 us -> 904 us (0.22)
  local copies, waits for them, and re-layouts: 1400 us -> 35.5 us
  waiting for transfers between devices: 1290 us -> 0.02 us
  Pallas kernels: 0 us -> 775 us
  matrix products: 776 us -> 54.5 us
  other arithmetic: 373 us -> 7.5 us
  blocking collectives: 140 us -> 0 us
    dynamic_update_slice x160 -> x0, local copies, waits for them, and re-layouts: 900 us -> none  [ssd_scan(): lax.scan(jax.checkpoint(ssd_block), start_state, pieces)]
    pallas_call x0 -> x4, Pallas kernels: none -> 775 us  [the longest x1 214 us: reduce_call(): pl.pallas_call(functools.partial(reduce_grads, count), in_specs=[pl.Block...]
    reduce_scatter x21 -> x1, waiting for transfers between devices: 765 us -> 0.01 us  [fused_body(): lax.psum_scatter(jnp.concatenate(turned, axis=0), (PIPE, DP, TENSOR), sca...]
    dot_general x348 -> x14, matrix products: 776 us -> 54.5 us  [the longest x10 49 us: tn(): lax.dot_general(a, b, (((0,), (0,)), ((), ())), preferred_element_type=F32)]
    all_gather x11 -> x0, waiting for transfers between devices: 418 us -> none  [the longest x4 257 us: layer_forward(): full_normed = lax.all_gather(normed, 'tensor', axis=0, tiled=True)]
    another operation x244 -> x1, other arithmetic: 125 us -> 0.86 us  [fused_body(): jnp.stack(pack)]
    unnamed x680 -> x59, local copies, waits for them, and re-layouts: 132 us -> 10.4 us
    reduce_sum x61 -> x4, other arithmetic: 122 us -> 1.28 us  [the longest x1 0.64 us: fused_body(): jnp.sum(vsums[q], axis=0)[:7]]
  transfers between devices with their start and end apart: 43 -> 1, of which waited for: 32 -> 0; matrix products, arithmetic and copies ran while one was open for 23% -> 7% of each run, Pallas kernels for 0% -> 24%
where the time goes in v1:
time: 904 us; the launch traced here: 887 us
  Pallas kernels  775 us (86%)
  matrix products  54.5 us (6%)
  local copies, waits for them, and re-layouts  35.5 us (4%)
  between operations  14.7 us (2%)
    pallas_call x1, Pallas kernels, reduce_call(): pl.pallas_call(functools.partial(reduce_grads, count), in_specs=[pl.Block...  214 us
    pallas_call x1, Pallas kernels, backward_fused_call(): return pl.pallas_call(kernel, **options)(*[array for array, _ in ins])  211 us
    pallas_call x1, Pallas kernels, gather_call(): pl.pallas_call(functools.partial(gather_weights, count), in_specs=[pl.Blo...  200 us
    pallas_call x1, Pallas kernels, forward_call(): return pl.pallas_call(kernel, **options)(*[array for array, _ in ins])  149 us
    dot_general x10, matrix products, tn(): lax.dot_general(a, b, (((0,), (0,)), ((), ())), preferred_element_type=F32)  49 us
  transfers between devices with their start and end apart: 1, of which 0 were waited for; matrix products, arithmetic and copies ran while one was open for 7% of the time, Pallas kernels for 24%

profile of v1, /device:TPU:0, one launch (start us, length us, event | category | flops | bytes accessed | tf_op | source)
XLA Modules:
  0.0 886.8 jit_solution(15526396652325088546)
XLA Ops:
  8.8 0.9 fusion.22.refs_3_
  11.2 1.3 fusion.42.refs_6_
  12.5 1.4 concatenate.19.refs_5_
  13.8 200.1 %shard_map.291 = (bf16[2,1536,1536]{2,1,0:T(8,128)(2,1)}, bf16[2,1536,1536]{2,1,0:T(8,128)(2,1)}, bf16[2,1536,1536]{2,1,0:T(8,128)(2,1)}, bf16[2,1536,512]{2,1,0...) custom-call(bf16[384,768]{1,0:T(8,128)(2,1)} %bitcast.162, ...), custom_call_target="tpu_custom_call" | custom-call | tf_op jit(solution)/shard_map/pallas_call | solution.py:915
  215.5 1.5 constant_dynamic-slice_fusion.3
  219.2 3.9 convolution_convert_fusion
  223.8 0.9 broadcast_in_dim.56.refs_1_.refs_3_
  224.7 149.0 %shard_map.292 = (bf16[3,256,1536]{2,1,0:T(8,128)(2,1)}, bf16[3,256,1536]{2,1,0:T(8,128)(2,1)}, bf16[6,256,1536]{2,1,0:T(8,128)(2,1)}, f32[6,256,128]{2,1,0:T(8,...) custom-call(bf16[3,256,1536]{2,1,0:T(8,128)(2,1)} %refs_1_.1, ...), custom_call_target="tpu_custom_call" | custom-call | flops 25367150592 | bytes 141557760 | tf_op jit(solution)/shard_map/pallas_call | solution.py:1776
  373.7 211.2 %shard_map.293 = (bf16[3,256,1536]{2,1,0:T(8,128)(2,1)}, bf16[2,3,256,1536]{3,2,1,0:T(8,128)(2,1)}, bf16[2,3,256,1536]{3,2,1,0:T(8,128)(2,1)}, bf16[2,3,256,256]...) custom-call(bf16[3,256,1536]{2,1,0:T(8,128)(2,1)} %refs_0_.3, ...), custom_call_target="tpu_custom_call" | custom-call | flops 38654705664 | bytes 141557760 | tf_op jit(solution)/shard_map/pallas_call | solution.py:1887
  584.9 2.7 convolution_bitcast_fusion.1
  587.5 2.5 convolution_bitcast_fusion
  590.0 1.8 pad_maximum_fusion
  591.9 4.4 fusion.62
  596.4 9.1 %bitcast_convert_fusion.refs_5_ = bf16[1536,1536]{1,0:T(8,128)(2,1)} fusion(bf16[2,3,256,1536]{3,2,1,0:T(8,128)(2,1)} %get-tuple-element.77, bf16[2,3,256,1536]{3,2,1,0:T(8,128)(2,1)} %get-tuple-element.76), kind=kOutput, calls=%fused_computation | convolution fusion | flops 3626237952 | bytes 9437184 | tf_op jit(solution)/shard_map/dot_general | solution.py:32
  605.6 5.9 bitcast_convert_fusion.3.refs_2_
  612.4 1.4 slice_bitcast_fusion.4
  615.2 2.2 fusion.29
  618.0 1.6 concatenate.21
  619.6 1.5 concatenate.22
  621.9 9.2 %bitcast_convert_fusion.1.refs_4_ = bf16[1536,1536]{1,0:T(8,128)(2,1)} fusion(bf16[2,3,256,1536]{3,2,1,0:T(8,128)(2,1)} %get-tuple-element.75, bf16[2,3,256,1536]{3,2,1,0:T(8,128)(2,1)} %get-tuple-element.73), kind=kOutput, calls=%fused_computation.1 | convolution fusion | flops 3626237952 | bytes 9437184 | tf_op jit(solution)/shard_map/dot_general | solution.py:32
  631.1 5.7 bitcast_convert_fusion.4.refs_1_
  636.8 5.7 bitcast_convert_fusion.2.refs_3_
  642.4 5.7 bitcast_convert_fusion.5.refs_0_
  648.1 214.3 %shard_map.294 = (f32[384,768]{1,0:T(8,128)}, f32[384,768]{1,0:T(8,128)}, f32[384,768]{1,0:T(8,128)}, f32[8,768]{1,0:T(8,128)}, f32[16,384]{1,0:T(8,128)}, /*index=5*/f32[8,1536]{1,0:T(8,128)}) custom-call(bf16[1536,1536]{1,0:T(8,128)(2,1)} %bitcast_convert_fusion.5.refs_0_, bf16[1536,1536]{1,0:T(8,128)(2,1)} %bitcast_convert_fusion.4.refs_1_, ...), custom_call_target="tpu_custom_call" | custom-call | tf_op jit(solution)/shard_map/pallas_call | solution.py:1127
  866.0 1.5 slice_reduce_fusion.8
  870.7 1.3 slice_bitcast_fusion
  872.0 1.4 copy.83
  873.4 1.1 copy-done.3
  874.5 1.4 copy.84
  876.6 1.0 copy.85
  877.7 1.0 copy.86
  878.7 1.0 copy.87
  (118 shorter events, 18.5 us)
Async XLA Ops:
  7.2 1.6 copy-start
  7.2 864.8 %reduce-scatter.2.cloned.1.call-start = ((), (), s32[]{:S(2)}) async-start(), calls=%async_computation.1 | async-start | bytes 3244032 | tf_op jit(solution)/shard_map/reduce_scatter | solution.py:2003
  584.9 2.7 copy-start.7
  591.9 13.6 %slice-start.6 = ((s8[4718592]{0:T(1024)(128)(4,1)}), s8[4194304]{0:T(1024)(128)(4,1)S(1)}, s32[]{:S(2)}) async-start(s8[4718592]{0:T(1024)(128)(4,1)} %bitcast.196), calls=%async_computation.8 | async-start | bytes 8388608
  591.9 13.6 %slice-start.8 = ((s8[4718592]{0:T(1024)(128)(4,1)}), s8[4194304]{0:T(1024)(128)(4,1)S(1)}, s32[]{:S(2)}) async-start(s8[4718592]{0:T(1024)(128)(4,1)} %bitcast.198), calls=%async_computation.10 | async-start | bytes 8388608
  596.4 9.1 %slice-start.7 = ((s8[4718592]{0:T(1024)(128)(4,1)}), s8[524288]{0:T(1024)(128)(4,1)S(1)}, s32[]{:S(2)}) async-start(s8[4718592]{0:T(1024)(128)(4,1)} %bitcast.196), calls=%async_computation.9 | async-start | bytes 1048576
  596.4 9.1 %slice-start.9 = ((s8[4718592]{0:T(1024)(128)(4,1)}), s8[524288]{0:T(1024)(128)(4,1)S(1)}, s32[]{:S(2)}) async-start(s8[4718592]{0:T(1024)(128)(4,1)} %bitcast.198), calls=%async_computation.11 | async-start | bytes 1048576
  605.5 5.9 copy-start.8
  605.5 6.0 copy-start.10
  605.5 6.0 copy-start.9
  605.5 6.7 copy-start.11
  617.5 13.6 %slice-start = ((s8[4718592]{0:T(1024)(128)(4,1)}), s8[524288]{0:T(1024)(128)(4,1)S(1)}, s32[]{:S(2)}) async-start(s8[4718592]{0:T(1024)(128)(4,1)} %bitcast.146), calls=%async_computation.2 | async-start | bytes 1048576
  621.0 10.0 %slice-start.4 = ((s8[4718592]{0:T(1024)(128)(4,1)}), s8[4194304]{0:T(1024)(128)(4,1)S(1)}, s32[]{:S(2)}) async-start(s8[4718592]{0:T(1024)(128)(4,1)} %bitcast.194), calls=%async_computation.6 | async-start | bytes 8388608
  621.9 9.2 %slice-start.1 = ((s8[4718592]{0:T(1024)(128)(4,1)}), s8[4194304]{0:T(1024)(128)(4,1)S(1)}, s32[]{:S(2)}) async-start(s8[4718592]{0:T(1024)(128)(4,1)} %bitcast.146), calls=%async_computation.3 | async-start | bytes 8388608
  621.9 9.2 %slice-start.5 = ((s8[4718592]{0:T(1024)(128)(4,1)}), s8[524288]{0:T(1024)(128)(4,1)S(1)}, s32[]{:S(2)}) async-start(s8[4718592]{0:T(1024)(128)(4,1)} %bitcast.194), calls=%async_computation.7 | async-start | bytes 1048576
  621.9 14.9 %slice-start.2 = ((s8[4718592]{0:T(1024)(128)(4,1)}), s8[4194304]{0:T(1024)(128)(4,1)S(1)}, s32[]{:S(2)}) async-start(s8[4718592]{0:T(1024)(128)(4,1)} %bitcast.192), calls=%async_computation.4 | async-start | bytes 8388608
  631.1 5.7 slice-start.3
  648.1 223.9 %copy-start.2 = (bf16[3,256,1536]{2,1,0:T(8,128)(2,1)S(1)}, bf16[3,256,1536]{2,1,0:T(8,128)(2,1)}, u32[]{:S(2)}) copy-start(bf16[3,256,1536]{2,1,0:T(8,128)(2,1)} %get-tuple-element.60) | copy-start | bytes 7077892
  872.0 2.5 copy-start.3
  874.5 2.1 copy-start.6
  874.5 3.1 copy-start.5
  874.5 5.1 copy-start.1
  876.6 2.0 copy-start.4
Sparse Core Ops, SparseCore 0:
  592.0 100.2 reduce-scatter.1

commit v2 on v1

--- a/solution.py
+++ b/solution.py
@@ -706,226 +706,249 @@
     return pl.ds(pl.multiple_of(index * size, size), size)
 
 
-def gather_weights(count, *refs):
-    (value, gate, out, step, state, chan, shared, wv, wg, wo, wt, ws, ch, sh) = refs[:14]
-    (own_sem, xs_sem, xr_sem, right_sem, left_sem, zr_sem, ys_sem, yr_sem, cs_sem, cr_sem) = refs[14:24]
-    (st_own, st_xs, st_xr, st_ys, st_yr, st_cs, st_cr, ch_s, ch_r) = refs[24:]
-    p, d, t = lax.axis_index(PIPE), lax.axis_index(DP), lax.axis_index(TENSOR)
-    y, c = d // 2, lax.rem(d, 2)
-    y_mate, core_mate, far_mate = 2 * (1 - y) + c, 2 * y + 1 - c, 2 * (1 - y) + 1 - c
-    sources, targets = (value, gate, out, step), (wv, wg, wo, wt)
-    kinds = len(sources)
-    rows = value.shape[0]
-
-    def half(kind):
-        return sources[kind].shape[1] // 2
-
-    def region(item, row, col):
-        kind = item % kinds
-        return targets[kind].at[item // kinds, aligned(row, rows), aligned(col, half(kind))]
-
-    def strip(item, row):
-        return targets[item % kinds].at[item // kinds, aligned(row, rows), :]
-
-    def own_copy(w):
-        src = sources[w].at[:, aligned(p, half(w))]
-        return pltpu.make_async_copy(src, targets[w].at[p, aligned(d, rows), aligned(t, half(w))], own_sem.at[w])
-
-    def swap_copy(w):
-        src = sources[w].at[:, aligned(1 - p, half(w))]
-        dst = targets[w].at[p, aligned(d, rows), aligned(t, half(w))]
-        return remote(src, dst, xs_sem.at[w], xr_sem.at[w], PIPE, 1 - p)
-
-    def z_copy(item, src, by, sem):
-        ref = region(item, d, src)
-        return remote(ref, ref, sem.at[item, src], zr_sem.at[item, src], TENSOR, t + by)
-
-    def y_copy(item, src):
-        ref = region(item, d, src)
-        return remote(ref, ref, ys_sem.at[item, src], yr_sem.at[item, src], DP, y_mate)
-
-    def core_copy(item, which):
-        ref = strip(item, d if which == 0 else y_mate)
-        return remote(ref, ref, cs_sem.at[item, which], cr_sem.at[item, which], DP, core_mate)
-
-    def y_arrival(item, src):
-        ref = region(item, y_mate, src)
-        return remote(ref, ref, ys_sem.at[item, src], yr_sem.at[item, src], DP, y_mate)
-
-    def core_arrival(item, which):
-        ref = strip(item, core_mate if which == 0 else far_mate)
-        return remote(ref, ref, cs_sem.at[item, which], cr_sem.at[item, which], DP, core_mate)
-
-    def swap_arrival(w):
-        ref = targets[w].at[1 - p, aligned(d, rows), aligned(t, half(w))]
-        return remote(sources[w].at[:, aligned(1 - p, half(w))], ref, xs_sem.at[w], xr_sem.at[w], PIPE, 1 - p)
-
-    def state_rows(layer, row):
-        return ws.at[layer, aligned(row, rows), :]
-
-    small = ((state, state_rows(p, d), state_rows(1 - p, d)), (chan, ch.at[p, t], ch.at[1 - p, t]), (shared, sh.at[p], sh.at[1 - p]))
-
-    def small_own(k):
-        return pltpu.make_async_copy(small[k][0], small[k][1], st_own.at[k])
-
-    def small_swap(k):
-        return remote(small[k][0], small[k][1], st_xs.at[k], st_xr.at[k], PIPE, 1 - p)
-
-    def small_arrival(k):
-        return remote(small[k][0], small[k][2], st_xs.at[k], st_xr.at[k], PIPE, 1 - p)
-
-    def state_y(layer):
-        ref = state_rows(layer, d)
-        return remote(ref, ref, st_ys.at[layer], st_yr.at[layer], DP, y_mate)
-
-    def state_y_arrival(layer):
-        ref = state_rows(layer, y_mate)
-        return remote(ref, ref, st_ys.at[layer], st_yr.at[layer], DP, y_mate)
-
-    def state_core(layer, which):
-        ref = state_rows(layer, d if which == 0 else y_mate)
-        return remote(ref, ref, st_cs.at[layer, which], st_cr.at[layer, which], DP, core_mate)
-
-    def state_core_arrival(layer, which):
-        ref = state_rows(layer, core_mate if which == 0 else far_mate)
-        return remote(ref, ref, st_cs.at[layer, which], st_cr.at[layer, which], DP, core_mate)
-
-    def chan_copy(k):
-        ref = ch.at[:, t]
-        return remote(ref, ref, ch_s.at[k], ch_r.at[k], TENSOR, lax.rem(t + k, count))
-
-    def chan_arrival(k):
-        ref = ch.at[:, lax.rem(t - k + count, count)]
-        return remote(ref, ref, ch_s.at[k], ch_r.at[k], TENSOR, lax.rem(t + k, count))
-
-    def begin(item):
-        if item < kinds:
-            own_copy(item).wait()
-            swap_arrival(item).wait_recv()
-
-        @pl.when(t < count - 1)
-        def _():
-            z_copy(item, t, 1, right_sem).start()
-
-        @pl.when(t > 0)
-        def _():
-            z_copy(item, t, -1, left_sem).start()
-
-        y_copy(item, t).start()
-
-    def relay(item):
-        for hop in range(1, count):
-            lower, upper = t - hop, t + hop
-
-            @pl.when(lower >= 0)
+class Gather:
+    sems = ((4,), (4,), (4,), "z", "z", "z", "z", "z", "c", "c", (3,), (3,), (3,), (2,), (2,), (2, 2), (2, 2), "n", "n")
+
+    @classmethod
+    def scratch(cls, count):
+        shapes = {"z": (8, count), "c": (8, 2, count), "n": (count,)}
+        return [pltpu.SemaphoreType.DMA(shapes.get(shape, shape)) for shape in cls.sems]
+
+    def __init__(self, count, sources, targets, small, sems):
+        self.count, self.sources, self.targets, self.small = count, sources, targets, small
+        (self.own_sem, self.xs_sem, self.xr_sem, self.right_sem, self.left_sem, self.zr_sem) = sems[:6]
+        (self.ys_sem, self.yr_sem, self.cs_sem, self.cr_sem, self.st_own, self.st_xs, self.st_xr) = sems[6:13]
+        (self.st_ys, self.st_yr, self.st_cs, self.st_cr, self.ch_s, self.ch_r) = sems[13:]
+        self.p, self.d, self.t = lax.axis_index(PIPE), lax.axis_index(DP), lax.axis_index(TENSOR)
+        y, c = self.d // 2, lax.rem(self.d, 2)
+        self.y_mate, self.core_mate, self.far_mate = 2 * (1 - y) + c, 2 * y + 1 - c, 2 * (1 - y) + 1 - c
+        self.kinds = len(sources)
+        self.rows = sources[0].shape[0]
+
+    def partners(self):
+        others = [(TENSOR, lax.rem(self.t + k, self.count)) for k in range(1, self.count)]
+        return others + [(PIPE, 1 - self.p), (DP, self.y_mate), (DP, self.core_mate)]
+
+    def source(self, kind, which):
+        ref = self.sources[kind]
+        if kind == self.kinds - 1:
+            return ref.at[aligned(which, ref.shape[0] // 2), :]
+        return ref.at[:, aligned(which, ref.shape[1] // 2)]
+
+    def region(self, kind, layer, row, col):
+        ref = self.sources[kind]
+        if kind == self.kinds - 1:
+            return self.targets[kind].at[layer, aligned(col, ref.shape[0] // 2), aligned(row, ref.shape[1])]
+        return self.targets[kind].at[layer, aligned(row, self.rows), aligned(col, ref.shape[1] // 2)]
+
+    def own_copy(self, w):
+        return pltpu.make_async_copy(self.source(w, self.p), self.region(w, self.p, self.d, self.t), self.own_sem.at[w])
+
+    def swap_copy(self, w):
+        dst = self.region(w, self.p, self.d, self.t)
+        return remote(self.source(w, 1 - self.p), dst, self.xs_sem.at[w], self.xr_sem.at[w], PIPE, 1 - self.p)
+
+    def swap_arrival(self, w):
+        dst = self.region(w, 1 - self.p, self.d, self.t)
+        return remote(self.source(w, 1 - self.p), dst, self.xs_sem.at[w], self.xr_sem.at[w], PIPE, 1 - self.p)
+
+    def z_copy(self, item, src, by, sem):
+        ref = self.region(item % self.kinds, item // self.kinds, self.d, src)
+        return remote(ref, ref, sem.at[item, src], self.zr_sem.at[item, src], TENSOR, self.t + by)
+
+    def right(self, item, src):
+        return self.z_copy(item, src, 1, self.right_sem)
+
+    def left(self, item, src):
+        return self.z_copy(item, src, -1, self.left_sem)
+
+    def y_copy(self, item, src, row=None):
+        ref = self.region(item % self.kinds, item // self.kinds, self.d if row is None else row, src)
+        return remote(ref, ref, self.ys_sem.at[item, src], self.yr_sem.at[item, src], DP, self.y_mate)
+
+    def core_copy(self, item, which, src, arrival=False):
+        row = (self.core_mate, self.far_mate)[which] if arrival else (self.d, self.y_mate)[which]
+        ref = self.region(item % self.kinds, item // self.kinds, row, src)
+        sems = self.cs_sem.at[item, which, src], self.cr_sem.at[item, which, src]
+        return remote(ref, ref, *sems, DP, self.core_mate)
+
+    def begin(self, item):
+        w, layer = item % self.kinds, item // self.kinds
+
+        @pl.when(self.p == layer)
+        def _():
+            self.own_copy(w).wait()
+
+        @pl.when(self.p != layer)
+        def _():
+            self.swap_arrival(w).wait_recv()
+
+        @pl.when(self.t < self.count - 1)
+        def _():
+            self.right(item, self.t).start()
+
+        @pl.when(self.t > 0)
+        def _():
+            self.left(item, self.t).start()
+
+        self.y_copy(item, self.t).start()
+        self.core_copy(item, 0, self.t).start()
+
+    def hop(self, item, hop):
+        t, count = self.t, self.count
+        lower, upper = t - hop, t + hop
+
+        @pl.when(lower >= 0)
+        def _():
+            self.right(item, lower).wait_recv()
+
+            @pl.when(t < count - 1)
             def _():
-                z_copy(item, lower, 1, right_sem).wait_recv()
-
-                @pl.when(t < count - 1)
-                def _():
-                    z_copy(item, lower, 1, right_sem).start()
-
-                y_copy(item, lower).start()
-
-            @pl.when(upper < count)
+                self.right(item, lower).start()
+
+            self.y_copy(item, lower).start()
+            self.core_copy(item, 0, lower).start()
+
+        @pl.when(upper < count)
+        def _():
+            self.left(item, upper).wait_recv()
+
+            @pl.when(t > 0)
             def _():
-                z_copy(item, upper, -1, left_sem).wait_recv()
-
-                @pl.when(t > 0)
-                def _():
-                    z_copy(item, upper, -1, left_sem).start()
-
-                y_copy(item, upper).start()
-
-        core_copy(item, 0).start()
-
-    def share(item):
+                self.left(item, upper).start()
+
+            self.y_copy(item, upper).start()
+            self.core_copy(item, 0, upper).start()
+
+    def share(self, item, src):
+        self.y_copy(item, src, self.y_mate).wait_recv()
+        self.core_copy(item, 1, src).start()
+
+    def arrived(self, item, src):
+        for which in range(2):
+            self.core_copy(item, which, src, True).wait_recv()
+
+    def sent(self, item):
+        t, count = self.t, self.count
         for src in range(count):
-            y_arrival(item, src).wait_recv()
-        core_copy(item, 1).start()
-
-    others = [(TENSOR, lax.rem(t + k, count)) for k in range(1, count)]
-    greet(others + [(PIPE, 1 - p), (DP, y_mate), (DP, core_mate)])
-    for k in range(3):
-        small_swap(k).start()
-        small_own(k).start()
-    order = [kinds - 1] + list(range(kinds - 1))
-    for w in order:
-        swap_copy(w).start()
-        own_copy(w).start()
-    for k in range(3):
-        small_own(k).wait()
-        small_arrival(k).wait_recv()
-    for layer in range(2):
-        state_y(layer).start()
-        state_core(layer, 0).start()
-    for k in range(1, count):
-        chan_copy(k).start()
-    order = order + [kinds + w for w in order]
-    begin(order[0])
-    for n, item in enumerate(order):
-        if n + 1 < len(order):
-            begin(order[n + 1])
-        relay(item)
-        if n == 0:
-            for layer in range(2):
-                state_y_arrival(layer).wait_recv()
-                state_core(layer, 1).start()
-        else:
-            share(order[n - 1])
-    share(order[-1])
-    for k in range(3):
-        small_swap(k).wait_send()
-    for k in range(1, count):
-        chan_copy(k).wait_send()
-        chan_arrival(k).wait_recv()
-    for layer in range(2):
-        state_y(layer).wait_send()
-        for which in range(2):
-            state_core_arrival(layer, which).wait_recv()
-            state_core(layer, which).wait_send()
-    for w in range(kinds):
-        swap_copy(w).wait_send()
-    for item in order:
-        for which in range(2):
-            core_arrival(item, which).wait_recv()
-            core_copy(item, which).wait_send()
-        for src in range(count):
-            y_copy(item, src).wait_send()
+            for which in range(2):
+                self.core_copy(item, which, src).wait_send()
+            self.y_copy(item, src).wait_send()
 
             @pl.when((src <= t) & (t < count - 1))
             def _():
-                z_copy(item, src, 1, right_sem).wait_send()
+                self.right(item, src).wait_send()
 
             @pl.when((src >= t) & (t > 0))
             def _():
-                z_copy(item, src, -1, left_sem).wait_send()
-
-
-def gather_call(value, gate, out, step, state, chan, shared, count, groups):
-    rows = value.shape[0]
-    model = groups * rows
-    dma = pltpu.SemaphoreType.DMA
-    big = [jax.ShapeDtypeStruct((2, model, count * v.shape[1] // 2), BF) for v in (value, gate, out, step)]
-    shapes = big + [
-        jax.ShapeDtypeStruct((2, model, state.shape[1]), BF),
-        jax.ShapeDtypeStruct((2, count) + chan.shape, F32),
-        jax.ShapeDtypeStruct((2,) + shared.shape, F32),
-    ]
-    return pl.pallas_call(
-        functools.partial(gather_weights, count),
-        in_specs=[pl.BlockSpec(memory_space=pl.ANY)] * 7,
-        out_specs=[pl.BlockSpec(memory_space=pl.ANY)] * 7,
-        out_shape=shapes,
-        scratch_shapes=[dma((4,))] * 3
-        + [dma((8, count))] * 5
-        + [dma((8, 2))] * 2
-        + [dma((3,))] * 3
-        + [dma((2,))] * 2
-        + [dma((2, 2))] * 2
-        + [dma((count,))] * 2,
-        compiler_params=pltpu.CompilerParams(collective_id=0, has_side_effects=True),
-    )(value, gate, out, step, state, chan, shared)
+                self.left(item, src).wait_send()
+
+
+    def small_target(self, k, layer):
+        target = self.small[k][1]
+        if k == 0:
+            return target.at[layer, aligned(self.d, self.rows), :]
+        if k == 1:
+            return target.at[layer, :, aligned(self.t, target.shape[2] // self.count)]
+        return target.at[layer]
+
+    def small_source(self, k, which):
+        ref = self.small[k][0]
+        return ref.at[:, aligned(which, ref.shape[1] // 2)] if k == 1 else ref
+
+    def small_own(self, k):
+        return pltpu.make_async_copy(self.small_source(k, self.p), self.small_target(k, self.p), self.st_own.at[k])
+
+    def small_swap(self, k, arrival=False):
+        dst = self.small_target(k, 1 - self.p if arrival else self.p)
+        return remote(self.small_source(k, 1 - self.p), dst, self.st_xs.at[k], self.st_xr.at[k], PIPE, 1 - self.p)
+
+    def state_rows(self, layer, row):
+        return self.small[0][1].at[layer, aligned(row, self.rows), :]
+
+    def state_y(self, layer, arrival=False):
+        ref = self.state_rows(layer, self.y_mate if arrival else self.d)
+        return remote(ref, ref, self.st_ys.at[layer], self.st_yr.at[layer], DP, self.y_mate)
+
+    def state_core(self, layer, which, arrival=False):
+        row = (self.core_mate, self.far_mate)[which] if arrival else (self.d, self.y_mate)[which]
+        ref = self.state_rows(layer, row)
+        return remote(ref, ref, self.st_cs.at[layer, which], self.st_cr.at[layer, which], DP, self.core_mate)
+
+    def channels(self, k, arrival=False):
+        target = self.small[1][1]
+        index = lax.rem(self.t - k + self.count, self.count) if arrival else self.t
+        ref = target.at[:, :, aligned(index, target.shape[2] // self.count)]
+        return remote(ref, ref, self.ch_s.at[k], self.ch_r.at[k], TENSOR, lax.rem(self.t + k, self.count))
+
+    def first_layer(self):
+        order = [self.kinds - 1] + list(range(self.kinds - 1))
+        for w in order:
+            self.swap_copy(w).start()
+            self.own_copy(w).start()
+        for k in range(3):
+            self.small_swap(k).start()
+            self.small_own(k).start()
+        order = [self.kinds - 1, 2 * self.kinds - 1] + list(range(self.kinds - 1))
+        for item in order:
+            self.begin(item)
+        for k in range(3):
+            self.small_own(k).wait()
+            self.small_swap(k, True).wait_recv()
+        for layer in range(2):
+            self.state_y(layer).start()
+            self.state_core(layer, 0).start()
+        for k in range(1, self.count):
+            self.channels(k).start()
+        for hop in range(1, self.count):
+            for item in order:
+                self.hop(item, hop)
+        for item in self.late_items():
+            self.begin(item)
+        for layer in range(2):
+            self.state_y(layer, True).wait_recv()
+            self.state_core(layer, 1).start()
+        for src in range(self.count):
+            for item in order:
+                self.share(item, src)
+        for item in order:
+            for src in range(self.count):
+                self.arrived(item, src)
+        for k in range(1, self.count):
+            self.channels(k, True).wait_recv()
+        for layer in range(2):
+            for which in range(2):
+                self.state_core(layer, which, True).wait_recv()
+
+    def late_items(self):
+        return [self.kinds + w for w in range(self.kinds - 1)]
+
+    def second_layer(self, steps, group_of):
+        items, stages = self.late_items(), []
+        hops = [(item, hop) for hop in range(1, self.count) for item in items]
+        for n, (item, hop) in enumerate(hops):
+            stages.append((2 + n * (steps - 5) // len(hops), functools.partial(self.hop, item, hop)))
+        for src in range(self.count):
+            for item in items:
+                stages.append((steps - 2 + group_of(src), functools.partial(self.share, item, src)))
+        for src in range(self.count):
+            for item in items:
+                stages.append((steps - 1 + group_of(src), functools.partial(self.arrived, item, src)))
+        return stages
+
+    def finish(self):
+        for k in range(3):
+            self.small_swap(k).wait_send()
+        for k in range(1, self.count):
+            self.channels(k).wait_send()
+        for layer in range(2):
+            self.state_y(layer).wait_send()
+            for which in range(2):
+                self.state_core(layer, which).wait_send()
+        for w in range(self.kinds):
+            self.swap_copy(w).wait_send()
+        for item in range(2 * self.kinds):
+            self.sent(item)
 
 
 def add_into(dst, src, chunk=64):
@@ -1164,10 +1187,12 @@
 
 
 def fused_forward(count, head_dim, micro, *refs):
-    (tokens, mask, wv, wg, wo, ws, wt, pv, ps, ph, pn) = refs[:11]
-    (out_h, low_h, mix_h, inv_o, nx_o, vpre_o, spre_o, x_o, bc_o, dtc_o, gate_o, y_o, gg_o, sin_o) = refs[11:25]
-    (nx_s, sc_s, dt_s, cum_s, cumt_s, acc_s, sq_s, psend, precv, sqsend, sqrecv, csend, crecv, hrecv, trecv) = refs[25:40]
-    (ps_sem, pr_sem, ss_sem, sr_sem, cs_sem, cr_sem, hs_sem, hr_sem, ts_sem, tr_sem, low_sem, out_sem, mix_sem) = refs[40:]
+    (tokens, mask, value, gate_w, out_w, step_w, state_w, chan, shared) = refs[:9]
+    (wv_h, wg_h, wo_h, wt_h, ws_h, pv_o, ps_o, ph_o, pn_o) = refs[9:18]
+    (out_h, low_h, mix_h, inv_o, nx_o, vpre_o, spre_o, x_o, bc_o, dtc_o, gate_o, y_o, gg_o, sin_o) = refs[18:32]
+    (nx_s, sc_s, dt_s, cum_s, cumt_s, acc_s, sq_s, psend, precv, sqsend, sqrecv, csend, crecv, hrecv, trecv) = refs[32:47]
+    (ps_sem, pr_sem, ss_sem, sr_sem, cs_sem, cr_sem, hs_sem, hr_sem, ts_sem, tr_sem, low_sem, out_sem, mix_sem) = refs[47:60]
+    (wv_s, wg_s, wo_s, ws_s, wt_s, chan_s, shared_s, w_sem, l_sem) = refs[60:69]
     q, s, g = pl.program_id(0), pl.program_id(1), pl.program_id(2)
     groups = dt_s.shape[0]
     p, t = lax.axis_index(PIPE), lax.axis_index(TENSOR)
@@ -1178,6 +1203,25 @@
     state = bc_o.shape[1] // 2
     per_group = GC // head_dim
     inner_total = 2 * groups * GC
+    gather = Gather(
+        count,
+        (value, gate_w, out_w, step_w),
+        (wv_h, wg_h, wo_h, wt_h),
+        ((state_w, ws_h), (chan, chan_s), (shared, shared_s)),
+        refs[69:],
+    )
+    big = ((wv_h, wv_s), (wg_h, wg_s), (wo_h, wo_s))
+
+    def weight_copy(step, k):
+        layer, group = step // (micro * groups), lax.rem(step, groups)
+        held = lax.rem(step, 2)
+        return pltpu.make_async_copy(big[k][0].at[layer, :, aligned(group, GC)], big[k][1].at[held], w_sem.at[held, k])
+
+    def layer_copies(layer):
+        return (
+            pltpu.make_async_copy(ws_h.at[layer], ws_s, l_sem.at[0]),
+            pltpu.make_async_copy(wt_h.at[layer], wt_s, l_sem.at[1]),
+        )
 
     def part_copy(i):
         return remote(psend.at[i], precv.at[i], ps_sem.at[i], pr_sem.at[i], PIPE, 1 - p)
@@ -1205,11 +1249,60 @@
 
     @pl.when((idx == 0) & (g == 0))
     def _():
-        greet(ring_neighbours(count) + [(PIPE, 1 - p)])
+        greet(gather.partners())
 
         @pl.when(t < count - 1)
         def _():
             tokens_copy().start()
+
+        gather.first_layer()
+        for k in range(3):
+            weight_copy(0, k).start()
+        pv_o[...] = chan_s[...]
+        heads = per_group * groups // count
+        half = groups * GC // count
+        place, lane = iota((groups * GC, LANES), 0), iota((groups * GC, LANES), 1)
+        first = half * (lane // heads) + lax.rem(lane, heads)
+        used = lane < per_group * groups
+        for layer in range(2):
+            per_head = chan_s[layer]
+            for kind in range(2):
+                pick = ((place == first + kind * heads) & used).astype(F32)
+                ph_o[layer, kind : kind + 1, :] = exact(per_head, pick)[7:8, :]
+            ph_o[layer, 2:, :] = jnp.zeros((6, LANES), F32)
+            pn_o[layer] = shared_s[layer]
+            for k in range(5):
+                ps_o[layer, k : k + 1, :] = shared_s[layer, 1:2, 2 * state * k : 2 * state * (k + 1)]
+            ps_o[layer, 5:, :] = jnp.zeros((3, 2 * state), F32)
+
+    columns = groups * GC // count
+    late = gather.second_layer(micro * groups, lambda src: src * columns // GC)
+    for step in sorted({step for step, _ in late}):
+
+        @pl.when(slot == step)
+        def _():
+            for when, stage in late:
+                if when == step:
+                    stage()
+
+    @pl.when((s == 0) & (g == 0))
+    def _():
+        for copy in layer_copies(q):
+            copy.start()
+        for copy in layer_copies(q):
+            copy.wait()
+
+    for k in range(3):
+        weight_copy(slot, k).wait()
+
+    @pl.when(slot + 1 < total_idx * groups)
+    def _():
+        for k in range(3):
+            weight_copy(slot + 1, k).start()
+
+    held = lax.rem(slot, 2)
+    ws, wt, wv, wg, wo = ws_s, wt_s, wv_s.at[held], wg_s.at[held], wo_s.at[held]
+    pv, ps, ph, pn = pv_o.at[q, :, aligned(g, GC)], ps_o.at[q], ph_o.at[q], pn_o.at[q]
 
     def normed(u):
         uf = u.astype(F32)
@@ -1255,7 +1348,8 @@
         scores = nt(bc[:, state:], bc[:, :state])
         lower = iota((rows, rows), 0) >= iota((rows, rows), 1)
         sc_s[...] = jnp.where(lower, scores, 0.0)
-        raw = nn(nx_s[HALO:, :], wt[...]) + ph[0:1, :]
+        raw = nt(nx_s[HALO:, :], wt[...])
+        raw = exact(raw, step_places(count, raw.shape[1], per_group * groups)) + ph[0:1, :]
         step = jnp.maximum(raw, 0.0) + jnp.log(1.0 + jnp.exp(-jnp.abs(raw)))
         cum = exact(lower.astype(F32), -step * jnp.exp(ph[1:2, :]))
         dtc_o[0] = step
@@ -1371,6 +1465,8 @@
         for i in range(micro):
             low_copy(i).wait()
 
+        gather.finish()
+
         @pl.when(t < count - 1)
         def _():
             tokens_copy().wait_send()
@@ -1382,6 +1478,12 @@
                 return carry
 
             lax.fori_loop(0, total_idx * groups, drain, 0)
+
+
+def step_places(count, rows, all_heads):
+    heads, size = all_heads // count, rows // count
+    place, lane = iota((rows, LANES), 0), iota((rows, LANES), 1)
+    return ((place == size * (lane // heads) + lax.rem(lane, heads)) & (lane < all_heads)).astype(F32)
 
 
 def through_rows(cumt, rows, head_dim, state):
@@ -1611,7 +1713,7 @@
 
         dst = conv_transposed(dsc, halo2_s[...], ps, rows).astype(BF)
         dst_o[...] = dst
-        psend[idx] = (acc_s[...] + nt(dst, ws[...]) + nt(dstep_o[...], wt[...])).astype(BF)
+        psend[idx] = (acc_s[...] + nt(dst, ws[...]) + nn(dstep_o[...], wt[...])).astype(BF)
         part_copy(idx).start()
 
     def finish(i):
@@ -1699,31 +1801,40 @@
     return item, item_cols, item_rows, layer_cols, layer_all
 
 
-def forward_call(tokens, mask, w, par, count, head_dim):
+def forward_call(tokens, mask, shards, chan, shared, count, groups_dp, head_dim):
     micro, rows, model = tokens.shape
-    width, states = w.value.shape[2], w.state.shape[2]
-    state = states // 2
+    value, gate, out, step, state_w = shards
+    half, states = value.shape[1] // 2, state_w.shape[1]
+    width, state = half * count, states // 2
     groups = width // GC
     item, item_cols, item_rows, layer_cols, layer_all = fused_specs(False)
     slots = 2 * micro
     dma = pltpu.SemaphoreType.DMA
     vmem = pltpu.VMEM
+    anywhere = pl.BlockSpec(memory_space=pl.ANY)
     ins = [
         (tokens, all_of(tokens.shape, 1)),
         (mask, all_of(mask.shape, 1)),
-        (w.value, layer_cols(model)),
-        (w.gate, layer_cols(model)),
-        (w.out, layer_cols(model)),
-        (w.state, layer_all(model, states)),
-        (w.step, layer_all(model, LANES)),
-        (par.value, layer_cols(8)),
-        (par.state, layer_all(8, states)),
-        (par.head, layer_all(8, LANES)),
-        (par.norm, layer_all(8, model)),
+        (value, anywhere),
+        (gate, anywhere),
+        (out, anywhere),
+        (step, anywhere),
+        (state_w, anywhere),
+        (chan, anywhere),
+        (shared, anywhere),
     ]
-    anywhere = pl.BlockSpec(memory_space=pl.ANY)
     pair = (2, micro)
+    step_rows = step.shape[0] // 2 * count
     outs = [
+        (((2, model, width), BF), anywhere),
+        (((2, model, width), BF), anywhere),
+        (((2, model, width), BF), anywhere),
+        (((2, step_rows, model), BF), anywhere),
+        (((2, model, states), BF), anywhere),
+        (((2, 8, width), F32), all_of((2, 8, width))),
+        (((2, 8, states), F32), all_of((2, 8, states))),
+        (((2, 8, LANES), F32), all_of((2, 8, LANES))),
+        (((2,) + shared.shape, F32), all_of((2,) + shared.shape)),
         (((micro, rows, model), BF), anywhere),
         (((micro, rows, model), BF), anywhere),
         (((slots, rows, model), BF), anywhere),
@@ -1769,7 +1880,16 @@
         dma((micro,)),
         dma((slots,)),
         dma((slots,)),
-    ]
+        vmem((2, model, GC), BF),
+        vmem((2, model, GC), BF),
+        vmem((2, model, GC), BF),
+        vmem((model, states), BF),
+        vmem((step_rows, model), BF),
+        vmem((2, 8, width), F32),
+        vmem((2,) + shared.shape, F32),
+        dma((2, 3)),
+        dma((2,)),
+    ] + Gather.scratch(count)
     kernel = functools.partial(fused_forward, count, head_dim, micro)
     flops = slots * (6 * rows * model * width + 6 * rows * rows * width)
     options = fused_options(pair + (groups,), ins, outs, scratch, 2, flops, 60 * slots * rows * width)
@@ -1821,7 +1941,7 @@
         (w.gate, layer_cols(model)),
         (w.out, layer_cols(model)),
         (w.state, layer_all(model, states)),
-        (w.step, layer_all(model, LANES)),
+        (w.step, layer_all(LANES, model)),
         (par.value, layer_cols(8)),
         (par.state, layer_all(8, states)),
         (par.head, layer_all(8, LANES)),
@@ -1918,47 +2038,28 @@
     all_heads = heads * blocks
     states = in_state.shape[2]
 
-    place = jnp.arange(2 * LANES)[None, :]
-    head = jnp.arange(2 * heads)[:, None]
-    step_lanes = (place == head // heads * LANES + lax.rem(head, heads)).astype(BF)
-    per_head = jnp.pad(jnp.concatenate([step_bias, decay_log], axis=1), ((0, 0), (0, 2 * half - 4 * heads)))
+    row = jnp.arange(2 * HALO)[:, None]
+    head = jnp.arange(2 * heads)[None, :]
+    step_rows = (row == head // heads * HALO + lax.rem(head, heads)).astype(BF)
+    step_shard = nt(step_rows, in_step[0]).astype(BF)
+    both = jnp.concatenate([step_bias.reshape(2, heads), decay_log.reshape(2, heads)], axis=1)
+    per_head = jnp.pad(both, ((0, 0), (0, half - 2 * heads))).reshape(1, 2 * half)
     skip = jnp.repeat(skip_gain, head_dim, axis=1)
     channel = jnp.concatenate([conv_value[0], bias_value, gate_gain, skip, per_head], axis=0)
-    shared = jnp.concatenate([norm_gain[0], conv_state[0].reshape(-1), bias_state[0]], axis=0)
-    shared = jnp.pad(shared, (0, -shared.shape[0] % (8 * LANES))).reshape(-1, LANES)
-    wv, wg, wo, wt, ws, channel, shared = gather_call(
-        in_value[0],
-        in_gate[0],
-        out_proj[0],
-        nn(in_step[0], step_lanes).astype(BF),
-        in_state[0],
-        channel,
-        shared,
-        blocks,
-        groups,
-    )
-    place = jnp.arange(blocks * LANES)[:, None]
-    packed = lax.rem(place, LANES) + heads * (place // LANES) == jnp.arange(LANES)[None, :]
-    packed = (packed & (lax.rem(place, LANES) < heads)).astype(BF)
-    step_w = nn(wt.reshape(2 * model, blocks * LANES), packed).astype(BF).reshape(2, model, LANES)
-    per_head = channel[:, :, 7, : 4 * heads].reshape(2, blocks, 2, 2, heads)
-    per_head = lax.dynamic_index_in_dim(per_head, layer, 3, keepdims=False)
-    head_par = per_head.transpose(0, 2, 1, 3).reshape(2, 2, all_heads)
-    head_par = jnp.pad(head_par, ((0, 0), (0, 6), (0, LANES - all_heads)))
-    channel = lax.dynamic_slice_in_dim(channel, layer * half, half, 3)
-    value_par = channel.transpose(0, 2, 1, 3).reshape(2, 8, width)
-    shared = shared.reshape(2, -1)
-    state_par = jnp.pad(shared[:, model : model + 5 * states].reshape(2, 5, states), ((0, 0), (0, 3), (0, 0)))
-    norm_par = jnp.broadcast_to(shared[:, None, :model], (2, 8, model))
-    par = Bundle(value=value_par, head=head_par, state=state_par, norm=norm_par)
-    w = Bundle(value=wv, gate=wg, out=wo, state=ws, step=step_w)
+    state_row = jnp.concatenate([conv_state[0].reshape(1, -1), bias_state], axis=1)
+    shared = jnp.concatenate([norm_gain, jnp.pad(state_row, ((0, 6), (0, model - 5 * states))), norm_gain], axis=0)
 
     valid = block * rows + jnp.arange(rows)[None, :] < lengths[:, None]
     mask = jnp.broadcast_to(valid.astype(F32)[:, :, None], (micro, rows, LANES))
 
-    out, low_out, mix, inv, nx, vpre, spre, x, bc, dtc, gate, y, gg, s_in = forward_call(
-        tokens_in, mask, w, par, blocks, head_dim
+    shards = (in_value[0], in_gate[0], out_proj[0], step_shard, in_state[0])
+    (wv, wg, wo, wt, ws, pv, ps, ph, pn, out, low_out, mix, inv, nx, vpre, spre, x, bc, dtc, gate, y, gg, s_in) = forward_call(
+        tokens_in, mask, shards, channel, shared, blocks, groups, head_dim
     )
+    places = step_places(blocks, wt.shape[1], all_heads).astype(BF)
+    step_w = jnp.stack([tn(places, wt[q]).astype(BF) for q in range(2)])
+    w = Bundle(value=wv, gate=wg, out=wo, state=ws, step=step_w)
+    par = Bundle(value=pv, head=ph, state=ps, norm=pn)
     kept = Bundle(
         inv=inv.reshape(2, micro, rows, LANES),
         mix=mix.reshape(2, micro, rows, model),

time: 904 us -> 843 us (0.933)
  Pallas kernels: 775 us -> 722 us
    pallas_call x1 -> x0, Pallas kernels: 200 us -> none  [gather_call(): pl.pallas_call(functools.partial(gather_weights, count), in_specs=[pl.Blo...]
    pallas_call x1, Pallas kernels: 149 us -> 274 us  [forward_call(): return pl.pallas_call(kernel, **options)(*[array for array, _ in ins])]
    pallas_call x1, Pallas kernels: 211 us -> 230 us  [backward_fused_call(): return pl.pallas_call(kernel, **options)(*[array for array, _ in ins])]
    dot_general x10 -> x12, matrix products: 49 us -> 51.4 us  [tn(): lax.dot_general(a, b, (((0,), (0,)), ((), ())), preferred_element_type=F32)]
  transfers between devices with their start and end apart: 1 -> 1, of which waited for: 0 -> 0; matrix products, arithmetic and copies ran while one was open for 7% -> 8% of each run, Pallas kernels for 24% -> 26%
where the time goes in v2:
time: 843 us; the launch traced here: 831 us
  Pallas kernels  722 us (86%)
  matrix products  52.7 us (6%)
  local copies, waits for them, and re-layouts  31.2 us (4%)
  between operations  14.9 us (2%)
  other arithmetic  10.5 us (1%)
    pallas_call x1, Pallas kernels, forward_call(): return pl.pallas_call(kernel, **options)(*[array for array, _ in ins])  274 us
    pallas_call x1, Pallas kernels, backward_fused_call(): return pl.pallas_call(kernel, **options)(*[array for array, _ in ins])  230 us
    pallas_call x1, Pallas kernels, reduce_call(): pl.pallas_call(functools.partial(reduce_grads, count), in_specs=[pl.Block...  218 us
    dot_general x12, matrix products, tn(): lax.dot_general(a, b, (((0,), (0,)), ((), ())), preferred_element_type=F32)  51.4 us
  transfers between devices with their start and end apart: 1, of which 0 were waited for; matrix products, arithmetic and copies ran while one was open for 8% of the time, Pallas kernels for 26%

profile of v2, /device:TPU:0, one launch (start us, length us, event | category | flops | bytes accessed | tf_op | source)
XLA Modules:
  0.0 831.3 jit_solution(13991058206385946552)
XLA Ops:
  7.8 1.3 reduce.27
  9.2 1.3 reduce.26
  13.6 1.4 pad_maximum_fusion.3.refs_8_
  15.8 1.4 concatenate.22.refs_7_
  18.1 273.7 %shard_map.291 = (bf16[2,1536,1536]{2,1,0:T(8,128)(2,1)}, bf16[2,1536,1536]{2,1,0:T(8,128)(2,1)}, bf16[2,1536,1536]{2,1,0:T(8,128)(2,1)}, bf16[2,64,1536]{2,1,0:...) custom-call(bf16[3,256,1536]{2,1,0:T(8,128)(2,1)} %refs_1_.1, ...), custom_call_target="tpu_custom_call" | custom-call | flops 25367150592 | bytes 141557760 | tf_op jit(solution)/shard_map/pallas_call | solution.py:1896
  291.8 1.2 fusion.22
  293.0 1.2 fusion.23
  294.2 0.9 pad_maximum_fusion.1.refs_18_
  295.2 230.4 %shard_map.292 = (bf16[3,256,1536]{2,1,0:T(8,128)(2,1)}, bf16[2,3,256,1536]{3,2,1,0:T(8,128)(2,1)}, bf16[2,3,256,1536]{3,2,1,0:T(8,128)(2,1)}, bf16[2,3,256,256]...) custom-call(bf16[3,256,1536]{2,1,0:T(8,128)(2,1)} %refs_0_.3, ...), custom_call_target="tpu_custom_call" | custom-call | flops 38654705664 | bytes 141557760 | tf_op jit(solution)/shard_map/pallas_call | solution.py:2007
  525.6 2.7 convolution_bitcast_fusion.1
  528.2 2.5 convolution_bitcast_fusion
  530.7 1.8 pad_maximum_fusion
  532.6 4.5 fusion.57
  537.2 9.0 %bitcast_convert_fusion.refs_5_ = bf16[1536,1536]{1,0:T(8,128)(2,1)} fusion(bf16[2,3,256,1536]{3,2,1,0:T(8,128)(2,1)} %get-tuple-element.81, bf16[2,3,256,1536]{3,2,1,0:T(8,128)(2,1)} %get-tuple-element.80), kind=kOutput, calls=%fused_computation | convolution fusion | flops 3626237952 | bytes 9437184 | tf_op jit(solution)/shard_map/dot_general | solution.py:32
  546.2 6.0 bitcast_convert_fusion.3.refs_2_
  553.1 1.4 slice_bitcast_fusion.4
  556.0 2.2 fusion.28
  558.8 1.6 concatenate.25
  560.3 1.5 concatenate.26
  562.7 9.2 %bitcast_convert_fusion.1.refs_4_ = bf16[1536,1536]{1,0:T(8,128)(2,1)} fusion(bf16[2,3,256,1536]{3,2,1,0:T(8,128)(2,1)} %get-tuple-element.79, bf16[2,3,256,1536]{3,2,1,0:T(8,128)(2,1)} %get-tuple-element.77), kind=kOutput, calls=%fused_computation.1 | convolution fusion | flops 3626237952 | bytes 9437184 | tf_op jit(solution)/shard_map/dot_general | solution.py:32
  571.9 5.7 bitcast_convert_fusion.4.refs_1_
  577.5 5.7 bitcast_convert_fusion.2.refs_3_
  583.2 5.7 bitcast_convert_fusion.5.refs_0_
  588.9 217.9 %shard_map.293 = (f32[384,768]{1,0:T(8,128)}, f32[384,768]{1,0:T(8,128)}, f32[384,768]{1,0:T(8,128)}, f32[8,768]{1,0:T(8,128)}, f32[16,384]{1,0:T(8,128)}, /*index=5*/f32[8,1536]{1,0:T(8,128)}) custom-call(bf16[1536,1536]{1,0:T(8,128)(2,1)} %bitcast_convert_fusion.5.refs_0_, bf16[1536,1536]{1,0:T(8,128)(2,1)} %bitcast_convert_fusion.4.refs_1_, ...), custom_call_target="tpu_custom_call" | custom-call | tf_op jit(solution)/shard_map/pallas_call | solution.py:1150
  810.4 1.5 slice_reduce_fusion.7
  815.0 1.3 slice_bitcast_fusion
  816.4 1.4 copy.73
  817.8 1.1 copy-done.3
  818.9 1.4 copy.74
  821.0 1.0 copy.75
  822.0 1.0 copy.76
  823.0 1.0 copy.77
  (113 shorter events, 16.6 us)
Async XLA Ops:
  7.2 7.9 copy-start
  7.2 809.2 %reduce-scatter.2.cloned.1.call-start = ((), (), s32[]{:S(2)}) async-start(), calls=%async_computation.1 | async-start | bytes 3244032 | tf_op jit(solution)/shard_map/reduce_scatter | solution.py:2104
  525.6 2.7 copy-start.7
  532.6 13.5 %slice-start.6 = ((s8[4718592]{0:T(1024)(128)(4,1)}), s8[4194304]{0:T(1024)(128)(4,1)S(1)}, s32[]{:S(2)}) async-start(s8[4718592]{0:T(1024)(128)(4,1)} %bitcast.181), calls=%async_computation.8 | async-start | bytes 8388608
  532.6 13.5 %slice-start.8 = ((s8[4718592]{0:T(1024)(128)(4,1)}), s8[4194304]{0:T(1024)(128)(4,1)S(1)}, s32[]{:S(2)}) async-start(s8[4718592]{0:T(1024)(128)(4,1)} %bitcast.183), calls=%async_computation.10 | async-start | bytes 8388608
  537.2 9.0 %slice-start.7 = ((s8[4718592]{0:T(1024)(128)(4,1)}), s8[524288]{0:T(1024)(128)(4,1)S(1)}, s32[]{:S(2)}) async-start(s8[4718592]{0:T(1024)(128)(4,1)} %bitcast.181), calls=%async_computation.9 | async-start | bytes 1048576
  537.2 9.0 %slice-start.9 = ((s8[4718592]{0:T(1024)(128)(4,1)}), s8[524288]{0:T(1024)(128)(4,1)S(1)}, s32[]{:S(2)}) async-start(s8[4718592]{0:T(1024)(128)(4,1)} %bitcast.183), calls=%async_computation.11 | async-start | bytes 1048576
  546.2 6.0 copy-start.8
  546.2 6.0 copy-start.9
  546.2 6.7 copy-start.10
  546.2 6.7 copy-start.11
  558.2 13.6 %slice-start = ((s8[4718592]{0:T(1024)(128)(4,1)}), s8[524288]{0:T(1024)(128)(4,1)S(1)}, s32[]{:S(2)}) async-start(s8[4718592]{0:T(1024)(128)(4,1)} %bitcast.140), calls=%async_computation.2 | async-start | bytes 1048576
  561.8 10.0 %slice-start.4 = ((s8[4718592]{0:T(1024)(128)(4,1)}), s8[4194304]{0:T(1024)(128)(4,1)S(1)}, s32[]{:S(2)}) async-start(s8[4718592]{0:T(1024)(128)(4,1)} %bitcast.179), calls=%async_computation.6 | async-start | bytes 8388608
  562.6 9.2 %slice-start.1 = ((s8[4718592]{0:T(1024)(128)(4,1)}), s8[4194304]{0:T(1024)(128)(4,1)S(1)}, s32[]{:S(2)}) async-start(s8[4718592]{0:T(1024)(128)(4,1)} %bitcast.140), calls=%async_computation.3 | async-start | bytes 8388608
  562.6 9.2 %slice-start.5 = ((s8[4718592]{0:T(1024)(128)(4,1)}), s8[524288]{0:T(1024)(128)(4,1)S(1)}, s32[]{:S(2)}) async-start(s8[4718592]{0:T(1024)(128)(4,1)} %bitcast.179), calls=%async_computation.7 | async-start | bytes 1048576
  562.7 14.9 %slice-start.2 = ((s8[4718592]{0:T(1024)(128)(4,1)}), s8[4194304]{0:T(1024)(128)(4,1)S(1)}, s32[]{:S(2)}) async-start(s8[4718592]{0:T(1024)(128)(4,1)} %bitcast.177), calls=%async_computation.4 | async-start | bytes 8388608
  571.8 5.7 slice-start.3
  588.9 227.5 %copy-start.2 = (bf16[3,256,1536]{2,1,0:T(8,128)(2,1)S(1)}, bf16[3,256,1536]{2,1,0:T(8,128)(2,1)}, u32[]{:S(2)}) copy-start(bf16[3,256,1536]{2,1,0:T(8,128)(2,1)} %get-tuple-element.55) | copy-start | bytes 7077892
  816.4 2.5 copy-start.3
  818.9 2.1 copy-start.6
  818.9 3.1 copy-start.5
  818.9 5.1 copy-start.1
  821.0 2.0 copy-start.4
Sparse Core Ops, SparseCore 0:
  532.7 100.9 reduce-scatter.1

commit v3 on v2

--- a/solution.py
+++ b/solution.py
@@ -951,239 +951,340 @@
             self.sent(item)
 
 
-def add_into(dst, src, chunk=64):
+class Reducer:
+    def __init__(self, count, factors, results, buffers, sems):
+        self.count, self.factors, self.results = count, factors, results
+        (self.a_s, self.b_s, self.dw_s, self.crecv, self.ysend, self.near_s, self.yrecv, self.total_s) = buffers[:8]
+        (self.z_s, self.zl_s, self.xsend, self.xrecv, self.turned_s) = buffers[8:]
+        (self.a_sem, self.b_sem, self.cs_sem, self.cr_sem, self.ys_sem, self.yr_sem) = sems[:6]
+        (self.rs_sem, self.rr_sem, self.ls_sem, self.lr_sem, self.xs_sem, self.xr_sem, self.o_sem) = sems[6:]
+        self.p, self.d, self.t = lax.axis_index(PIPE), lax.axis_index(DP), lax.axis_index(TENSOR)
+        self.y, self.c = self.d // 2, lax.rem(self.d, 2)
+        self.y_mate, self.core_mate = 2 * (1 - self.y) + self.c, 2 * self.y + 1 - self.c
+        self.kinds = 3
+        self.pieces = 2 * self.kinds * count
+        self.ticks = self.pieces + count + 3
+        self.rows, self.half = self.xsend.shape[1], self.xsend.shape[2]
+
+    @staticmethod
+    def scratch(count, micro, rows, model, half, groups):
+        piece = (model // groups, half)
+        vmem, dma = pltpu.VMEM, pltpu.SemaphoreType.DMA
+        buffers = [
+            vmem((micro, rows, model), BF),
+            vmem((2, micro, rows, half), BF),
+            vmem((3, model, half), BF),
+            vmem((4, 2) + piece, BF),
+            vmem((4,) + piece, BF),
+            vmem((4,) + piece, BF),
+            vmem((4,) + piece, BF),
+            vmem((4,) + piece, BF),
+            vmem((6 * count,) + piece, BF),
+            vmem((6,) + piece, BF),
+            vmem((6,) + piece, BF),
+            vmem((3,) + piece, BF),
+            vmem((model, micro * rows), BF),
+        ]
+        sems = [dma((1,)), dma((2,)), dma((3, 2)), dma((4, 2)), dma((4,)), dma((4,))]
+        sems += [dma((6 * count,)) for _ in range(4)] + [dma((6,)), dma((3,)), dma((3, 2))]
+        return buffers, sems
+
+    def partners(self):
+        return ring_neighbours(self.count) + [(PIPE, 1 - self.p), (DP, self.y_mate), (DP, self.core_mate)]
+
+    def layer_of(self, m):
+        return m // (self.kinds * self.count)
+
+    def a_copy(self, which):
+        return pltpu.make_async_copy(self.factors[which % 2].at[which // 2], self.a_s, self.a_sem.at[0])
+
+    def b_copy(self, m, w):
+        src = self.factors[2 + w].at[self.layer_of(m), :, :, aligned(lax.rem(m, self.count), self.half)]
+        held = lax.rem(m, 2)
+        return pltpu.make_async_copy(src, self.b_s.at[held], self.b_sem.at[held])
+
+    def b_start(self, m):
+        for w in range(self.kinds):
+
+            @pl.when(lax.rem(m // self.count, self.kinds) == w)
+            def _():
+                self.b_copy(m, w).start()
+
+    def core_copy(self, m, row):
+        held, ring = lax.rem(m, 3), lax.rem(m, 4)
+        src = self.dw_s.at[held, aligned(2 * row + 1 - self.c, self.rows), :]
+        sems = self.cs_sem.at[held, row], self.cr_sem.at[ring, row]
+        return remote(src, self.crecv.at[ring, row], *sems, DP, self.core_mate)
+
+    def y_copy(self, m):
+        held = lax.rem(m, 4)
+        return remote(self.ysend.at[held], self.yrecv.at[held], self.ys_sem.at[held], self.yr_sem.at[held], DP, self.y_mate)
+
+    def right(self, m):
+        ref = self.z_s.at[m]
+        return remote(ref, ref, self.rs_sem.at[m], self.rr_sem.at[m], TENSOR, self.t + 1)
+
+    def left(self, m, last):
+        dst = self.zl_s.at[m // self.count] if last else self.z_s.at[m]
+        return remote(self.z_s.at[m], dst, self.ls_sem.at[m], self.lr_sem.at[m], TENSOR, self.t - 1)
+
+    def x_copy(self, item):
+        w = lax.rem(item, self.kinds)
+        return remote(self.xsend.at[item], self.xrecv.at[w], self.xs_sem.at[item], self.xr_sem.at[w], PIPE, 1 - self.p)
+
+    def when_valid(self, m, condition=None):
+        valid = (m >= 0) & (m < self.pieces)
+        return pl.when(valid if condition is None else valid & condition)
+
+    def tick(self, n):
+        count, t, rows = self.count, self.t, self.rows
+
+        @self.when_valid(n - 4)
+        def _():
+            m = n - 4
+            held = lax.rem(m, 4)
+            self.y_copy(m).wait()
+            add_to(self.total_s.at[held], self.near_s.at[held], self.yrecv.at[held])
+
+        @self.when_valid(n - 2)
+        def _():
+            m = n - 2
+            held, ring = lax.rem(m, 3), lax.rem(m, 4)
+            for row in range(2):
+                self.core_copy(m, row).wait()
+
+            def own(row):
+                return self.dw_s.at[held, aligned(2 * row + self.c, rows), :]
+
+            add_to(self.ysend.at[ring], own(1 - self.y), self.crecv.at[ring, 1 - self.y])
+            self.y_copy(m).start()
+            add_to(self.near_s.at[ring], own(self.y), self.crecv.at[ring, self.y])
+
+        def pass_on(m, first, arrival, send):
+            total = self.total_s.at[lax.rem(m, 4)]
+
+            @pl.when(first)
+            def _():
+                self.z_s[m] = total[...]
+
+            @pl.when(jnp.logical_not(first))
+            def _():
+                arrival.wait_recv()
+                add_to(self.z_s.at[m], self.z_s.at[m], total)
+
+            send()
+
+        to_right, to_left = n - 4 - t, n - 3 - count + t
+
+        @self.when_valid(to_right, t < lax.rem(to_right + count, count))
+        def _():
+            pass_on(to_right, t == 0, self.right(to_right), lambda: self.right(to_right).start())
+
+        @self.when_valid(to_left, t > lax.rem(to_left + count, count))
+        def _():
+            owner = lax.rem(to_left, count)
+
+            def send():
+                @pl.when(owner == t - 1)
+                def _():
+                    self.left(to_left, True).start()
+
+                @pl.when(owner != t - 1)
+                def _():
+                    self.left(to_left, False).start()
+
+            pass_on(to_left, t == count - 1, self.left(to_left, False), send)
+
+        done = n - 3 - count
+
+        @self.when_valid(done, t == lax.rem(done + count, count))
+        def _():
+            w = done // count
+            mine = self.xsend.at[w]
+            mine[...] = self.total_s[lax.rem(done, 4)]
+
+            @pl.when(t > 0)
+            def _():
+                self.right(done).wait_recv()
+                add_to(mine, mine, self.z_s.at[done])
+
+            @pl.when(t < count - 1)
+            def _():
+                self.left(done, True).wait_recv()
+                add_to(mine, mine, self.zl_s.at[w])
+
+            @pl.when(self.p != self.layer_of(done))
+            def _():
+                self.x_copy(w).start()
+
+        @self.when_valid(n)
+        def _():
+            @pl.when(n == 0)
+            def _():
+                self.a_copy(0).start()
+                self.b_start(n)
+
+            starts = [layer * self.kinds * count + 2 * count * which for layer in range(2) for which in range(2)]
+            for which, start in enumerate(starts):
+
+                @pl.when(n == start)
+                def _():
+                    self.a_copy(which).wait()
+                    micro, long, model = self.a_s.shape
+                    for row in range(model // rows):
+                        at = slice(rows * row, rows * (row + 1))
+                        self.turned_s[at, :] = self.a_s[:, :, at].reshape(micro * long, rows).T
+                    if which + 1 < len(starts):
+                        self.a_copy(which + 1).start()
+
+            @pl.when(n + 1 < self.pieces)
+            def _():
+                self.b_start(n + 1)
+
+            self.b_copy(n, 0).wait()
+            b = self.b_s[lax.rem(n, 2)]
+            b = b.reshape(b.shape[0] * b.shape[1], self.half)
+            held = lax.rem(n, 3)
+            for row in range(self.dw_s.shape[1] // rows):
+                at = slice(rows * row, rows * (row + 1))
+                self.dw_s[held, at, :] = nn(self.turned_s[at, :], b).astype(BF)
+            for row in range(2):
+                self.core_copy(n, row).start()
+
+    def result_copy(self, w, other):
+        src = self.xrecv.at[w] if other else self.xsend.at[self.kinds * self.p + w]
+        dst = self.results.at[w, :, aligned(1 - self.p if other else self.p, self.half)]
+        return pltpu.make_async_copy(src, dst, self.o_sem.at[w, int(other)])
+
+    def close(self):
+        count, t = self.count, self.t
+        for w in range(self.kinds):
+            self.result_copy(w, False).start()
+            self.x_copy(w).wait_recv()
+            self.result_copy(w, True).start()
+        for m in range(self.pieces):
+
+            @pl.when(t < m % count)
+            def _():
+                self.right(m).wait_send()
+
+            @pl.when(t > m % count)
+            def _():
+                self.left(m, False).wait_send()
+
+        for w in range(self.kinds):
+            self.x_copy(self.kinds * (1 - self.p) + w).wait_send()
+            for other in (False, True):
+                self.result_copy(w, other).wait()
+
+
+def add_to(dst, one, other, chunk=64):
     def step(i, carry):
         at = aligned(i, chunk)
-        dst[at, :] = (dst[at, :].astype(F32) + src[at, :].astype(F32)).astype(BF)
+        dst[at, :] = (one[at, :].astype(F32) + other[at, :].astype(F32)).astype(BF)
         return carry
 
     lax.fori_loop(0, dst.shape[0] // chunk, step, 0)
 
 
+class Sums:
+    def __init__(self, count, rows, half, pack, outs, buffers):
+        self.count, self.rows, self.half, self.pack, self.outs = count, rows, half, pack, outs
+        (self.total_s, self.part_s, self.far_s, self.ss, self.rs) = buffers
+        self.p, self.d, self.t = lax.axis_index(PIPE), lax.axis_index(DP), lax.axis_index(TENSOR)
+        y, c = self.d // 2, lax.rem(self.d, 2)
+        self.steps, bit = [(DP, 2 * y + 1 - c), (DP, 2 * (1 - y) + c)], 1
+        while bit < count:
+            self.steps.append((TENSOR, self.t + bit * (1 - 2 * lax.rem(self.t // bit, 2))))
+            bit *= 2
+
+    @staticmethod
+    def scratch(count, shape):
+        steps = 2 + (count - 1).bit_length()
+        vmem, dma = pltpu.VMEM, pltpu.SemaphoreType.DMA
+        return [vmem((steps + 1,) + shape, F32), vmem((steps,) + shape, F32), vmem(shape[1:], F32), dma((steps + 1,)), dma((steps + 1,))]
+
+    def partners(self):
+        return [step for step in self.steps if step[0] == TENSOR]
+
+    def copy(self, k):
+        axis, index = self.steps[k]
+        return remote(self.total_s.at[k], self.part_s.at[k], self.ss.at[k], self.rs.at[k], axis, index)
+
+    def pipe_copy(self):
+        k = len(self.steps)
+        return remote(self.total_s.at[k, 1 - self.p], self.far_s, self.ss.at[k], self.rs.at[k], PIPE, 1 - self.p)
+
+    def begin(self):
+        self.total_s[0] = self.pack[...]
+        self.copy(0).start()
+
+    def step(self, k):
+        self.copy(k).wait_recv()
+        self.total_s[k + 1] = self.total_s[k] + self.part_s[k]
+        if k + 1 < len(self.steps):
+            self.copy(k + 1).start()
+        else:
+            self.pipe_copy().start()
+
+    def close(self):
+        chan_o, step_o, rest_o = self.outs
+        k = len(self.steps)
+        self.pipe_copy().wait_recv()
+        mine, far, t = self.total_s.at[k, self.p], self.far_s, self.t
+        for ref, where in ((mine, self.p), (far, 1 - self.p)):
+            chan_o[:, aligned(where, self.half)] = ref[0:8, aligned(t, self.half)]
+            step_o[aligned(where, 8), :] = ref[pl.ds(pl.multiple_of(8 + 8 * t, 8), 8), aligned(self.d, self.rows)]
+        last = far.shape[0] - 8
+        row = iota((8, far.shape[1]), 0)
+        rest_o[...] = mine[last:, :] + jnp.where(row == 0, 0.0, far[last:, :])
+        for k in range(len(self.steps)):
+            self.copy(k).wait_send()
+        self.pipe_copy().wait_send()
+
+
 def reduce_grads(count, *refs):
-    grads, pack, results, (chan_o, step_o, rest_o) = refs[:6], refs[6], refs[7:10], refs[10:13]
-    (own, crecv, yrecv, rrecv, lrecv, xsend, xrecv) = refs[13:20]
-    (own_sem, cs_sem, cr_sem, ys_sem, yr_sem, rs_sem, rr_sem, ls_sem, lr_sem, xs_sem, xr_sem) = refs[20:31]
-    (total_s, part_s, far_s, sum_ss, sum_rs) = refs[31:]
-    p, d, t = lax.axis_index(PIPE), lax.axis_index(DP), lax.axis_index(TENSOR)
-    y, c = d // 2, lax.rem(d, 2)
-    y_mate, core_mate = 2 * (1 - y) + c, 2 * y + 1 - c
-    items, kinds = 6, 3
-    rows, half = xsend.shape[1], xsend.shape[2]
-
-    def core_copy(item, row):
-        src = grads[item].at[aligned(2 * row + 1 - c, rows), :]
-        return remote(src, crecv.at[item, row], cs_sem.at[item, row], cr_sem.at[item, row], DP, core_mate)
-
-    def own_copy(item, row):
-        src = grads[item].at[aligned(2 * row + c, rows), :]
-        return pltpu.make_async_copy(src, own.at[item % 2, row], own_sem.at[item % 2, row])
-
-    def y_copy(item):
-        return remote(crecv.at[item, 1 - y], yrecv.at[item], ys_sem.at[item], yr_sem.at[item], DP, y_mate)
-
-    def right_copy(item, j):
-        ref = rrecv.at[item, j]
-        return remote(ref, ref, rs_sem.at[item, j], rr_sem.at[item, j], TENSOR, t + 1)
-
-    def left_copy(item, j):
-        ref = lrecv.at[item, j]
-        return remote(ref, ref, ls_sem.at[item, j], lr_sem.at[item, j], TENSOR, t - 1)
-
-    def x_copy(item):
-        return remote(xsend.at[item], xrecv.at[item % kinds], xs_sem.at[item], xr_sem.at[item % kinds], PIPE, 1 - p)
-
-    def near(item):
-        for row in range(2):
-            own_copy(item, row).wait()
-            core_copy(item, row).wait_recv()
-            add_into(crecv.at[item, row], own.at[item % 2, row])
-        y_copy(item).start()
-        if item + 2 < items:
-            for row in range(2):
-                own_copy(item + 2, row).start()
-
-    def far(item):
-        y_copy(item).wait_recv()
-        add_into(yrecv.at[item], crecv.at[item, y])
-
-        def column(j):
-            return yrecv.at[item, :, aligned(j, half)]
-
-        for j in range(count - 1, 0, -1):
-
-            @pl.when(t < j)
+    factors, pack, results, sums_o = refs[:5], refs[5], refs[6], refs[7:10]
+    reducer = Reducer(count, factors, results, refs[10:23], refs[23:36])
+    sums = Sums(count, reducer.rows, reducer.half, pack, sums_o, refs[36:])
+    greet(reducer.partners() + sums.partners())
+    sums.begin()
+
+    def step(n, carry):
+        reducer.tick(n)
+        for k in range(len(sums.steps)):
+
+            @pl.when(n == 2 * k + 2)
             def _():
-                @pl.when(t == 0)
-                def _():
-                    rrecv[item, j] = column(j)[...]
-
-                @pl.when(t > 0)
-                def _():
-                    right_copy(item, j).wait_recv()
-                    add_into(rrecv.at[item, j], column(j))
-
-                right_copy(item, j).start()
-
-        for j in range(count - 1):
-
-            @pl.when(t > j)
-            def _():
-                @pl.when(t == count - 1)
-                def _():
-                    lrecv[item, j] = column(j)[...]
-
-                @pl.when(t < count - 1)
-                def _():
-                    left_copy(item, j).wait_recv()
-                    add_into(lrecv.at[item, j], column(j))
-
-                left_copy(item, j).start()
-
-    def close(item):
-        w = item % kinds
-        total = xsend.at[item]
-        total[...] = yrecv[item, :, aligned(t, half)]
-
-        @pl.when(t > 0)
-        def _():
-            right_copy(item, t).wait_recv()
-            add_into(total, rrecv.at[item, t])
-
-        @pl.when(t < count - 1)
-        def _():
-            left_copy(item, t).wait_recv()
-            add_into(total, lrecv.at[item, t])
-
-        @pl.when(p != item // kinds)
-        def _():
-            x_copy(item).start()
-
-        @pl.when(p == item // kinds)
-        def _():
-            results[w][:, aligned(p, half)] = total[...].astype(F32)
-
-    steps, bit = [(DP, core_mate), (DP, y_mate)], 1
-    while bit < count:
-        steps.append((TENSOR, t + bit * (1 - 2 * lax.rem(t // bit, 2))))
-        bit *= 2
-
-    def sum_copy(k):
-        axis, index = steps[k]
-        return remote(total_s.at[k], part_s.at[k], sum_ss.at[k], sum_rs.at[k], axis, index)
-
-    def pipe_copy():
-        k = len(steps)
-        return remote(total_s.at[k, 1 - p], far_s, sum_ss.at[k], sum_rs.at[k], PIPE, 1 - p)
-
-    def sum_step(k):
-        sum_copy(k).wait_recv()
-        total_s[k + 1] = total_s[k] + part_s[k]
-        if k + 1 < len(steps):
-            sum_copy(k + 1).start()
-        else:
-            pipe_copy().start()
-
-    def sum_close():
-        k = len(steps)
-        pipe_copy().wait_recv()
-        mine = total_s.at[k, p]
-        for ref, where in ((mine, p), (far_s, 1 - p)):
-            chan_o[:, aligned(where, half)] = ref[0:8, aligned(t, half)]
-            step_o[aligned(where, 8), :] = ref[pl.ds(pl.multiple_of(8 + 8 * t, 8), 8), aligned(d, rows)]
-        last = total_s.shape[2] - 8
-        row = iota((8, total_s.shape[3]), 0)
-        rest_o[...] = mine[last:, :] + jnp.where(row == 0, 0.0, far_s[last:, :])
-
-    others = [axis_index for axis_index in steps if axis_index[0] == TENSOR]
-    greet(ring_neighbours(count) + [(PIPE, 1 - p), (DP, y_mate), (DP, core_mate)] + others)
-    total_s[0] = pack[...]
-    sum_copy(0).start()
-    for item in range(items):
-        for row in range(2):
-            core_copy(item, row).start()
-            if item < 2:
-                own_copy(item, row).start()
-    for k in range(items + 2):
-        if k < items:
-            near(k)
-        if 1 <= k <= items:
-            far(k - 1)
-        if k >= 2:
-            close(k - 2)
-        if 1 <= k <= len(steps):
-            sum_step(k - 1)
-    sum_close()
-    for k in range(len(steps)):
-        sum_copy(k).wait_send()
-    pipe_copy().wait_send()
-    for w in range(kinds):
-        x_copy(w).wait_recv()
-        results[w][:, aligned(1 - p, half)] = xrecv[w].astype(F32)
-    for item in range(items):
-        for row in range(2):
-            core_copy(item, row).wait_send()
-        y_copy(item).wait_send()
-
-        @pl.when(p != item // kinds)
-        def _():
-            x_copy(item).wait_send()
-
-        for j in range(count):
-
-            @pl.when(t < j)
-            def _():
-                right_copy(item, j).wait_send()
-
-            @pl.when(t > j)
-            def _():
-                left_copy(item, j).wait_send()
-
-
-def reduce_call(grads, pack, count, groups):
-    model, width = grads[0].shape
-    rows, half = model // groups, width // count
-    dma = pltpu.SemaphoreType.DMA
-    vmem = pltpu.VMEM
-    steps = 2 + (count - 1).bit_length()
+                sums.step(k)
+
+        return carry
+
+    lax.fori_loop(0, reducer.ticks, step, 0)
+    sums.close()
+    reducer.close()
+
+
+def reduce_call(factors, pack, count, groups):
+    _, micro, rows, model = factors[0].shape
+    width = factors[2].shape[3]
+    half = width // count
+    buffers, sems = Reducer.scratch(count, micro, rows, model, half, groups)
     inside = pl.BlockSpec(memory_space=pltpu.VMEM)
+    anywhere = pl.BlockSpec(memory_space=pl.ANY)
     return pl.pallas_call(
         functools.partial(reduce_grads, count),
-        in_specs=[pl.BlockSpec(memory_space=pl.ANY)] * 6 + [inside],
-        out_specs=[inside] * 6,
-        out_shape=[jax.ShapeDtypeStruct((rows, 2 * half), F32)] * 3
-        + [
+        in_specs=[anywhere] * 5 + [inside],
+        out_specs=[anywhere] + [inside] * 3,
+        out_shape=[
+            jax.ShapeDtypeStruct((3, model // groups, 2 * half), BF),
             jax.ShapeDtypeStruct((8, 2 * half), F32),
-            jax.ShapeDtypeStruct((16, rows), F32),
+            jax.ShapeDtypeStruct((16, model // groups), F32),
             jax.ShapeDtypeStruct((8, width), F32),
         ],
-        scratch_shapes=[
-            vmem((2, 2, rows, width), BF),
-            vmem((6, 2, rows, width), BF),
-            vmem((6, rows, width), BF),
-            vmem((6, count, rows, half), BF),
-            vmem((6, count, rows, half), BF),
-            vmem((6, rows, half), BF),
-            vmem((3, rows, half), BF),
-            dma((2, 2)),
-            dma((6, 2)),
-            dma((6, 2)),
-            dma((6,)),
-            dma((6,)),
-            dma((6, count)),
-            dma((6, count)),
-            dma((6, count)),
-            dma((6, count)),
-            dma((6,)),
-            dma((3,)),
-            vmem((steps + 1,) + pack.shape, F32),
-            vmem((steps,) + pack.shape, F32),
-            vmem(pack.shape[1:], F32),
-            dma((steps + 1,)),
-            dma((steps + 1,)),
-        ],
+        scratch_shapes=buffers + sems + Sums.scratch(count, pack.shape),
         compiler_params=pltpu.CompilerParams(collective_id=1, has_side_effects=True, vmem_limit_bytes=VMEM_LIMIT),
-    )(*grads, pack)
+    )(*factors, pack)
 
 
 def fused_forward(count, head_dim, micro, *refs):
@@ -2081,14 +2182,9 @@
 
     lane = jnp.arange(LANES)[:, None]
     by_block = (8 * (lane // heads) + lax.rem(lane, heads) == jnp.arange(LANES)[None, :]) & (lane < all_heads)
-    big, pack, turned = [], [], []
+    pack, turned = [], []
     for q in range(2):
         normed = long(nx, q)
-        big += [
-            tn(normed, long(dval, q)).astype(BF),
-            tn(normed, long(dgate, q)).astype(BF),
-            tn(long(sgm, q), long(gg, q)).astype(BF),
-        ]
         turned.append(tn(long(dst, q), normed))
         step_lanes = nn(long(dstep, q), by_block.astype(BF)).astype(BF)
         step_grad = tn(step_lanes[:, : 8 * blocks], normed)
@@ -2104,7 +2200,10 @@
     turned = lax.psum_scatter(
         jnp.concatenate(turned, axis=0), (PIPE, DP, TENSOR), scatter_dimension=0, tiled=True
     )
-    grad_value, grad_gate, grad_out, chan, step_grad, rest = reduce_call(big, jnp.stack(pack), blocks, groups)
+    pack = jnp.stack(pack)
+    factors = (nx, sgm, dval, dgate, gg)
+    large, chan, step_grad, rest = reduce_call(factors, pack, blocks, groups)
+    grad_value, grad_gate, grad_out = [large[w].astype(F32) for w in range(3)]
 
     step_grad = step_grad.reshape(2, 8, shard_rows)[:, :heads].reshape(2 * heads, shard_rows).T
     grad_state = turned.T

time: 843 us -> 795 us (0.943)
  matrix products: 52.7 us -> 9.88 us
  local copies, waits for them, and re-layouts: 31.2 us -> 22.6 us
    dot_general x12 -> x6, matrix products: 51.4 us -> 8.59 us  [tn(): lax.dot_general(a, b, (((0,), (0,)), ((), ())), preferred_element_type=F32)]
  transfers between devices with their start and end apart: 1 -> 1, of which waited for: 0 -> 0; matrix products, arithmetic and copies ran while one was open for 8% -> 3% of each run, Pallas kernels for 26% -> 28%
where the time goes in v3:
time: 795 us; the launch traced here: 780 us
  Pallas kernels  720 us (91%)
  local copies, waits for them, and re-layouts  22.6 us (3%)
  between operations  14.4 us (2%)
  other arithmetic  13.4 us (2%)
  matrix products  9.88 us (1%)
    pallas_call x1, Pallas kernels, forward_call(): return pl.pallas_call(kernel, **options)(*[array for array, _ in ins])  274 us
    pallas_call x1, Pallas kernels, backward_fused_call(): return pl.pallas_call(kernel, **options)(*[array for array, _ in ins])  230 us
    pallas_call x1, Pallas kernels, reduce_call(): pl.pallas_call(functools.partial(reduce_grads, count), in_specs=[anywhere...  216 us
  transfers between devices with their start and end apart: 1, of which 0 were waited for; matrix products, arithmetic and copies ran while one was open for 3% of the time, Pallas kernels for 28%

profile of v3, /device:TPU:0, one launch (start us, length us, event | category | flops | bytes accessed | tf_op | source)
XLA Modules:
  0.0 779.9 jit_solution(3284210421284270715)
XLA Ops:
  7.8 1.3 reduce.27
  9.2 1.3 reduce.26
  10.7 0.7 broadcast_in_dim.21
  11.5 0.7 copy.45
  12.2 0.7 compare_convert_fusion
  12.9 0.7 select_maximum_fusion
  13.6 1.4 pad_maximum_fusion.3.refs_8_
  15.1 0.7 convolution_convert_fusion.2.refs_5_
  15.8 1.4 concatenate.22.refs_7_
  17.2 0.9 broadcast_in_dim.20.refs_1_.refs_3_
  18.1 273.6 %shard_map.291 = (bf16[2,1536,1536]{2,1,0:T(8,128)(2,1)}, bf16[2,1536,1536]{2,1,0:T(8,128)(2,1)}, bf16[2,1536,1536]{2,1,0:T(8,128)(2,1)}, bf16[2,64,1536]{2,1,0:...) custom-call(bf16[3,256,1536]{2,1,0:T(8,128)(2,1)} %refs_1_.1, ...), custom_call_target="tpu_custom_call" | custom-call | flops 25367150592 | bytes 141557760 | tf_op jit(solution)/shard_map/pallas_call | solution.py:1997
  291.7 1.2 fusion.2
  292.9 1.2 fusion.3
  294.1 0.9 pad_maximum_fusion.1.refs_18_
  295.1 230.2 %shard_map.292 = (bf16[3,256,1536]{2,1,0:T(8,128)(2,1)}, bf16[2,3,256,1536]{3,2,1,0:T(8,128)(2,1)}, bf16[2,3,256,1536]{3,2,1,0:T(8,128)(2,1)}, bf16[2,3,256,256]...) custom-call(bf16[3,256,1536]{2,1,0:T(8,128)(2,1)} %refs_0_.3, ...), custom_call_target="tpu_custom_call" | custom-call | flops 38654705664 | bytes 141557760 | tf_op jit(solution)/shard_map/pallas_call | solution.py:2108
  525.3 2.6 convolution_bitcast_fusion.1
  527.9 2.5 convolution_bitcast_fusion
  530.4 1.9 pad_maximum_fusion
  532.3 0.9 copy-done.6
  534.1 2.9 fusion.33
  537.5 0.8 slice_bitcast_fusion.4
  539.3 0.9 pad_maximum_fusion.2.refs_5_
  540.2 215.9 %shard_map.293 = (bf16[3,384,768]{2,1,0:T(8,128)(2,1)}, f32[8,768]{1,0:T(8,128)}, f32[16,384]{1,0:T(8,128)}, f32[8,1536]{1,0:T(8,128)}) custom-call(bf16[2,3,256,1536]{3,2,1,0:T(8,128)(2,1)} %get-tuple-element.75.refs_0_, bf16[2,3,256,1536]{3,2,1,0:T(8,128)(2,1)} %get-tuple-element.76.refs_1_, bf16[2,3,256,1536]{3,2,1,0:T(8,128)(2,1)} %get-tuple-element.77.refs_2_, ...), custom_call_target="tpu_custom_call" | custom-call | tf_op jit(solution)/shard_map/pallas_call | solution.py:1275
  756.1 0.7 reshape.213
  757.5 0.8 slice.154
  758.3 0.8 slice_reduce_fusion.6
  759.7 1.5 slice_reduce_fusion.7
  764.4 1.3 slice_bitcast_fusion
  765.7 3.4 slice_convert_fusion
  769.2 1.4 copy.52
  770.6 1.1 copy-done.3
  771.7 1.4 copy.53
  (74 shorter events, 7.6 us)
Async XLA Ops:
  7.2 7.9 %copy-start = (bf16[1,384,12]{1,2,0:T(8,128)(2,1)S(1)}, bf16[1,384,12]{1,2,0:T(8,128)(2,1)}, u32[]{:S(2)}) copy-start(bf16[1,384,12]{1,2,0:T(8,128)(2,1)} %param.23) | copy-start | bytes 27652
  7.2 762.0 %reduce-scatter.2.cloned.1.call-start = ((), (), s32[]{:S(2)}) async-start(), calls=%async_computation.1 | async-start | bytes 3244032 | tf_op jit(solution)/shard_map/reduce_scatter | solution.py:2200
  525.3 2.7 copy-start.4
  532.3 1.0 copy-start.6
  532.3 1.0 copy-start.7
  532.3 1.0 copy-start.8
  532.3 1.5 copy-start.5
  765.7 3.4 copy-start.2
  769.2 2.5 copy-start.3
  769.2 3.9 copy-start.1
Sparse Core Ops, SparseCore 0:
  532.4 119.0 reduce-scatter.1

commit v4 on v3

--- a/solution.py
+++ b/solution.py
@@ -18,6 +18,7 @@
 HALO = 16
 GC = 256
 LANES = 128
+LOG2E = 1.4426950408889634
 
 
 def nn(a, b):
@@ -37,7 +38,7 @@
 
 
 def sigmoid(v):
-    return 1.0 / (1.0 + jnp.exp(-v))
+    return 0.5 * jnp.tanh(0.5 * v) + 0.5
 
 
 def iota(shape, dim):
@@ -1291,11 +1292,11 @@
     (tokens, mask, value, gate_w, out_w, step_w, state_w, chan, shared) = refs[:9]
     (wv_h, wg_h, wo_h, wt_h, ws_h, pv_o, ps_o, ph_o, pn_o) = refs[9:18]
     (out_h, low_h, mix_h, inv_o, nx_o, vpre_o, spre_o, x_o, bc_o, dtc_o, gate_o, y_o, gg_o, sin_o) = refs[18:32]
-    (nx_s, sc_s, dt_s, cum_s, cumt_s, acc_s, sq_s, psend, precv, sqsend, sqrecv, csend, crecv, hrecv, trecv) = refs[32:47]
-    (ps_sem, pr_sem, ss_sem, sr_sem, cs_sem, cr_sem, hs_sem, hr_sem, ts_sem, tr_sem, low_sem, out_sem, mix_sem) = refs[47:60]
-    (wv_s, wg_s, wo_s, ws_s, wt_s, chan_s, shared_s, w_sem, l_sem) = refs[60:69]
+    (nx_s, sc_s, wide_s, place_s, cum_s, cumt_s, acc_s, sq_s, psend, precv, sqsend, sqrecv, csend, crecv, hrecv, trecv) = refs[32:48]
+    (ps_sem, pr_sem, ss_sem, sr_sem, cs_sem, cr_sem, hs_sem, hr_sem, ts_sem, tr_sem, low_sem, out_sem, mix_sem) = refs[48:61]
+    (wv_s, wg_s, wo_s, ws_s, wt_s, chan_s, shared_s, w_sem, l_sem) = refs[61:70]
     q, s, g = pl.program_id(0), pl.program_id(1), pl.program_id(2)
-    groups = dt_s.shape[0]
+    groups = cum_s.shape[0]
     p, t = lax.axis_index(PIPE), lax.axis_index(TENSOR)
     idx = q * micro + s
     slot = idx * groups + g
@@ -1309,7 +1310,7 @@
         (value, gate_w, out_w, step_w),
         (wv_h, wg_h, wo_h, wt_h),
         ((state_w, ws_h), (chan, chan_s), (shared, shared_s)),
-        refs[69:],
+        refs[70:],
     )
     big = ((wv_h, wv_s), (wg_h, wg_s), (wo_h, wo_s))
 
@@ -1356,6 +1357,7 @@
         def _():
             tokens_copy().start()
 
+        fill_places(place_s, head_dim)
         gather.first_layer()
         for k in range(3):
             weight_copy(0, k).start()
@@ -1456,7 +1458,9 @@
         dtc_o[0] = step
         dtc_o[1] = cum
         dtc_o[2] = sigmoid(raw)
-        group_lanes(step, dt_s, groups, per_group)
+        to_end = jnp.exp(cum[rows - 1 : rows, :] - cum)
+        fill_wide(wide_s, (step, step * to_end, jnp.exp(cum)))
+        cum = cum * LOG2E
         group_lanes(cum, cum_s, groups, per_group)
         group_rows(cum, cumt_s, groups, per_group)
         acc_s[...] = jnp.zeros_like(acc_s)
@@ -1467,10 +1471,9 @@
     conv = conv_rows(pre, pv, rows)
     x = conv * sigmoid(conv)
     x_o[...] = x.astype(BF)
-    step, cum, cumt = dt_s[g], cum_s[g], cumt_s[g]
-    to_end = jnp.exp(cum[rows - 1 : rows, :] - cum)
-    xp = (x * spread(step, GC, head_dim)).astype(BF)
-    xr = (x * spread(step * to_end, GC, head_dim)).astype(BF)
+    cum, cumt, places = cum_s[g], cumt_s[g], place_s[g]
+    xp = (x * nn(wide_s[0], places)).astype(BF)
+    xr = (x * nn(wide_s[1], places)).astype(BF)
     local = tn(xr, bc_o[:, :state])
 
     @pl.when(t == 0)
@@ -1487,21 +1490,24 @@
         csend[slot] = (through_rows(cumt, rows, head_dim, state) * sin_o[...].astype(F32) + local).astype(BF)
         chain_copy(slot).start()
 
-    scores = sc_s[...]
     lane = iota((rows, LANES), 1)
+    cut = rows // 2
     within = []
     for pair in range(GC // LANES):
         cols = slice(LANES * pair, LANES * (pair + 1))
         outs = []
         for i in (2 * pair, 2 * pair + 1):
-            diff = cum[:, i : i + 1] - cumt[i : i + 1, :]
-            mix = (jnp.exp(jnp.minimum(diff, 0.0)) * scores).astype(BF)
-            outs.append(nn(mix, xp[:, cols]))
+            parts = []
+            for first, seen in ((0, cut), (cut, rows)):
+                diff = cum[first : first + cut, i : i + 1] - cumt[i : i + 1, :seen]
+                mix = (jnp.exp2(jnp.minimum(diff, 0.0)) * sc_s[first : first + cut, :seen]).astype(BF)
+                parts.append(nn(mix, xp[:seen, cols]))
+            outs.append(jnp.concatenate(parts, axis=0))
         within.append(jnp.where(lane < head_dim, outs[0], outs[1]))
     gate = nn(nx_s[HALO:, :], wg[...])
     gate_o[...] = gate
     carried = nt(bc_o[:, state:], sin_o[...])
-    y = jnp.concatenate(within, axis=1) + pv[6:7, :] * x + spread(jnp.exp(cum), GC, head_dim) * carried
+    y = jnp.concatenate(within, axis=1) + pv[6:7, :] * x + nn(wide_s[2], places) * carried
     y_o[...] = y
     gated = y * (gate * sigmoid(gate))
     gg = (gated * pv[5:6, :]).astype(BF)
@@ -1587,8 +1593,22 @@
     return ((place == size * (lane // heads) + lax.rem(lane, heads)) & (lane < all_heads)).astype(F32)
 
 
+def fill_places(place_s, head_dim):
+    shape = place_s.shape[1:]
+    head, col = lax.rem(iota(shape, 0), LANES), iota(shape, 1) // head_dim
+    for g in range(place_s.shape[0]):
+        place_s[g] = (head == col + g * (GC // head_dim)).astype(BF)
+
+
+def fill_wide(wide_s, values):
+    for k, value in enumerate(values):
+        high = value.astype(BF)
+        wide_s[k, :, :LANES] = high
+        wide_s[k, :, LANES:] = (value - high.astype(F32)).astype(BF)
+
+
 def through_rows(cumt, rows, head_dim, state):
-    end = jnp.exp(cumt[:, rows - 1 : rows])
+    end = jnp.exp2(cumt[:, rows - 1 : rows])
     parts = [jnp.broadcast_to(end[i : i + 1, :], (head_dim, state)) for i in range(GC // head_dim)]
     return jnp.concatenate(parts, axis=0)
 
@@ -1598,11 +1618,11 @@
     (wv, wg, wo, ws, wt, pv, ps, ph, pn) = refs[14:23]
     (grad_h, dval_o, dgate_o, dst_o, dstep_o, sgm_o, vs_o, ss_o, hs_o, norm_o) = refs[23:33]
     (gm_s, rowsc_s, gin_s, halo_s, halo2_s, acc_s, nacc_s) = refs[33:40]
-    (sct_s, scts_s, wsum_s, dbc_s, dt_s, cum_s, cumt_s, net_s, rv_s, ddir_s, k_s, rt_s, rall_s) = refs[40:53]
-    (psend, precv, csend, crecv, hsend, hrecv, tsend, trecv) = refs[53:61]
-    (ps_sem, pr_sem, cs_sem, cr_sem, hs_sem, hr_sem, ts_sem, tr_sem, out_sem) = refs[61:]
+    (sct_s, scts_s, wsum_s, dbc_s, wide_s, place_s, cum_s, cumt_s, net_s, rv_s, ddir_s, k_s, rt_s, rall_s) = refs[40:54]
+    (psend, precv, csend, crecv, hsend, hrecv, tsend, trecv) = refs[54:62]
+    (ps_sem, pr_sem, cs_sem, cr_sem, hs_sem, hr_sem, ts_sem, tr_sem, out_sem) = refs[62:]
     turn, s, g = pl.program_id(0), pl.program_id(1), pl.program_id(2)
-    groups = dt_s.shape[0]
+    groups = cum_s.shape[0]
     p, t = lax.axis_index(PIPE), lax.axis_index(TENSOR)
     idx = turn * micro + s
     slot = idx * groups + g
@@ -1630,6 +1650,7 @@
     @pl.when((idx == 0) & (g == 0))
     def _():
         greet(ring_neighbours(count) + [(PIPE, 1 - p)])
+        fill_places(place_s, head_dim)
         nacc_s[...] = jnp.zeros_like(nacc_s)
 
     @pl.when((g == 0) & (turn == 0))
@@ -1655,13 +1676,16 @@
         dbc_s[...] = jnp.zeros_like(dbc_s)
         rall_s[...] = jnp.zeros_like(rall_s)
         acc_s[...] = jnp.zeros_like(acc_s)
-        group_lanes(dtc[0], dt_s, groups, per_group)
-        group_lanes(dtc[1], cum_s, groups, per_group)
-        group_rows(dtc[1], cumt_s, groups, per_group)
-
-    step, cum, cumt = dt_s[g], cum_s[g], cumt_s[g]
-    last = cum[rows - 1 : rows, :]
-    fromx = spread(jnp.exp(cum), GC, head_dim)
+        for part_s in (net_s, rv_s, ddir_s, k_s):
+            part_s[...] = jnp.zeros_like(part_s)
+        cum = dtc[1]
+        fill_wide(wide_s, (dtc[0], jnp.exp(cum[rows - 1 : rows, :] - cum), jnp.exp(cum)))
+        cum = cum * LOG2E
+        group_lanes(cum, cum_s, groups, per_group)
+        group_rows(cum, cumt_s, groups, per_group)
+
+    cum, cumt, places = cum_s[g], cumt_s[g], place_s[g]
+    fromx = nn(wide_s[2], places)
 
     gs = nn(gm_s[...], wo[...])
     inverse, shrink = inv[:, 0:1], rowsc_s[:, 0:1]
@@ -1693,9 +1717,8 @@
         csend[slot] = (through_rows(cumt, rows, head_dim, state) * gin_s[...].astype(F32) + dsl).astype(BF)
         chain_copy(slot).start()
 
-    to_end = jnp.exp(last - cum)
-    stepx = spread(step, GC, head_dim)
-    endx = spread(to_end, GC, head_dim)
+    stepx = nn(wide_s[0], places)
+    endx = nn(wide_s[1], places)
     xf = x[...].astype(F32)
     xp = (xf * stepx).astype(BF)
     xr = (xf * stepx * endx).astype(BF)
@@ -1705,8 +1728,10 @@
     dbc_s[:, state:] += nn(dye, s_in[...])
 
     lane = iota((rows, LANES), 1)
-    wsum = wsum_s[...]
-    colsum = jnp.zeros((rows, LANES), F32)
+    cut = rows // 2
+    blocks = ((slice(0, cut), slice(0, rows)), (slice(cut, rows), slice(cut, rows)))
+    wsums = [wsum_s[js, at] for js, at in blocks]
+    colsums = [jnp.zeros((cut, LANES), F32)] * 2
     within = []
     for pair in range(GC // LANES):
         cols = slice(LANES * pair, LANES * (pair + 1))
@@ -1715,26 +1740,32 @@
         for side in range(2):
             i = 2 * pair + side
             mine = (lane < head_dim) if side == 0 else (lane >= head_dim)
-            decay = jnp.exp(jnp.minimum(cumt[i : i + 1, :] - cum[:, i : i + 1], 0.0))
-            outs.append(nn((decay * sct_s[...]).astype(BF), dyp))
-            weight = decay * nt(jnp.where(mine, xpp, jnp.zeros_like(xpp)), dyp)
-            wsum = wsum + weight
-            pairs = (weight * scts_s[...]).astype(BF)
-            colsum = colsum + nn(pairs, (lane == i).astype(BF))
-            rt_s[g, i : i + 1, :] = jnp.sum(pairs.astype(F32), axis=0, keepdims=True)
+            xph = jnp.where(mine, xpp, jnp.zeros_like(xpp))
+            parts, rowsums = [], []
+            for k, (js, at) in enumerate(blocks):
+                decay = jnp.exp2(jnp.minimum(cumt[i : i + 1, at] - cum[js, i : i + 1], 0.0))
+                parts.append(nn((decay * sct_s[js, at]).astype(BF), dyp[at]))
+                weight = decay * nt(xph[js], dyp[at])
+                wsums[k] = wsums[k] + weight
+                pairs = (weight * scts_s[js, at]).astype(BF)
+                colsums[k] = colsums[k] + nn(pairs, (lane[at] == i + per_group * g).astype(BF))
+                rowsums.append(jnp.sum(pairs.astype(F32), axis=0, keepdims=True))
+            outs.append(jnp.concatenate(parts, axis=0))
+            rt_s[g, i : i + 1, :cut] = rowsums[0][:, :cut]
+            rt_s[g, i : i + 1, cut:] = rowsums[0][:, cut:] + rowsums[1]
         within.append(jnp.where(lane < head_dim, outs[0], outs[1]))
-    wsum_s[...] = wsum
+    for k, (js, at) in enumerate(blocks):
+        wsum_s[js, at] = wsums[k]
+    colsum = jnp.concatenate(colsums, axis=0)
     u = jnp.concatenate(within, axis=1) + endx * gb
 
-    heads = (iota((GC, LANES), 0) // head_dim == iota((GC, LANES), 1)).astype(BF)
-    ddir_s[g] = nn((xf * u).astype(BF), heads)
-    net_s[g] = nn((dyef * cs).astype(BF), heads) - colsum
-    rv_s[g] = step * to_end * nn((xf * gb).astype(BF), heads)
-    inner = gin_s[...].astype(F32) * s_in[...].astype(F32)
-    per_channel = lax.dot_general(
-        jnp.ones((8, inner.shape[1]), F32), inner, (((1,), (1,)), ((), ())), precision=HIGHEST, preferred_element_type=F32
-    )
-    k_s[g] = jnp.exp(last) * exact(per_channel, heads.astype(F32))
+    heads = (iota((GC, LANES), 0) // head_dim + per_group * g == iota((GC, LANES), 1)).astype(BF)
+    ddir_s[...] += nn((xf * u).astype(BF), heads)
+    net_s[...] += nn((dyef * cs).astype(BF), heads) - colsum
+    rv_s[...] += nn((xf * gb).astype(BF), heads)
+    inner = (gin_s[...].astype(F32) * s_in[...].astype(F32)).astype(BF)
+    per_channel = nt(jnp.ones((16, inner.shape[1]), BF), inner)
+    k_s[...] += nn(per_channel.astype(BF), heads)[:8]
 
     dx = stepx * u + pv[6:7, :] * dyf
     dconv = dx * silu_slope(conv_rows(vpre, pv, rows))
@@ -1780,17 +1811,16 @@
         ssums = conv_sums(dsc, spre, rows)
         ssums.append(jnp.zeros((3, 2 * state), F32))
         ss_o[...] = jnp.concatenate(ssums, axis=0)
-        net, rv, ddir, const = net_s[0], rv_s[0], ddir_s[0], k_s[0]
-        rall_s[0:per_group, :] = rt_s[0, 0:per_group, :]
-        for other in range(1, groups):
+        for other in range(groups):
             shift = per_group * other
-            net = net + pltpu.roll(net_s[other], shift, 1)
-            rv = rv + pltpu.roll(rv_s[other], shift, 1)
-            ddir = ddir + pltpu.roll(ddir_s[other], shift, 1)
-            const = const + pltpu.roll(k_s[other], shift, 1)
             rall_s[shift : shift + per_group, :] = rt_s[other, 0:per_group, :]
-        net = net + rall_s[...].T
-        da = exact((second >= first).astype(F32), net) + exact((second < first).astype(F32), rv) + const[0:1, :]
+        total, step = dtc[1], dtc[0]
+        last = total[rows - 1 : rows, :]
+        net = net_s[...] + rall_s[...].T
+        rv = rv_s[...] * step * jnp.exp(last - total)
+        da = exact((second >= first).astype(F32), net) + exact((second < first).astype(F32), rv)
+        da = da + jnp.exp(last) * k_s[0:1, :]
+        ddir = ddir_s[...]
         rate = jnp.exp(ph[1:2, :])
         dstep = (ddir - da * rate) * dtc[2]
         dstep_o[...] = dstep.astype(BF)
@@ -1951,12 +1981,12 @@
         ((pair + (rows, width), BF), item_cols(rows)),
         ((pair + (width, state), BF), item_rows(state)),
     ]
-    lanes = vmem((groups, rows, LANES), F32)
     scratch = [
         vmem((rows + HALO, model), BF),
         vmem((rows, rows), F32),
-        lanes,
-        lanes,
+        vmem((3, rows, 2 * LANES), BF),
+        vmem((groups, 2 * LANES, GC), BF),
+        vmem((groups, rows, LANES), F32),
         vmem((groups, 8, rows), F32),
         vmem((rows, model), F32),
         vmem((rows, LANES), F32),
@@ -2061,7 +2091,7 @@
         ((pair + (8, LANES), F32), item(8, LANES)),
         (((2, 8, model), F32), all_of((2, 8, model))),
     ]
-    lanes = vmem((groups, rows, LANES), F32)
+    lanes = vmem((rows, LANES), F32)
     square = vmem((rows, rows), F32)
     scratch = [
         vmem((rows, model), BF),
@@ -2075,13 +2105,14 @@
         square,
         square,
         vmem((rows, states), F32),
-        lanes,
-        lanes,
+        vmem((3, rows, 2 * LANES), BF),
+        vmem((groups, 2 * LANES, GC), BF),
+        vmem((groups, rows, LANES), F32),
         vmem((groups, 8, rows), F32),
         lanes,
         lanes,
         lanes,
-        vmem((groups, 8, LANES), F32),
+        vmem((8, LANES), F32),
         vmem((groups, 8, rows), F32),
         vmem((LANES, rows), F32),
         vmem((slots, rows, model), BF),

time: 795 us -> 779 us (0.980)
  the two profiles are of different devices: /device:TPU:0 before, /device:TPU:30 now
where the time goes in v4:
time: 779 us; the launch traced here: 778 us
  Pallas kernels  718 us (92%)
  local copies, waits for them, and re-layouts  22.5 us (3%)
  between operations  14.4 us (2%)
  other arithmetic  13.4 us (2%)
  matrix products  9.9 us (1%)
    pallas_call x1, Pallas kernels, forward_call(): return pl.pallas_call(kernel, **options)(*[array for array, _ in ins])  296 us
    pallas_call x1, Pallas kernels, reduce_call(): pl.pallas_call(functools.partial(reduce_grads, count), in_specs=[anywhere...  244 us
    pallas_call x1, Pallas kernels, backward_fused_call(): return pl.pallas_call(kernel, **options)(*[array for array, _ in ins])  178 us
  transfers between devices with their start and end apart: 1, of which 0 were waited for; matrix products, arithmetic and copies ran while one was open for 3% of the time, Pallas kernels for 31%

profile of v4, /device:TPU:30, one launch (start us, length us, event | category | flops | bytes accessed | tf_op | source)
XLA Modules:
  0.0 777.9 jit_solution(16409463049644516852)
XLA Ops:
  7.8 1.3 reduce.27
  9.2 1.3 reduce.26
  10.7 0.7 broadcast_in_dim.21
  11.5 0.7 copy.45
  12.2 0.7 compare_convert_fusion
  12.9 0.7 select_maximum_fusion
  13.6 1.4 pad_maximum_fusion.3.refs_8_
  15.1 0.7 convolution_convert_fusion.2.refs_5_
  15.8 1.4 concatenate.22.refs_7_
  17.2 0.9 broadcast_in_dim.20.refs_1_.refs_3_
  18.1 295.9 %shard_map.291 = (bf16[2,1536,1536]{2,1,0:T(8,128)(2,1)}, bf16[2,1536,1536]{2,1,0:T(8,128)(2,1)}, bf16[2,1536,1536]{2,1,0:T(8,128)(2,1)}, bf16[2,64,1536]{2,1,0:...) custom-call(bf16[3,256,1536]{2,1,0:T(8,128)(2,1)} %refs_1_.1, ...), custom_call_target="tpu_custom_call" | custom-call | flops 25367150592 | bytes 141557760 | tf_op jit(solution)/shard_map/pallas_call | solution.py:2027
  314.0 1.2 fusion.2
  315.2 1.2 fusion.3
  316.5 0.9 pad_maximum_fusion.1.refs_18_
  317.4 178.2 %shard_map.292 = (bf16[3,256,1536]{2,1,0:T(8,128)(2,1)}, bf16[2,3,256,1536]{3,2,1,0:T(8,128)(2,1)}, bf16[2,3,256,1536]{3,2,1,0:T(8,128)(2,1)}, bf16[2,3,256,256]...) custom-call(bf16[3,256,1536]{2,1,0:T(8,128)(2,1)} %refs_0_.3, ...), custom_call_target="tpu_custom_call" | custom-call | flops 38654705664 | bytes 141557760 | tf_op jit(solution)/shard_map/pallas_call | solution.py:2139
  495.6 2.6 convolution_bitcast_fusion.1
  498.3 2.5 convolution_bitcast_fusion
  500.7 1.9 pad_maximum_fusion
  502.6 0.9 copy-done.6
  504.5 2.8 fusion.33
  507.8 0.8 slice_bitcast_fusion.4
  509.6 0.9 pad_maximum_fusion.2.refs_5_
  510.5 243.6 %shard_map.293 = (bf16[3,384,768]{2,1,0:T(8,128)(2,1)}, f32[8,768]{1,0:T(8,128)}, f32[16,384]{1,0:T(8,128)}, f32[8,1536]{1,0:T(8,128)}) custom-call(bf16[2,3,256,1536]{3,2,1,0:T(8,128)(2,1)} %get-tuple-element.75.refs_0_, bf16[2,3,256,1536]{3,2,1,0:T(8,128)(2,1)} %get-tuple-element.76.refs_1_, bf16[2,3,256,1536]{3,2,1,0:T(8,128)(2,1)} %get-tuple-element.77.refs_2_, ...), custom_call_target="tpu_custom_call" | custom-call | tf_op jit(solution)/shard_map/pallas_call | solution.py:1276
  754.0 0.7 reshape.213
  755.4 0.8 slice.154
  756.2 0.8 slice_reduce_fusion.6
  757.6 1.5 slice_reduce_fusion.7
  762.3 1.3 slice_bitcast_fusion
  763.7 3.4 slice_convert_fusion
  767.1 1.4 copy.52
  768.5 1.1 copy-done.3
  769.6 1.4 copy.53
  (74 shorter events, 7.6 us)
Async XLA Ops:
  7.2 7.9 %copy-start = (bf16[1,384,12]{1,2,0:T(8,128)(2,1)S(1)}, bf16[1,384,12]{1,2,0:T(8,128)(2,1)}, u32[]{:S(2)}) copy-start(bf16[1,384,12]{1,2,0:T(8,128)(2,1)} %param.23) | copy-start | bytes 27652
  7.2 759.9 %reduce-scatter.2.cloned.1.call-start = ((), (), s32[]{:S(2)}) async-start(), calls=%async_computation.1 | async-start | bytes 3244032 | tf_op jit(solution)/shard_map/reduce_scatter | solution.py:2231
  495.6 2.7 copy-start.4
  502.6 1.0 copy-start.6
  502.6 1.0 copy-start.7
  502.6 1.0 copy-start.8
  502.6 1.5 copy-start.5
  763.7 3.4 copy-start.2
  767.1 2.5 copy-start.3
  767.1 3.9 copy-start.1
Sparse Core Ops, SparseCore 0:
  502.7 128.8 reduce-scatter.1

commit v5 on v4

--- a/solution.py
+++ b/solution.py
@@ -35,6 +35,23 @@
 
 def exact(a, b):
     return jnp.dot(a, b, precision=HIGHEST, preferred_element_type=F32)
+
+
+def in_parts(v):
+    high = v.astype(BF)
+    rest = v - high.astype(F32)
+    middle = rest.astype(BF)
+    return high, middle, (rest - middle.astype(F32)).astype(BF)
+
+
+def pick_rows(places, v):
+    total, width = nn(places, jnp.concatenate(in_parts(v), axis=1)), v.shape[1]
+    return total[:, :width] + (total[:, width : 2 * width] + total[:, 2 * width :])
+
+
+def pick_cols(v, places):
+    high, middle, lowest = [nn(part, places) for part in in_parts(v)]
+    return high + (middle + lowest)
 
 
 def sigmoid(v):
@@ -964,7 +981,7 @@
         self.y_mate, self.core_mate = 2 * (1 - self.y) + self.c, 2 * self.y + 1 - self.c
         self.kinds = 3
         self.pieces = 2 * self.kinds * count
-        self.ticks = self.pieces + count + 3
+        self.ticks = self.pieces + count + 2
         self.rows, self.half = self.xsend.shape[1], self.xsend.shape[2]
 
     @staticmethod
@@ -993,6 +1010,10 @@
     def partners(self):
         return ring_neighbours(self.count) + [(PIPE, 1 - self.p), (DP, self.y_mate), (DP, self.core_mate)]
 
+    def owner(self, m):
+        place = lax.rem(m, self.count)
+        return place // 2 + lax.rem(place, 2) * (self.count - 1 - 2 * (place // 2))
+
     def layer_of(self, m):
         return m // (self.kinds * self.count)
 
@@ -1000,7 +1021,7 @@
         return pltpu.make_async_copy(self.factors[which % 2].at[which // 2], self.a_s, self.a_sem.at[0])
 
     def b_copy(self, m, w):
-        src = self.factors[2 + w].at[self.layer_of(m), :, :, aligned(lax.rem(m, self.count), self.half)]
+        src = self.factors[2 + w].at[self.layer_of(m), :, :, aligned(self.owner(m), self.half)]
         held = lax.rem(m, 2)
         return pltpu.make_async_copy(src, self.b_s.at[held], self.b_sem.at[held])
 
@@ -1077,13 +1098,13 @@
 
         to_right, to_left = n - 4 - t, n - 3 - count + t
 
-        @self.when_valid(to_right, t < lax.rem(to_right + count, count))
+        @self.when_valid(to_right, t < self.owner(jnp.maximum(to_right, 0)))
         def _():
             pass_on(to_right, t == 0, self.right(to_right), lambda: self.right(to_right).start())
 
-        @self.when_valid(to_left, t > lax.rem(to_left + count, count))
-        def _():
-            owner = lax.rem(to_left, count)
+        @self.when_valid(to_left, t > self.owner(jnp.maximum(to_left, 0)))
+        def _():
+            owner = self.owner(to_left)
 
             def send():
                 @pl.when(owner == t - 1)
@@ -1096,10 +1117,7 @@
 
             pass_on(to_left, t == count - 1, self.left(to_left, False), send)
 
-        done = n - 3 - count
-
-        @self.when_valid(done, t == lax.rem(done + count, count))
-        def _():
+        def last(done):
             w = done // count
             mine = self.xsend.at[w]
             mine[...] = self.total_s[lax.rem(done, 4)]
@@ -1117,6 +1135,10 @@
             @pl.when(self.p != self.layer_of(done))
             def _():
                 self.x_copy(w).start()
+
+        outer = (t == 0) | (t == count - 1)
+        for done, ready in ((n - 3 - count, outer), (n - 2 - count, jnp.logical_not(outer))):
+            self.when_valid(done, ready & (t == self.owner(jnp.maximum(done, 0))))(functools.partial(last, done))
 
         @self.when_valid(n)
         def _():
@@ -1165,11 +1187,11 @@
             self.result_copy(w, True).start()
         for m in range(self.pieces):
 
-            @pl.when(t < m % count)
+            @pl.when(t < self.owner(m))
             def _():
                 self.right(m).wait_send()
 
-            @pl.when(t > m % count)
+            @pl.when(t > self.owner(m))
             def _():
                 self.left(m, False).wait_send()
 
@@ -1370,8 +1392,8 @@
         for layer in range(2):
             per_head = chan_s[layer]
             for kind in range(2):
-                pick = ((place == first + kind * heads) & used).astype(F32)
-                ph_o[layer, kind : kind + 1, :] = exact(per_head, pick)[7:8, :]
+                pick = ((place == first + kind * heads) & used).astype(BF)
+                ph_o[layer, kind : kind + 1, :] = pick_cols(per_head, pick)[7:8, :]
             ph_o[layer, 2:, :] = jnp.zeros((6, LANES), F32)
             pn_o[layer] = shared_s[layer]
             for k in range(5):
@@ -1452,9 +1474,9 @@
         lower = iota((rows, rows), 0) >= iota((rows, rows), 1)
         sc_s[...] = jnp.where(lower, scores, 0.0)
         raw = nt(nx_s[HALO:, :], wt[...])
-        raw = exact(raw, step_places(count, raw.shape[1], per_group * groups)) + ph[0:1, :]
+        raw = pick_cols(raw, step_places(count, raw.shape[1], per_group * groups).astype(BF)) + ph[0:1, :]
         step = jnp.maximum(raw, 0.0) + jnp.log(1.0 + jnp.exp(-jnp.abs(raw)))
-        cum = exact(lower.astype(F32), -step * jnp.exp(ph[1:2, :]))
+        cum = pick_rows(lower.astype(BF), -step * jnp.exp(ph[1:2, :]))
         dtc_o[0] = step
         dtc_o[1] = cum
         dtc_o[2] = sigmoid(raw)
@@ -1818,7 +1840,7 @@
         last = total[rows - 1 : rows, :]
         net = net_s[...] + rall_s[...].T
         rv = rv_s[...] * step * jnp.exp(last - total)
-        da = exact((second >= first).astype(F32), net) + exact((second < first).astype(F32), rv)
+        da = pick_rows((second >= first).astype(BF), net) + pick_rows((second < first).astype(BF), rv)
         da = da + jnp.exp(last) * k_s[0:1, :]
         ddir = ddir_s[...]
         rate = jnp.exp(ph[1:2, :])

time: 779 us -> 769 us (0.987)
  the two profiles are of different devices: /device:TPU:30 before, /device:TPU:0 now
where the time goes in v5:
time: 769 us; the launch traced here: 759 us
  Pallas kernels  699 us (91%)
  local copies, waits for them, and re-layouts  22.6 us (3%)
  between operations  14.4 us (2%)
  other arithmetic  13.4 us (2%)
  matrix products  9.88 us (1%)
    pallas_call x1, Pallas kernels, forward_call(): return pl.pallas_call(kernel, **options)(*[array for array, _ in ins])  271 us
    pallas_call x1, Pallas kernels, reduce_call(): pl.pallas_call(functools.partial(reduce_grads, count), in_specs=[anywhere...  214 us
    pallas_call x1, Pallas kernels, backward_fused_call(): return pl.pallas_call(kernel, **options)(*[array for array, _ in ins])  214 us
  transfers between devices with their start and end apart: 1, of which 0 were waited for; matrix products, arithmetic and copies ran while one was open for 3% of the time, Pallas kernels for 28%

profile of v5, /device:TPU:0, one launch (start us, length us, event | category | flops | bytes accessed | tf_op | source)
XLA Modules:
  0.0 759.3 jit_solution(2875730745290196748)
XLA Ops:
  7.8 1.3 reduce.27
  9.2 1.3 reduce.26
  10.7 0.7 broadcast_in_dim.21
  11.5 0.7 copy.45
  12.2 0.7 compare_convert_fusion
  12.9 0.7 select_maximum_fusion
  13.6 1.4 pad_maximum_fusion.3.refs_8_
  15.1 0.7 convolution_convert_fusion.2.refs_5_
  15.8 1.4 concatenate.22.refs_7_
  17.2 0.9 broadcast_in_dim.20.refs_1_.refs_3_
  18.1 271.2 %shard_map.291 = (bf16[2,1536,1536]{2,1,0:T(8,128)(2,1)}, bf16[2,1536,1536]{2,1,0:T(8,128)(2,1)}, bf16[2,1536,1536]{2,1,0:T(8,128)(2,1)}, bf16[2,64,1536]{2,1,0:...) custom-call(bf16[3,256,1536]{2,1,0:T(8,128)(2,1)} %refs_1_.1, ...), custom_call_target="tpu_custom_call" | custom-call | flops 25367150592 | bytes 141557760 | tf_op jit(solution)/shard_map/pallas_call | solution.py:2049
  289.3 1.2 fusion.2
  290.5 1.2 fusion.3
  291.7 0.9 pad_maximum_fusion.1.refs_18_
  292.7 213.5 %shard_map.292 = (bf16[3,256,1536]{2,1,0:T(8,128)(2,1)}, bf16[2,3,256,1536]{3,2,1,0:T(8,128)(2,1)}, bf16[2,3,256,1536]{3,2,1,0:T(8,128)(2,1)}, bf16[2,3,256,256]...) custom-call(bf16[3,256,1536]{2,1,0:T(8,128)(2,1)} %refs_0_.3, ...), custom_call_target="tpu_custom_call" | custom-call | flops 38654705664 | bytes 141557760 | tf_op jit(solution)/shard_map/pallas_call | solution.py:2161
  506.2 2.6 convolution_bitcast_fusion.1
  508.9 2.5 convolution_bitcast_fusion
  511.3 1.9 pad_maximum_fusion
  513.2 0.9 copy-done.6
  515.1 2.9 fusion.33
  518.5 0.8 slice_bitcast_fusion.4
  520.3 0.9 pad_maximum_fusion.2.refs_5_
  521.2 214.3 %shard_map.293 = (bf16[3,384,768]{2,1,0:T(8,128)(2,1)}, f32[8,768]{1,0:T(8,128)}, f32[16,384]{1,0:T(8,128)}, f32[8,1536]{1,0:T(8,128)}) custom-call(bf16[2,3,256,1536]{3,2,1,0:T(8,128)(2,1)} %get-tuple-element.75.refs_0_, bf16[2,3,256,1536]{3,2,1,0:T(8,128)(2,1)} %get-tuple-element.76.refs_1_, bf16[2,3,256,1536]{3,2,1,0:T(8,128)(2,1)} %get-tuple-element.77.refs_2_, ...), custom_call_target="tpu_custom_call" | custom-call | tf_op jit(solution)/shard_map/pallas_call | solution.py:1298
  735.4 0.7 reshape.213
  736.8 0.8 slice.154
  737.6 0.8 slice_reduce_fusion.6
  739.0 1.5 slice_reduce_fusion.7
  743.7 1.3 slice_bitcast_fusion
  745.1 3.4 slice_convert_fusion
  748.5 1.4 copy.52
  749.9 1.1 copy-done.3
  751.0 1.4 copy.53
  (74 shorter events, 7.6 us)
Async XLA Ops:
  7.2 7.9 %copy-start = (bf16[1,384,12]{1,2,0:T(8,128)(2,1)S(1)}, bf16[1,384,12]{1,2,0:T(8,128)(2,1)}, u32[]{:S(2)}) copy-start(bf16[1,384,12]{1,2,0:T(8,128)(2,1)} %param.23) | copy-start | bytes 27652
  7.2 741.3 %reduce-scatter.2.cloned.1.call-start = ((), (), s32[]{:S(2)}) async-start(), calls=%async_computation.1 | async-start | bytes 3244032 | tf_op jit(solution)/shard_map/reduce_scatter | solution.py:2253
  506.2 2.7 copy-start.4
  513.2 1.0 copy-start.6
  513.2 1.0 copy-start.7
  513.2 1.0 copy-start.8
  513.2 1.5 copy-start.5
  745.1 3.4 copy-start.2
  748.5 2.5 copy-start.3
  748.5 3.9 copy-start.1
Sparse Core Ops, SparseCore 0:
  513.4 119.9 reduce-scatter.1
